TPU v7x, 128 devices: a whole 4x4x4 slice. The times are simulated.
128 devices in a mesh: row: 32 (over x, z_lo, y), col: 4 (over z_hi, core).
Axes of the slice: x: 4, y: 4, z: 4 (z_hi: 2, z_lo: 2; z = z_hi * 2 + z_lo), core: 2. Of those that a mesh axis runs over, the one named last changes fastest.
Arguments:
- vectors: float32 [2, 131072, 1024], P(None, ('row', 'col')), may hold values from -6 to 6
- panel_store: float32 [2, 2, 131072, 256], P(None, None, ('row', 'col')), may hold values from -0.015625 to 0.015625
- block_ids: int32 [2, 16384], P(None, ('row', 'col')), may hold values from 0 to 16383, as said below
- offsets: int32 [2], replicated, may hold values from 0 to 16383
- tri_factors: float32 [2, 2, 256, 256], replicated, may hold values from -6 to 6
Outputs:
- transformed: float32 [2, 131072, 1024], P(None, ('row', 'col'))
Inputs may be any that keep to these rules, and one draw needn't show every extreme that they name: `block_ids`: for each panel the ids are a permutation of the 16384 row blocks; list slot t of the shard held by any device (t counted within that shard, 0 to 127) holds a block of strip t, that is an id g with g // 128 equal to t.
All inputs are finite; a program needn't handle non-finite values.
Results may differ from a plain program's by a relative error of at most 0.0003.
Values sent between devices are 32-bit elements; how exact they have to be, the bound alone decides.
A program may use at most 192 MiB of HBM per device.

v0:
```python
import jax
import jax.numpy as jnp
from jax import lax
from jax.sharding import PartitionSpec as P

highest = lax.Precision.HIGHEST


def contract(first_op, second_op):
    return lax.dot_general(
        first_op,
        second_op,
        (((0,), (0,)), ((), ())),
        precision=highest,
        preferred_element_type=jnp.float32,
    )


def matmul(first_op, second_op):
    return jnp.dot(first_op, second_op, precision=highest, preferred_element_type=jnp.float32)


def adjoint_times(first_op, second_op):
    real_part = contract(first_op[0], second_op[0]) + contract(first_op[1], second_op[1])
    imag_part = contract(first_op[0], second_op[1]) - contract(first_op[1], second_op[0])
    return jnp.stack([real_part, imag_part])


def complex_times(first_op, second_op):
    real_part = matmul(first_op[0], second_op[0]) - matmul(first_op[1], second_op[1])
    imag_part = matmul(first_op[0], second_op[1]) + matmul(first_op[1], second_op[0])
    return jnp.stack([real_part, imag_part])


def adjoint_upper(factor):
    upper_part = jnp.triu(factor)
    return jnp.stack([upper_part[0].T, -upper_part[1].T])


def mask_panel(values, first_row, offset):
    row_count = values.shape[1]
    col_count = values.shape[2]
    row_index = first_row + jnp.arange(row_count, dtype=jnp.int32)[:, None]
    limit = offset + jnp.arange(col_count, dtype=jnp.int32)[None, :]
    below = row_index > limit
    diagonal = row_index == limit
    real_part = jnp.where(
        below, values[0], jnp.where(diagonal, jnp.ones_like(values[0]), jnp.zeros_like(values[0]))
    )
    imag_part = jnp.where(below, values[1], jnp.zeros_like(values[1]))
    return jnp.stack([real_part, imag_part])


def apply_panels(columns, householder, tri_factors, reduce_all):
    current = columns
    for panel in range(householder.shape[0]):
        summed = reduce_all(adjoint_times(householder[panel], current))
        update = complex_times(adjoint_upper(tri_factors[panel]), summed)
        current = current - complex_times(householder[panel], update)
    return current


def per_device(vectors, panel_store, block_ids, offsets, tri_factors):
    panel_count = panel_store.shape[0]
    row_count = panel_store.shape[2]
    col_width = panel_store.shape[3]
    slot_count = block_ids.shape[1]
    block_rows = row_count // slot_count
    outgoing = panel_store.reshape(panel_count, 2, slot_count, block_rows * col_width)
    labels = block_ids.astype(jnp.float32).reshape(panel_count, 1, slot_count)
    arrived, arrived_ids = (
        lax.all_to_all(outgoing, ("row", "col"), split_axis=2, concat_axis=2, tiled=True),
        lax.all_to_all(labels, ("row", "col"), split_axis=2, concat_axis=2, tiled=True),
    )
    local_ids = arrived_ids[:, 0, :].astype(jnp.int32) % slot_count
    ordering = jnp.argsort(local_ids, axis=1)
    placed = jnp.take_along_axis(arrived, ordering[:, None, :, None], axis=2)
    placed = placed.reshape(panel_count, 2, row_count, col_width)
    first_row = lax.axis_index(("row", "col")) * row_count
    stacked = jnp.stack(
        [mask_panel(placed[panel], first_row, offsets[panel]) for panel in range(panel_count)]
    )

    def reduce_strips(partial_sum):
        return lax.psum(partial_sum, ("row", "col"))

    return apply_panels(vectors, stacked, tri_factors, reduce_strips)


def solution(mesh):
    placed = (
        P(None, ("row", "col"), None),
        P(None, None, ("row", "col"), None),
        P(None, ("row", "col")),
        P(),
        P(),
    )
    return jax.shard_map(
        per_device,
        mesh=mesh,
        in_specs=placed,
        out_specs=P(None, ("row", "col"), None),
        check_vma=False,
    )
```

profile of v0, /device:TPU:1, one launch (start us, length us, event | category | flops | bytes accessed | tf_op | source)
XLA Modules:
  0.0 555.9 jit_solution(735607799687048648)
XLA Ops:
  6.5 0.8 copy.11
  7.9 11.5 %all-to-all-start = ((f32[2,1,128]{0,1,2:T(1,128)}), f32[2,1,128]{0,1,2:T(1,128)S(1)}, u32[]{:S(2)}, u32[]{:S(2)}) async-start(f32[2,1,128]{0,1,2:T(1,128)} %bitcast.1), calls=%async_computation | async-start | bytes 131072 | tf_op jit(solution)/shard_map/all_to_all | solution.py:73
  19.4 4.9 reshape.265
  24.3 7.4 %copy.13 = f32[2,2,128,2048]{3,1,0,2:T(2,128)} copy(f32[2,2,128,2048]{3,2,1,0:T(8,128)} %reshape.265) | data formatting | bytes 8388608 | tf_op jit(solution)/shard_map/reshape | solution.py:69
  31.7 10.2 %all-to-all-start.1 = ((f32[2,2,128,2048]{3,1,0,2:T(2,128)}), f32[2,2,128,2048]{3,1,0,2:T(2,128)}, u32[]{:S(2)}, u32[]{:S(2)}) async-start(f32[2,2,128,2048]{3,1,0,2:T(2,128)} %copy.13), calls=%async_computation.1 | async-start | bytes 8388608 | tf_op jit(solution)/shard_map/all_to_all | solution.py:72
  45.6 1.1 gt.68
  46.7 1.1 sort.19.cloned.1.call-done
  48.5 0.7 fusion.79
  49.2 44.9 %all-to-all-done.1 = f32[2,2,128,2048]{3,1,0,2:T(2,128)} async-done(((f32[2,2,128,2048]{3,1,0,2:T(2,128)}), f32[2,2,128,2048]{3,1,0,2:T(2,128)}, u32[]{:S(2)}, u32[]{:S(2)}) %all-to-all-start.1) | async-done | bytes 4194336 | tf_op jit(solution)/shard_map/all_to_all | solution.py:72
  94.1 6.5 %copy.14 = f32[2,2,128,2048]{3,1,2,0:T(2,128)} copy(f32[2,2,128,2048]{3,1,0,2:T(2,128)} %all-to-all-done.1) | data formatting | bytes 8388608 | tf_op jit(solution)/shard_map/all_to_all | solution.py:72
  100.7 14.6 %gather_fusion = f32[256,2,2048]{2,1,0:T(2,128)} fusion(f32[2,2,128,2048]{3,1,2,0:T(2,128)} %copy.14, s32[256]{0:T(256)S(1)} %fusion.79), kind=kCustom, calls=%fused_computation | custom fusion | bytes 8390656 | tf_op jit(solution)/shard_map/jit(take_along_axis)/gather | solution.py:77
  115.3 4.1 select_bitcast_fusion
  119.4 33.5 %slice_reduce_fusion = (f32[128,2048]{1,0:T(8,128)}, f32[128,2048]{1,0:T(8,128)}, f32[128,2048]{1,0:T(8,128)S(1)}, f32[128,2048]{1,0:T(8,128)}, f32[128,2048]{1,...) fusion(f32[2,2,128,2048]{3,1,2,0:T(2,128)S(1)} %select_bitcast_fusion, ...), kind=kLoop, calls=%fused_computation.66 | loop fusion | flops 2621440 | bytes 13647872 | tf_op jit(solution)/shard_map/slice | solution.py:50
  153.0 1.4 select_n.94
  154.4 5.8 %fusion = f32[256,1024]{1,0:T(8,128)S(1)} fusion(f32[1024,256]{1,0:T(8,128)S(1)} %select_n.94, f32[2,1024,1024]{2,1,0:T(8,128)} %param.5), kind=kOutput, calls=%fused_computation.5 | convolution fusion | flops 3221225472 | bytes 6291456 | tf_op jit(solution)/shard_map/dot_general | solution.py:10
  160.2 5.8 %fusion.2 = f32[256,1024]{1,0:T(8,128)S(1)} fusion(f32[1024,256]{1,0:T(8,128)S(1)} %select_n.96, f32[2,1024,1024]{2,1,0:T(8,128)} %param.5), kind=kOutput, calls=%fused_computation.7 | convolution fusion | flops 3221225472 | bytes 6291456 | tf_op jit(solution)/shard_map/dot_general | solution.py:10
  166.0 5.7 %fusion.29 = f32[1,256,1024]{2,1,0:T(8,128)S(1)} fusion(f32[256,1024]{1,0:T(8,128)S(1)} %fusion, f32[1024,256]{1,0:T(8,128)S(1)} %select_n.96, f32[2,1024,1024]{2,1,0:T(8,128)} %param.5), kind=kOutput, calls=%fused_computation.41 | convolution fusion | flops 3221487616 | bytes 7340032 | tf_op jit(solution)/shard_map/dot_general | solution.py:10
  171.7 3.7 fusion.23
  175.4 1.5 pad_maximum_fusion
  177.2 1.2 bitcast_select_fusion
  178.7 1.4 select_n.103
  180.1 2.4 squeeze.68
  182.5 144.2 %all-reduce.3.cloned.1.call-done = f32[2,256,1024]{2,1,0:T(8,128)} async-done(((f32[2,256,1024]{2,1,0:T(8,128)}), f32[2,256,1024]{2,1,0:T(8,128)}) %all-reduce.3.cloned.1.call-update) | async-done | bytes 2097168 | tf_op jit(solution)/shard_map/psum | solution.py:85
  326.7 2.4 fusion.36
  329.2 2.5 convolution_subtract_fusion.1
  331.7 3.8 fusion.41
  335.5 1.0 fusion.37
  336.6 1.1 convolution_add_fusion.1
  337.7 4.0 fusion.40
  341.7 3.9 subtract_bitcast_fusion.1
  345.6 3.9 add_bitcast_fusion.1
  349.6 3.2 maximum_subtract_fusion
  353.3 3.7 fusion.8
  357.0 3.7 fusion.9
  360.7 3.7 fusion.19
  364.4 3.9 fusion.17
  368.3 1.5 pad_maximum_fusion.1
  370.0 1.4 squeeze.77
  371.4 147.2 %all-reduce.5.cloned.1.call-done = f32[2,256,1024]{2,1,0:T(8,128)} async-done(((f32[2,256,1024]{2,1,0:T(8,128)}), f32[2,256,1024]{2,1,0:T(8,128)}) %all-reduce.5.cloned.1.call-update) | async-done | bytes 2097168 | tf_op jit(solution)/shard_map/psum | solution.py:85
  518.6 2.3 fusion.38
  520.9 2.4 convolution_subtract_fusion
  523.3 3.8 fusion.43
  527.1 1.0 fusion.39
  528.2 1.1 convolution_add_fusion
  529.3 4.0 fusion.42
  533.3 3.9 subtract_bitcast_fusion
  537.3 5.2 add_bitcast_fusion
  542.5 6.6 %maximum_subtract_fusion.1 = f32[2,1024,1024]{2,1,0:T(8,128)} fusion(f32[1,1024,1024]{2,1,0:T(8,128)} %add_bitcast_fusion, f32[1,1024,1024]{2,1,0:T(8,128)S(1)} %subtract_bitcast_fusion, f32[2,1024,1024]{2,1,0:T(8,128)S(1)} %bitcast.129, f32[1,1024,1024]{2,1,0:T(8,128)S(1)} %copy-done.3, f32[1,1024,1024]{2,1,0:T(8,128)S(1)} %copy-done.1), kind=kLoop, calls=%fused_computation.2 | loop fusion | flops 8388608 | bytes 33554432 | tf_op jit(solution)/shard_map/sub | solution.py:59
  (69 shorter events, 6.7 us)
Async XLA Ops:
  7.9 23.8 %all-to-all-start = ((f32[2,1,128]{0,1,2:T(1,128)}), f32[2,1,128]{0,1,2:T(1,128)S(1)}, u32[]{:S(2)}, u32[]{:S(2)}) async-start(f32[2,1,128]{0,1,2:T(1,128)} %bitcast.1), calls=%async_computation | async-start | bytes 131072 | tf_op jit(solution)/shard_map/all_to_all | solution.py:73
  31.7 10.3 %copy-start.12 = (s32[2]{0:T(128)S(1)}, s32[2]{0:T(128)}, u32[]{:S(2)}) copy-start(s32[2]{0:T(128)} %param.8) | copy-start | bytes 28
  31.7 62.4 %all-to-all-start.1 = ((f32[2,2,128,2048]{3,1,0,2:T(2,128)}), f32[2,2,128,2048]{3,1,0,2:T(2,128)}, u32[]{:S(2)}, u32[]{:S(2)}) async-start(f32[2,2,128,2048]{3,1,0,2:T(2,128)} %copy.13), calls=%async_computation.1 | async-start | bytes 8388608 | tf_op jit(solution)/shard_map/all_to_all | solution.py:72
  41.9 5.9 %sort.19.cloned.1.call-start = ((), (), s32[]{:S(2)}) async-start(), calls=%async_computation.4 | async-start | bytes 6176 | tf_op jit(solution)/shard_map/jit(argsort)/sort | solution.py:76
  45.2 281.6 %all-reduce.3.cloned.1.call-start = ((), (), s32[]{:S(2)}) async-start(), calls=%async_computation.2 | async-start | bytes 4194304 | tf_op jit(solution)/shard_map/psum | solution.py:85
  154.4 17.2 %slice-start = ((s8[8388608]{0:T(1024)(128)(4,1)}), s8[4194304]{0:T(1024)(128)(4,1)S(1)}, s32[]{:S(2)}) async-start(s8[8388608]{0:T(1024)(128)(4,1)} %bitcast.124), calls=%async_computation.6 | async-start | bytes 8388608
  160.2 11.5 %slice-start.1 = ((s8[8388608]{0:T(1024)(128)(4,1)}), s8[4194304]{0:T(1024)(128)(4,1)S(1)}, s32[]{:S(2)}) async-start(s8[8388608]{0:T(1024)(128)(4,1)} %bitcast.124), calls=%async_computation.7 | async-start | bytes 8388608
  175.4 1.9 copy-start.11
  175.4 3.0 copy-start.10
  176.9 341.7 %all-reduce.5.cloned.1.call-start = ((), (), s32[]{:S(2)}) async-start(), calls=%async_computation.3 | async-start | bytes 4194304 | tf_op jit(solution)/shard_map/psum | solution.py:85
  326.7 5.0 copy-start.4
  329.2 6.4 %copy-start.5 = (f32[2,256,1024]{2,1,0:T(8,128)S(1)}, f32[2,256,1024]{2,1,0:T(8,128)}, u32[]{:S(2)}) copy-start(f32[2,256,1024]{2,1,0:T(8,128)} %all-reduce.3.cloned.1.call-done) | copy-start | bytes 6291460
  329.2 6.4 %copy-start.8 = (f32[2,256,256]{2,1,0:T(8,128)S(1)}, f32[2,256,256]{2,1,0:T(8,128)}, u32[]{:S(2)}) copy-start(f32[2,256,256]{2,1,0:T(8,128)} %get-tuple-element.22) | copy-start | bytes 1572868
  341.7 7.8 %slice-start.2 = ((s8[8388608]{0:T(1024)(128)(4,1)}), s8[4194304]{0:T(1024)(128)(4,1)S(1)}, s32[]{:S(2)}) async-start(s8[8388608]{0:T(1024)(128)(4,1)} %bitcast.126), calls=%async_computation.8 | async-start | bytes 8388608
  345.6 3.9 copy-start
  345.6 3.9 slice-start.3
  349.6 3.8 copy-start.2
  368.3 1.6 copy-start.9
  369.8 148.8 %copy-start.7 = (f32[2,256,256]{2,1,0:T(8,128)S(1)}, f32[2,256,256]{2,1,0:T(8,128)}, u32[]{:S(2)}) copy-start(f32[2,256,256]{2,1,0:T(8,128)} %get-tuple-element.21) | copy-start | bytes 1572868
  520.9 6.3 %copy-start.6 = (f32[2,256,1024]{2,1,0:T(8,128)S(1)}, f32[2,256,1024]{2,1,0:T(8,128)}, u32[]{:S(2)}) copy-start(f32[2,256,1024]{2,1,0:T(8,128)} %all-reduce.5.cloned.1.call-done) | copy-start | bytes 6291460
  533.3 9.2 %slice-start.4 = ((s8[8388608]{0:T(1024)(128)(4,1)}), s8[4194304]{0:T(1024)(128)(4,1)S(1)}, s32[]{:S(2)}) async-start(s8[8388608]{0:T(1024)(128)(4,1)} %bitcast.128), calls=%async_computation.10 | async-start | bytes 8388608
  533.3 9.2 %copy-start.3 = (f32[1,1024,1024]{2,1,0:T(8,128)S(1)}, f32[1,1024,1024]{2,1,0:T(8,128)}, u32[]{:S(2)}) copy-start(f32[1,1024,1024]{2,1,0:T(8,128)} %copy-done.2) | copy-start | bytes 12582916
  537.3 5.2 slice-start.5
  537.3 5.2 copy-start.1
Sparse Core Ops, SparseCore 0:
  45.3 2.2 sort.21.cloned.1.call-done
  177.0 149.6 all-reduce.2
  369.9 148.6 all-reduce.4
  (1 shorter events, 0.0 us)
where the time goes:
time: 561 us; the launch traced here: 556 us
  waiting for transfers between devices  336 us (60%)
  matrix products  82.2 us (15%)
  other arithmetic  55.5 us (10%)
  local copies, waits for them, and re-layouts  45.8 us (8%)
  starting transfers between devices  22.2 us (4%)
  between operations  13.9 us (2%)
    psum x2, waiting for transfers between devices, reduce_strips(): return lax.psum(partial_sum, ('row', 'col'))  291 us
    dot_general x16, matrix products, matmul(): jnp.dot(first_op, second_op, precision=highest, preferred_element_type=jn...  46.4 us
    all_to_all x1, waiting for transfers between devices, per_device(): lax.all_to_all(outgoing, ('row', 'col'), split_axis=2, concat_axis=2, til...  44.9 us
    dot_general x8, matrix products, contract(): lax.dot_general(first_op, second_op, (((0,), (0,)), ((), ())), precision=...  35.8 us
    slice x1, other arithmetic, mask_panel(): imag_part = jnp.where(below, values[1], jnp.zeros_like(values[1]))  33.5 us
    gather x1, local copies, waits for them, and re-layouts, per_device(): placed = jnp.take_along_axis(arrived, ordering[:, None, :, None], axis=2)  14.6 us
    reshape x2, local copies, waits for them, and re-layouts, per_device(): panel_store.reshape(panel_count, 2, slot_count, block_rows * col_width)  12.2 us
    all_to_all x1, starting transfers between devices, per_device(): lax.all_to_all(labels, ('row', 'col'), split_axis=2, concat_axis=2, tiled...  11.5 us
  transfers between devices with their start and end apart: 4, of which 3 were waited for; matrix products, arithmetic and copies ran while one was open for 4% of the time, Pallas kernels for 0%

commit v1 on v0

v1 whole, which is shorter than its diff:
```python
import functools

import jax
import jax.numpy as jnp
from jax import lax
from jax.experimental import pallas as pl
from jax.experimental.pallas import tpu as pltpu
from jax.sharding import PartitionSpec as P


MESH = pl.DeviceIdType.MESH


def strip_of(x, y, z, core):
    return ((x * 2 + z % 2) * 4 + y) * 4 + (z // 2) * 2 + core


def exchange_kernel(rows, store_ref, ids_ref, blocks_ref, ids_out_ref, send_sem, recv_sem, id_send_sem, id_recv_sem, own_sem):
    row = lax.axis_index("row")
    col = lax.axis_index("col")
    me = row * 4 + col
    x = row // 8
    y = row % 4
    z = (col // 2) * 2 + (row // 4) % 2
    core = col % 2

    barrier = pltpu.get_barrier_semaphore()

    def greet(step, carry):
        peer = (me + step) % 128
        pl.semaphore_signal(barrier, inc=1, device_id=(peer // 4, peer % 4), device_id_type=MESH)
        return carry

    lax.fori_loop(1, 128, greet, 0)
    own_blocks = pltpu.make_async_copy(
        store_ref.at[:, :, pl.ds(pl.multiple_of(me * rows, rows), rows), :], blocks_ref.at[me], own_sem.at[0]
    )
    own_ids = pltpu.make_async_copy(ids_ref, ids_out_ref.at[me], own_sem.at[1])
    own_blocks.start()
    own_ids.start()
    pl.semaphore_wait(barrier, 127)

    def peer_of(step):
        spread = (step // 2 * 27) % 64
        return strip_of(
            (x + spread % 4) % 4, (y + (spread // 4) % 4) % 4, (z + spread // 16) % 4, (core + step) % 2
        )

    def copies(target, source):
        device = (target // 4, target % 4)
        return (
            pltpu.make_async_remote_copy(
                store_ref.at[:, :, pl.ds(pl.multiple_of(target * rows, rows), rows), :],
                blocks_ref.at[source],
                send_sem.at[target],
                recv_sem.at[source],
                device_id=device,
                device_id_type=MESH,
            ),
            pltpu.make_async_remote_copy(
                ids_ref,
                ids_out_ref.at[source],
                id_send_sem.at[target],
                id_recv_sem.at[source],
                device_id=device,
                device_id_type=MESH,
            ),
        )

    def send(step, carry):
        for copy in copies(peer_of(step), me):
            copy.start()
        return carry

    lax.fori_loop(1, 128, send, 0)
    own_blocks.wait()
    own_ids.wait()

    def finish(step, carry):
        peer = (me + step) % 128
        for copy in copies(peer, peer):
            copy.wait_recv()
            copy.wait_send()
        return carry

    lax.fori_loop(1, 128, finish, 0)


def exchange(panel_store, block_ids):
    panel_count, parts, row_count, col_width = panel_store.shape
    slot_count = block_ids.shape[1]
    rows = row_count // slot_count
    return pl.pallas_call(
        functools.partial(exchange_kernel, rows),
        out_shape=(
            jax.ShapeDtypeStruct((slot_count, panel_count, parts, rows, col_width), jnp.float32),
            jax.ShapeDtypeStruct((slot_count, panel_count, slot_count), jnp.int32),
        ),
        in_specs=[pl.BlockSpec(memory_space=pl.ANY)] * 2,
        out_specs=[pl.BlockSpec(memory_space=pl.ANY)] * 2,
        scratch_shapes=[
            pltpu.SemaphoreType.DMA((128,)),
            pltpu.SemaphoreType.DMA((128,)),
            pltpu.SemaphoreType.DMA((128,)),
            pltpu.SemaphoreType.DMA((128,)),
            pltpu.SemaphoreType.DMA((2,)),
        ],
        compiler_params=pltpu.CompilerParams(collective_id=0, has_side_effects=True),
        name="exchange",
    )(panel_store, block_ids)


VMEM_LIMIT = 60 * 1024 * 1024


def split(value):
    high = value.astype(jnp.bfloat16)
    return high, (value - high.astype(jnp.float32)).astype(jnp.bfloat16)


def dot(first_op, second_op):
    return jnp.dot(first_op, second_op, preferred_element_type=jnp.float32)


def split_dot(first_op, second_op):
    return (
        dot(first_op[0], second_op[0]) + dot(first_op[0], second_op[1]) + dot(first_op[1], second_op[0])
    )


def left_forms(real_part, imag_part):
    return split(real_part + imag_part), split(real_part), split(imag_part)


def right_forms(real_part, imag_part):
    return split(real_part), split(imag_part - real_part), split(real_part + imag_part)


def complex_dot(left, right):
    shared = split_dot(left[0], right[0])
    real_part = shared - split_dot(left[2], right[2])
    imag_part = shared + split_dot(left[1], right[1])
    return real_part, imag_part


def adjoint_upper(tri_ref, panel):
    shape = tri_ref.shape[2:]
    upper = lax.broadcasted_iota(jnp.int32, shape, 0) <= lax.broadcasted_iota(jnp.int32, shape, 1)
    return jnp.where(upper, tri_ref[panel, 0], 0.0).T, -jnp.where(upper, tri_ref[panel, 1], 0.0).T


def product_kernel(
    offsets_ref, ids_ref, blocks_ref, tri_ref, vectors_ref, y_ref, g_ref, x_ref, order_ref, slot_ref, panel_ref, left_ref, sem
):
    @pl.when(pl.program_id(0) == 0)
    def _():
        me = lax.axis_index("row") * 4 + lax.axis_index("col")
        source = lax.broadcasted_iota(jnp.int32, (128, 128), 0)
        lane = lax.broadcasted_iota(jnp.int32, (128, 128), 1)
        for panel in range(2):
            listed = jnp.sum(jnp.where(lane == me, ids_ref[:, panel, :], 0), axis=1, keepdims=True)
            place = listed - me * 128
            order_ref[panel : panel + 1, :] = jnp.sum(
                jnp.where(place == lane, source, 0), axis=0, keepdims=True
            )
        fetch = pltpu.make_async_copy(order_ref, slot_ref, sem)
        fetch.start()
        fetch.wait()

        def place_block(block, carry):
            first = pl.multiple_of(block * 8, 8)
            row_index = me * 1024 + block * 8 + lax.broadcasted_iota(jnp.int32, (8, 256), 0)
            for panel in range(2):
                slot = slot_ref[panel, block]
                limit = offsets_ref[panel] + lax.broadcasted_iota(jnp.int32, (8, 256), 1)
                below = row_index > limit
                diagonal = jnp.where(row_index == limit, 1.0, 0.0)
                panel_ref[0, panel, pl.ds(first, 8), :] = jnp.where(below, blocks_ref[slot, panel, 0], diagonal)
                panel_ref[1, panel, pl.ds(first, 8), :] = jnp.where(below, blocks_ref[slot, panel, 1], 0.0)
            return carry

        lax.fori_loop(0, 128, place_block, 0, unroll=4)

        for panel in range(2):
            for first in range(0, 1024, 256):
                forms = left_forms(
                    panel_ref[0, panel, first : first + 256, :].T, -panel_ref[1, panel, first : first + 256, :].T
                )
                for form in range(3):
                    for piece in range(2):
                        left_ref[form, piece, panel * 256 : (panel + 1) * 256, first : first + 256] = forms[form][piece]

        left = [(left_ref[form, 0, 256:512, :], left_ref[form, 1, 256:512, :]) for form in range(3)]
        real_part, imag_part = complex_dot(left, right_forms(panel_ref[0, 0], panel_ref[1, 0]))
        g_ref[0:256, :] = real_part[:, :128]
        g_ref[256:512, :] = real_part[:, 128:]
        g_ref[512:768, :] = imag_part[:, :128]
        g_ref[768:1024, :] = imag_part[:, 128:]

        for panel in range(2):
            factor = right_forms(*adjoint_upper(tri_ref, panel))

            def scale_rows(step, carry):
                rows = pl.ds(pl.multiple_of(step * 256, 256), 256)
                real_part, imag_part = complex_dot(
                    left_forms(panel_ref[0, panel, rows, :], panel_ref[1, panel, rows, :]), factor
                )
                x_ref[0, rows, panel * 256 : (panel + 1) * 256] = real_part
                x_ref[1, rows, panel * 256 : (panel + 1) * 256] = imag_part
                return carry

            lax.fori_loop(0, 4, scale_rows, 0)

    left = [(left_ref[form, 0], left_ref[form, 1]) for form in range(3)]
    real_part, imag_part = complex_dot(left, right_forms(vectors_ref[0], vectors_ref[1]))
    for tile in range(2):
        y_ref[tile, 0:512, :] = real_part[:, tile * 128 : (tile + 1) * 128]
        y_ref[tile, 512:1024, :] = imag_part[:, tile * 128 : (tile + 1) * 128]


def products(offsets, arrived_ids, arrived, tri_factors, vectors):
    f32 = jnp.float32
    whole = pl.BlockSpec(memory_space=pltpu.VMEM)
    return pl.pallas_call(
        product_kernel,
        grid=(4,),
        out_shape=(
            jax.ShapeDtypeStruct((8, 1024, 128), f32),
            jax.ShapeDtypeStruct((1024, 128), f32),
            jax.ShapeDtypeStruct((2, 1024, 512), f32),
        ),
        in_specs=[
            pl.BlockSpec(memory_space=pltpu.SMEM),
            whole,
            whole,
            whole,
            pl.BlockSpec((2, 1024, 256), lambda step: (0, 0, step)),
        ],
        out_specs=[pl.BlockSpec((2, 1024, 128), lambda step: (step, 0, 0)), whole, whole],
        scratch_shapes=[
            pltpu.VMEM((8, 128), jnp.int32),
            pltpu.SMEM((8, 128), jnp.int32),
            pltpu.VMEM((2, 2, 1024, 256), f32),
            pltpu.VMEM((3, 2, 512, 1024), jnp.bfloat16),
            pltpu.SemaphoreType.DMA,
        ],
        compiler_params=pltpu.CompilerParams(vmem_limit_bytes=VMEM_LIMIT, dimension_semantics=("arbitrary",)),
        name="products",
    )(offsets, arrived_ids, arrived, tri_factors, vectors)


TILES = 9
LINKS = 6


def sum_kernel(y_ref, g_ref, total_ref, held_ref, landed_ref, send_sem, recv_sem):
    row = lax.axis_index("row")
    col = lax.axis_index("col")
    x = row // 8
    y = row % 4
    z = (col // 2) * 2 + (row // 4) % 2
    core = col % 2

    def device(x, y, z, core):
        strip = strip_of(x, y, z, core)
        return (strip // 4, strip % 4)

    near = lambda place: place + 1 - 2 * (place % 2)
    far = lambda place: 3 - place
    near_bit = lambda place: ((place + 1) // 2) % 2
    far_bit = lambda place: place // 2
    links = [
        (device(near(x), y, z, core), near_bit(x)),
        (device(x, near(y), z, core), near_bit(y)),
        (device(x, y, near(z), core), near_bit(z)),
        (device(far(x), y, z, core), far_bit(x)),
        (device(x, far(y), z, core), far_bit(y)),
        (device(x, y, far(z), core), far_bit(z)),
    ]
    sibling = device(x, y, z, 1 - core)

    barrier = pltpu.get_barrier_semaphore()
    for peer in [sibling] + [link[0] for link in links]:
        pl.semaphore_signal(barrier, inc=1, device_id=peer, device_id_type=MESH)
    pl.semaphore_wait(barrier, LINKS + 1)

    def rows(first, count):
        return pl.ds(pl.multiple_of(first, 8), count)

    def given(tile):
        return g_ref if tile == 0 else y_ref.at[tile - 1]

    started = []

    def send(tile, step, source, target, peer):
        copy = pltpu.make_async_remote_copy(
            source,
            target,
            send_sem.at[tile, step],
            recv_sem.at[tile, step],
            device_id=peer,
            device_id_type=MESH,
        )
        copy.start()
        started.append(copy)
        return copy

    base = [0, 512, 768, 896, 960, 992, 1008]
    pending = []
    lows = [0] * TILES
    for tile in range(TILES):
        pending.append(
            send(
                tile,
                0,
                given(tile).at[rows((1 - core) * 512, 512), :],
                landed_ref.at[tile, pl.ds(0, 512), :],
                sibling,
            )
        )
    for step in range(LINKS + 1):
        size = 512 >> step
        for tile in range(TILES):
            pending[tile].wait_recv()
            low = lows[tile]
            arrived = landed_ref[tile, pl.ds(base[step], size), :]
            if step == 0:
                held_ref[tile, :, :] = given(tile)[rows(core * 512, 512), :] + arrived
            elif step < LINKS:
                held_ref[tile, rows(low, size), :] += arrived
            else:
                final = held_ref[tile, rows(low, size), :] + arrived
                total_ref[tile, rows(core * 512 + low, size), :] = final
            if step < LINKS:
                peer, bit = links[(tile + step) % LINKS]
                half = size // 2
                pending[tile] = send(
                    tile,
                    step + 1,
                    held_ref.at[tile, rows(low + (1 - bit) * half, half), :],
                    landed_ref.at[tile, pl.ds(base[step + 1], half), :],
                    peer,
                )
                lows[tile] = low + bit * half
    for step in range(LINKS + 1):
        size = 8 << step
        for tile in range(TILES):
            if step > 0:
                pending[tile].wait_recv()
                bit = links[(tile + LINKS - step) % LINKS][1]
                lows[tile] = lows[tile] - bit * (size // 2)
            peer = links[(tile + LINKS - 1 - step) % LINKS][0] if step < LINKS else sibling
            place = total_ref.at[tile, rows(core * 512 + lows[tile], size), :]
            pending[tile] = send(tile, LINKS + 1 + step, place, place, peer)
    for tile in range(TILES):
        pending[tile].wait_recv()
    for copy in started:
        copy.wait_send()


def sum_products(partial, gram):
    f32 = jnp.float32
    whole = pl.BlockSpec(memory_space=pltpu.VMEM)
    return pl.pallas_call(
        sum_kernel,
        out_shape=jax.ShapeDtypeStruct((TILES, 1024, 128), f32),
        in_specs=[whole, whole],
        out_specs=whole,
        scratch_shapes=[
            pltpu.VMEM((TILES, 512, 128), f32),
            pltpu.VMEM((TILES, 1024, 128), f32),
            pltpu.SemaphoreType.DMA((TILES, 2 * LINKS + 2)),
            pltpu.SemaphoreType.DMA((TILES, 2 * LINKS + 2)),
        ],
        compiler_params=pltpu.CompilerParams(
            vmem_limit_bytes=VMEM_LIMIT, collective_id=1, has_side_effects=True
        ),
        name="sum_products",
    )(partial, gram)


def update_kernel(g_ref, y_ref, x_ref, tri_ref, vectors_ref, out_ref, left_ref):
    @pl.when(pl.program_id(0) == 0)
    def _():
        gram = g_ref[0]
        gram_real = jnp.concatenate([gram[0:256], gram[256:512]], axis=1)
        gram_imag = jnp.concatenate([gram[512:768], gram[768:1024]], axis=1)
        cross = complex_dot(left_forms(gram_real, gram_imag), right_forms(*adjoint_upper(tri_ref, 0)))
        cross = right_forms(*cross)

        def correct_rows(step, carry):
            rows = pl.ds(pl.multiple_of(step * 256, 256), 256)
            second = (x_ref[0, rows, 256:512], x_ref[1, rows, 256:512])
            forms_second = left_forms(*second)
            real_part, imag_part = complex_dot(forms_second, cross)
            forms_first = left_forms(x_ref[0, rows, 0:256] - real_part, x_ref[1, rows, 0:256] - imag_part)
            for form in range(3):
                for piece in range(2):
                    left_ref[form, piece, rows, 0:256] = forms_first[form][piece]
                    left_ref[form, piece, rows, 256:512] = forms_second[form][piece]
            return carry

        lax.fori_loop(0, 4, correct_rows, 0)

    left = [(left_ref[form, 0], left_ref[form, 1]) for form in range(3)]
    summed = jnp.concatenate([y_ref[0], y_ref[1]], axis=1)
    real_part, imag_part = complex_dot(left, right_forms(summed[0:512], summed[512:1024]))
    out_ref[0] = vectors_ref[0] - real_part
    out_ref[1] = vectors_ref[1] - imag_part


def update(total, scaled, tri_factors, vectors):
    whole = pl.BlockSpec(memory_space=pltpu.VMEM)
    columns = pl.BlockSpec((2, 1024, 256), lambda step: (0, 0, step))
    return pl.pallas_call(
        update_kernel,
        grid=(4,),
        out_shape=jax.ShapeDtypeStruct(vectors.shape, jnp.float32),
        in_specs=[
            pl.BlockSpec((1, 1024, 128), lambda step: (0, 0, 0)),
            pl.BlockSpec((pl.Element(2), pl.Element(1024), pl.Element(128)), lambda step: (1 + 2 * step, 0, 0)),
            whole,
            whole,
            columns,
        ],
        out_specs=columns,
        scratch_shapes=[pltpu.VMEM((3, 2, 1024, 512), jnp.bfloat16)],
        compiler_params=pltpu.CompilerParams(vmem_limit_bytes=VMEM_LIMIT, dimension_semantics=("arbitrary",)),
        name="update",
    )(total, total, scaled, tri_factors, vectors)


def per_device(vectors, panel_store, block_ids, offsets, tri_factors):
    arrived, arrived_ids = exchange(panel_store, block_ids)
    partial, gram, scaled = products(offsets, arrived_ids, arrived, tri_factors, vectors)
    total = sum_products(partial, gram)
    return update(total, scaled, tri_factors, vectors)


def solution(mesh):
    placed = (
        P(None, ("row", "col"), None),
        P(None, None, ("row", "col"), None),
        P(None, ("row", "col")),
        P(),
        P(),
    )
    return jax.shard_map(
        per_device,
        mesh=mesh,
        in_specs=placed,
        out_specs=P(None, ("row", "col"), None),
        check_vma=False,
    )
```

time: 561 us -> 171 us (0.30)
  waiting for transfers between devices: 336 us -> 0 us
  Pallas kernels: 0 us -> 171 us
  matrix products: 82.2 us -> 0 us
  other arithmetic: 55.5 us -> 0 us
  local copies, waits for them, and re-layouts: 45.8 us -> 0 us
  starting transfers between devices: 22.2 us -> 0 us
  between operations: 13.9 us -> 0.02 us
    psum x2 -> x0, waiting for transfers between devices: 291 us -> none  [reduce_strips(): return lax.psum(partial_sum, ('row', 'col'))]
    pallas_call x0 -> x4, Pallas kernels: none -> 171 us  [the longest x1 69.8 us: exchange(): pl.pallas_call(functools.partial(exchange_kernel, rows), out_shape=(jax.S...]
    dot_general x24 -> x0, matrix products: 82.2 us -> none  [the longest x16 46.4 us: matmul(): jnp.dot(first_op, second_op, precision=highest, preferred_element_type=jn...]
    all_to_all x2 -> x0, waiting for transfers between devices: 44.9 us -> none  [the longest x1 44.9 us: per_device(): lax.all_to_all(outgoing, ('row', 'col'), split_axis=2, concat_axis=2, til...]
    slice x1 -> x0, other arithmetic: 33.5 us -> none  [mask_panel(): imag_part = jnp.where(below, values[1], jnp.zeros_like(values[1]))]
    all_to_all x2 -> x0, starting transfers between devices: 21.7 us -> none  [the longest x1 11.5 us: per_device(): lax.all_to_all(labels, ('row', 'col'), split_axis=2, concat_axis=2, tiled...]
    gather x1 -> x0, local copies, waits for them, and re-layouts: 14.6 us -> none  [per_device(): placed = jnp.take_along_axis(arrived, ordering[:, None, :, None], axis=2)]
    reshape x2 -> x0, local copies, waits for them, and re-layouts: 12.2 us -> none  [per_device(): panel_store.reshape(panel_count, 2, slot_count, block_rows * col_width)]
  transfers between devices with their start and end apart: 4 -> 0, of which waited for: 3 -> 0; matrix products, arithmetic and copies ran while one was open for 4% -> 0% of each run, Pallas kernels for 0% -> 0%
where the time goes in v1:
time: 171 us
  Pallas kernels  171 us (100%)
    pallas_call x1, Pallas kernels, exchange(): pl.pallas_call(functools.partial(exchange_kernel, rows), out_shape=(jax.S...  69.8 us
    pallas_call x1, Pallas kernels, sum_products(): pl.pallas_call(sum_kernel, out_shape=jax.ShapeDtypeStruct((TILES, 1024, 1...  60.4 us
    pallas_call x1, Pallas kernels, products(): pl.pallas_call(product_kernel, grid=(4,), out_shape=(jax.ShapeDtypeStruct...  22.7 us
    pallas_call x1, Pallas kernels, update(): pl.pallas_call(update_kernel, grid=(4,), out_shape=jax.ShapeDtypeStruct(v...  18.3 us

profile of v1, /device:TPU:1, one launch (start us, length us, event | category | flops | bytes accessed | tf_op | source)
XLA Modules:
  0.0 171.3 jit_solution(17576771689771835245)
XLA Ops:
  0.0 69.8 %exchange.1 = (f32[128,2,2,8,256]{4,3,2,1,0:T(8,128)}, s32[128,2,128]{2,1,0:T(2,128)}) custom-call(f32[2,2,1024,256]{3,2,1,0:T(8,128)} %store_ref.1, s32[2,128]{1,0:T(2,128)} %ids_ref.1), custom_call_target="tpu_custom_call" | custom-call | tf_op jit(solution)/shard_map/exchange/pallas_call | solution.py:93
  69.9 22.7 %products.1 = (f32[8,1024,128]{2,1,0:T(8,128)}, f32[1024,128]{1,0:T(8,128)}, f32[2,1024,512]{2,1,0:T(8,128)}) custom-call(s32[2]{0:T(128)} %offsets_ref.1, s32[128,2,128]{2,1,0:T(2,128)} %get-tuple-element.10.ids_ref, f32[128,2,2,8,256]{4,3,2,1,0:T(8,128)} %get-tuple-element.11.blocks_ref, f32[2,2,256,256]{3,2,1,0:T(8,128)} %tri_ref.3, ...), custom_call_target="tpu_custom_call" | custom-call | tf_op jit(solution)/shard_map/products/pallas_call | solution.py:224
  92.5 60.4 %sum_products.1.g_ref.y_ref = f32[9,1024,128]{2,1,0:T(8,128)} custom-call(f32[8,1024,128]{2,1,0:T(8,128)} %get-tuple-element.12.y_ref, f32[1024,128]{1,0:T(8,128)} %get-tuple-element.13.g_ref), custom_call_target="tpu_custom_call" | custom-call | tf_op jit(solution)/shard_map/sum_products/pallas_call | solution.py:364
  152.9 18.3 %update.1 = f32[2,1024,1024]{2,1,0:T(8,128)} custom-call(f32[9,1024,128]{2,1,0:T(8,128)} %sum_products.1.g_ref.y_ref, f32[9,1024,128]{2,1,0:T(8,128)} %sum_products.1.g_ref.y_ref, f32[2,1024,512]{2,1,0:T(8,128)} %get-tuple-element.14.x_ref, f32[2,2,256,256]{3,2,1,0:T(8,128)} %tri_ref.3, f32[2,1024,1024]{2,1,0:T(8,128)} %vectors_ref.3), custom_call_target="tpu_custom_call" | custom-call | tf_op jit(solution)/shard_map/update/pallas_call | solution.py:415

commit v2 on v1

--- a/solution.py
+++ b/solution.py
@@ -15,7 +15,23 @@
     return ((x * 2 + z % 2) * 4 + y) * 4 + (z // 2) * 2 + core
 
 
-def exchange_kernel(rows, store_ref, ids_ref, blocks_ref, ids_out_ref, send_sem, recv_sem, id_send_sem, id_recv_sem, own_sem):
+def exchange_kernel(
+    rows,
+    store_ref,
+    ids_ref,
+    blocks_ref,
+    ids_out_ref,
+    relay_ref,
+    send_sem,
+    recv_sem,
+    id_send_sem,
+    id_recv_sem,
+    hop_send_sem,
+    hop_recv_sem,
+    last_send_sem,
+    last_recv_sem,
+    own_sem,
+):
     row = lax.axis_index("row")
     col = lax.axis_index("col")
     me = row * 4 + col
@@ -32,55 +48,146 @@
         return carry
 
     lax.fori_loop(1, 128, greet, 0)
-    own_blocks = pltpu.make_async_copy(
-        store_ref.at[:, :, pl.ds(pl.multiple_of(me * rows, rows), rows), :], blocks_ref.at[me], own_sem.at[0]
-    )
+
+    def listed(strip):
+        return pl.ds(pl.multiple_of(strip * rows, rows), rows)
+
+    own_blocks = pltpu.make_async_copy(store_ref.at[:, :, listed(me), :], blocks_ref.at[me], own_sem.at[0])
     own_ids = pltpu.make_async_copy(ids_ref, ids_out_ref.at[me], own_sem.at[1])
     own_blocks.start()
     own_ids.start()
     pl.semaphore_wait(barrier, 127)
 
-    def peer_of(step):
+    def remote(source, target, sent, received, strip):
+        return pltpu.make_async_remote_copy(
+            source,
+            target,
+            sent,
+            received,
+            device_id=(strip // 4, strip % 4),
+            device_id_type=MESH,
+        )
+
+    def offset(step):
         spread = (step // 2 * 27) % 64
-        return strip_of(
-            (x + spread % 4) % 4, (y + (spread // 4) % 4) % 4, (z + spread // 16) % 4, (core + step) % 2
+        return spread % 4, (spread // 4) % 4, spread // 16
+
+    def opposite(shift):
+        return (shift // 2) * (1 - shift % 2)
+
+    def has_opposite(step):
+        dx, dy, dz = offset(step)
+        return opposite(dx) + opposite(dy) + opposite(dz) > 0
+
+    def shifted(step, sign, core):
+        dx, dy, dz = offset(step)
+        return strip_of((x + sign * dx + 4) % 4, (y + sign * dy + 4) % 4, (z + sign * dz + 4) % 4, core)
+
+    def target_of(step):
+        return shifted(step, 1, (core + step) % 2)
+
+    def origin_of(step):
+        return shifted(step, -1, (core + step) % 2)
+
+    def relay_of(step):
+        dx, dy, dz = offset(step)
+        return strip_of((x + 4 - opposite(dx)) % 4, (y + 4 - opposite(dy)) % 4, (z + 4 - opposite(dz)) % 4, core)
+
+    def relayed_origin(step):
+        dx, dy, dz = offset(step)
+        return (x + opposite(dx)) % 4, (y + opposite(dy)) % 4, (z + opposite(dz)) % 4
+
+    def relayed_target(step):
+        dx, dy, dz = offset(step)
+        from_x, from_y, from_z = relayed_origin(step)
+        return strip_of((from_x + dx) % 4, (from_y + dy) % 4, (from_z + dz) % 4, (core + step) % 2)
+
+    def whole_copy(step, strip, source):
+        return remote(
+            store_ref.at[:, :, listed(strip), :], blocks_ref.at[source], send_sem.at[step], recv_sem.at[step], strip
         )
 
-    def copies(target, source):
-        device = (target // 4, target % 4)
-        return (
-            pltpu.make_async_remote_copy(
-                store_ref.at[:, :, pl.ds(pl.multiple_of(target * rows, rows), rows), :],
-                blocks_ref.at[source],
-                send_sem.at[target],
-                recv_sem.at[source],
-                device_id=device,
-                device_id_type=MESH,
-            ),
-            pltpu.make_async_remote_copy(
-                ids_ref,
-                ids_out_ref.at[source],
-                id_send_sem.at[target],
-                id_recv_sem.at[source],
-                device_id=device,
-                device_id_type=MESH,
-            ),
+    def first_panel_copy(step, strip, source):
+        return remote(
+            store_ref.at[0, :, listed(strip), :],
+            blocks_ref.at[source, 0],
+            send_sem.at[step],
+            recv_sem.at[step],
+            strip,
         )
 
+    def hop_copy(step):
+        return remote(
+            store_ref.at[1, :, listed(target_of(step)), :],
+            relay_ref.at[step],
+            hop_send_sem.at[step],
+            hop_recv_sem.at[step],
+            relay_of(step),
+        )
+
+    def last_copy(step, strip, source):
+        return remote(
+            relay_ref.at[step], blocks_ref.at[source, 1], last_send_sem.at[step], last_recv_sem.at[step], strip
+        )
+
+    def id_copy(step, strip, source):
+        return remote(ids_ref, ids_out_ref.at[source], id_send_sem.at[step], id_recv_sem.at[step], strip)
+
+    def send_ids(step, carry):
+        id_copy(step, target_of(step), me).start()
+        return carry
+
     def send(step, carry):
-        for copy in copies(peer_of(step), me):
-            copy.start()
+        opposed = has_opposite(step)
+
+        @pl.when(opposed)
+        def _():
+            hop_copy(step).start()
+            first_panel_copy(step, target_of(step), me).start()
+
+        @pl.when(jnp.logical_not(opposed))
+        def _():
+            whole_copy(step, target_of(step), me).start()
+
         return carry
 
-    lax.fori_loop(1, 128, send, 0)
+    def forward(step, carry):
+        @pl.when(has_opposite(step))
+        def _():
+            hop_copy(step).wait_recv()
+            last_copy(step, relayed_target(step), strip_of(*relayed_origin(step), core)).start()
+
+        return carry
+
+    lead = 24
+    lax.fori_loop(1, lead + 1, send, 0)
+    lax.fori_loop(1, 128, send_ids, 0)
+
+    def both(step, carry):
+        send(step + lead, carry)
+        return forward(step, carry)
+
+    lax.fori_loop(1, 128 - lead, both, 0)
+    lax.fori_loop(128 - lead, 128, forward, 0)
     own_blocks.wait()
     own_ids.wait()
 
     def finish(step, carry):
-        peer = (me + step) % 128
-        for copy in copies(peer, peer):
-            copy.wait_recv()
-            copy.wait_send()
+        strip = target_of(step)
+        source = origin_of(step)
+        id_copy(step, strip, source).wait()
+        opposed = has_opposite(step)
+
+        @pl.when(opposed)
+        def _():
+            first_panel_copy(step, strip, source).wait()
+            hop_copy(step).wait_send()
+            last_copy(step, strip, source).wait()
+
+        @pl.when(jnp.logical_not(opposed))
+        def _():
+            whole_copy(step, strip, source).wait()
+
         return carry
 
     lax.fori_loop(1, 128, finish, 0)
@@ -98,13 +205,9 @@
         ),
         in_specs=[pl.BlockSpec(memory_space=pl.ANY)] * 2,
         out_specs=[pl.BlockSpec(memory_space=pl.ANY)] * 2,
-        scratch_shapes=[
-            pltpu.SemaphoreType.DMA((128,)),
-            pltpu.SemaphoreType.DMA((128,)),
-            pltpu.SemaphoreType.DMA((128,)),
-            pltpu.SemaphoreType.DMA((128,)),
-            pltpu.SemaphoreType.DMA((2,)),
-        ],
+        scratch_shapes=[pltpu.VMEM((slot_count, parts, rows, col_width), jnp.float32)]
+        + [pltpu.SemaphoreType.DMA((128,))] * 8
+        + [pltpu.SemaphoreType.DMA((2,))],
         compiler_params=pltpu.CompilerParams(collective_id=0, has_side_effects=True),
         name="exchange",
     )(panel_store, block_ids)
@@ -250,39 +353,73 @@
 
 
 TILES = 9
-LINKS = 6
+STAGES = 10
+
+
+def arrival_order():
+    free = [0.0] * 7
+    ready = []
+    for tile in range(TILES):
+        free[6] += 0.45
+        ready.append((free[6] + 1.5, tile, 0))
+    order = []
+    now = 0.0
+    while ready:
+        ready.sort()
+        arrived, tile, stage = ready.pop(0)
+        order.append((tile, stage))
+        now = max(now, arrived) + 0.15
+        following = stage + 1
+        if following == STAGES:
+            continue
+        if following in (4, 5):
+            finish = now + 0.3
+        else:
+            if following == 9:
+                link, cost = 6, 0.45
+            elif following < 4:
+                link, cost = (tile + following - 1) % 6, 2.7 / 2 ** (following - 1)
+            else:
+                link, cost = (tile + 8 - following) % 6, 2.7 / 2 ** (8 - following)
+            free[link] = max(free[link], now) + cost
+            finish = free[link]
+        ready.append((finish + 1.5, tile, following))
+    return order
 
 
 def sum_kernel(y_ref, g_ref, total_ref, held_ref, landed_ref, send_sem, recv_sem):
     row = lax.axis_index("row")
     col = lax.axis_index("col")
-    x = row // 8
-    y = row % 4
-    z = (col // 2) * 2 + (row // 4) % 2
+    here = (row // 8, row % 4, (col // 2) * 2 + (row // 4) % 2)
     core = col % 2
 
-    def device(x, y, z, core):
-        strip = strip_of(x, y, z, core)
+    def device(place, core):
+        strip = strip_of(*place, core)
         return (strip // 4, strip % 4)
 
-    near = lambda place: place + 1 - 2 * (place % 2)
-    far = lambda place: 3 - place
-    near_bit = lambda place: ((place + 1) // 2) % 2
-    far_bit = lambda place: place // 2
-    links = [
-        (device(near(x), y, z, core), near_bit(x)),
-        (device(x, near(y), z, core), near_bit(y)),
-        (device(x, y, near(z), core), near_bit(z)),
-        (device(far(x), y, z, core), far_bit(x)),
-        (device(x, far(y), z, core), far_bit(y)),
-        (device(x, y, far(z), core), far_bit(z)),
-    ]
-    sibling = device(x, y, z, 1 - core)
+    near = [place + 1 - 2 * (place % 2) for place in here]
+    far = [3 - place for place in here]
+    sibling = device(here, 1 - core)
+    other = near + far
+    bits = [((place + 1) // 2) % 2 for place in here] + [place // 2 for place in here]
+
+    def across(links):
+        place = list(here)
+        for link in links:
+            place[link % 3] = other[link]
+        return device(place, core)
 
     barrier = pltpu.get_barrier_semaphore()
-    for peer in [sibling] + [link[0] for link in links]:
+    peers = [sibling]
+    for first in (None, 0, 3):
+        for second in (None, 1, 4):
+            for third in (None, 2, 5):
+                chosen = [link for link in (first, second, third) if link is not None]
+                if chosen:
+                    peers.append(across(chosen))
+    for peer in peers:
         pl.semaphore_signal(barrier, inc=1, device_id=peer, device_id_type=MESH)
-    pl.semaphore_wait(barrier, LINKS + 1)
+    pl.semaphore_wait(barrier, len(peers))
 
     def rows(first, count):
         return pl.ds(pl.multiple_of(first, 8), count)
@@ -290,72 +427,98 @@
     def given(tile):
         return g_ref if tile == 0 else y_ref.at[tile - 1]
 
-    started = []
-
-    def send(tile, step, source, target, peer):
-        copy = pltpu.make_async_remote_copy(
+    def send(tile, stage, source, target, peer):
+        pltpu.make_async_remote_copy(
             source,
             target,
-            send_sem.at[tile, step],
-            recv_sem.at[tile, step],
+            send_sem.at[tile, stage],
+            recv_sem.at[tile, stage],
             device_id=peer,
             device_id_type=MESH,
-        )
-        copy.start()
-        started.append(copy)
-        return copy
-
-    base = [0, 512, 768, 896, 960, 992, 1008]
-    pending = []
+        ).start()
+
+    counts = [512, 256, 128, 64, 56, 56, 64, 128, 256, 512]
+    base = [0, 512, 768, 896, 960]
+
+    def wait(tile, stage, sem):
+        some = landed_ref.at[tile, pl.ds(0, counts[stage]), :]
+        pltpu.make_async_copy(some, some, sem.at[tile, stage]).wait()
+
+    def order_of(tile):
+        return [(tile + step) % 6 for step in range(6)]
+
+    def eighth(tile, flips=0):
+        index = 0
+        for place, link in enumerate(order_of(tile)[3:]):
+            bit = 1 - bits[link] if flips & (4 >> place) else bits[link]
+            index = index * 2 + bit
+        return index
+
+    def flipped(tile, flips):
+        return across([link for place, link in enumerate(order_of(tile)[3:]) if flips & (4 >> place)])
+
     lows = [0] * TILES
-    for tile in range(TILES):
-        pending.append(
+
+    def total_rows(tile, count):
+        return total_ref.at[tile, rows(core * 512 + lows[tile], count), :]
+
+    def advance(tile, stage):
+        order = order_of(tile)
+        low = lows[tile]
+        if stage == 0:
+            held_ref[tile, :, :] = given(tile)[rows(core * 512, 512), :] + landed_ref[tile, 0:512, :]
+        elif stage < 4:
+            size = counts[stage]
+            held_ref[tile, rows(low, size), :] += landed_ref[tile, base[stage] : base[stage] + size, :]
+        elif stage == 4:
+            own = rows(low + eighth(tile) * 8, 8)
+            final = held_ref[tile, own, :]
+            for flips in range(1, 8):
+                final += landed_ref[tile, base[4] + flips * 8 - 8 : base[4] + flips * 8, :]
+            total_ref[tile, rows(core * 512 + low + eighth(tile) * 8, 8), :] = final
+        if stage < 3:
+            size = counts[stage + 1]
+            link = order[stage]
+            keep = bits[link]
             send(
                 tile,
-                0,
-                given(tile).at[rows((1 - core) * 512, 512), :],
-                landed_ref.at[tile, pl.ds(0, 512), :],
-                sibling,
+                stage + 1,
+                held_ref.at[tile, rows(low + (1 - keep) * size, size), :],
+                landed_ref.at[tile, pl.ds(base[stage + 1], size), :],
+                across([link]),
             )
-        )
-    for step in range(LINKS + 1):
-        size = 512 >> step
-        for tile in range(TILES):
-            pending[tile].wait_recv()
-            low = lows[tile]
-            arrived = landed_ref[tile, pl.ds(base[step], size), :]
-            if step == 0:
-                held_ref[tile, :, :] = given(tile)[rows(core * 512, 512), :] + arrived
-            elif step < LINKS:
-                held_ref[tile, rows(low, size), :] += arrived
-            else:
-                final = held_ref[tile, rows(low, size), :] + arrived
-                total_ref[tile, rows(core * 512 + low, size), :] = final
-            if step < LINKS:
-                peer, bit = links[(tile + step) % LINKS]
-                half = size // 2
-                pending[tile] = send(
+            lows[tile] = low + keep * size
+        elif stage == 3:
+            for flips in range(1, 8):
+                send(
                     tile,
-                    step + 1,
-                    held_ref.at[tile, rows(low + (1 - bit) * half, half), :],
-                    landed_ref.at[tile, pl.ds(base[step + 1], half), :],
-                    peer,
+                    4,
+                    held_ref.at[tile, rows(low + eighth(tile, flips) * 8, 8), :],
+                    landed_ref.at[tile, pl.ds(base[4] + flips * 8 - 8, 8), :],
+                    flipped(tile, flips),
                 )
-                lows[tile] = low + bit * half
-    for step in range(LINKS + 1):
-        size = 8 << step
-        for tile in range(TILES):
-            if step > 0:
-                pending[tile].wait_recv()
-                bit = links[(tile + LINKS - step) % LINKS][1]
-                lows[tile] = lows[tile] - bit * (size // 2)
-            peer = links[(tile + LINKS - 1 - step) % LINKS][0] if step < LINKS else sibling
-            place = total_ref.at[tile, rows(core * 512 + lows[tile], size), :]
-            pending[tile] = send(tile, LINKS + 1 + step, place, place, peer)
+        elif stage == 4:
+            place = total_ref.at[tile, rows(core * 512 + low + eighth(tile) * 8, 8), :]
+            for flips in range(1, 8):
+                send(tile, 5, place, place, flipped(tile, flips))
+        elif stage < 8:
+            if stage > 5:
+                lows[tile] = low - bits[order[8 - stage]] * counts[stage]
+            place = total_rows(tile, counts[stage + 1])
+            send(tile, stage + 1, place, place, across([order[7 - stage]]))
+        elif stage == 8:
+            lows[tile] = low - bits[order[0]] * counts[stage]
+            place = total_rows(tile, 512)
+            send(tile, 9, place, place, sibling)
+
     for tile in range(TILES):
-        pending[tile].wait_recv()
-    for copy in started:
-        copy.wait_send()
+        send(tile, 0, given(tile).at[rows((1 - core) * 512, 512), :], landed_ref.at[tile, pl.ds(0, 512), :], sibling)
+    for tile, stage in arrival_order():
+        wait(tile, stage, recv_sem)
+        advance(tile, stage)
+    for tile in range(TILES):
+        for stage in range(STAGES):
+            wait(tile, stage, send_sem)
 
 
 def sum_products(partial, gram):
@@ -369,8 +532,8 @@
         scratch_shapes=[
             pltpu.VMEM((TILES, 512, 128), f32),
             pltpu.VMEM((TILES, 1024, 128), f32),
-            pltpu.SemaphoreType.DMA((TILES, 2 * LINKS + 2)),
-            pltpu.SemaphoreType.DMA((TILES, 2 * LINKS + 2)),
+            pltpu.SemaphoreType.DMA((TILES, STAGES)),
+            pltpu.SemaphoreType.DMA((TILES, STAGES)),
         ],
         compiler_params=pltpu.CompilerParams(
             vmem_limit_bytes=VMEM_LIMIT, collective_id=1, has_side_effects=True

time: 171 us -> 185 us (1.082)
  Pallas kernels: 171 us -> 185 us
    pallas_call x1, Pallas kernels: 69.8 us -> 87.7 us  [exchange(): pl.pallas_call(functools.partial(exchange_kernel, rows), out_shape=(jax.S...]
    pallas_call x1, Pallas kernels: 60.4 us -> 55.9 us  [sum_products(): pl.pallas_call(sum_kernel, out_shape=jax.ShapeDtypeStruct((TILES, 1024, 1...]
where the time goes in v2:
time: 185 us
  Pallas kernels  185 us (100%)
    pallas_call x1, Pallas kernels, exchange(): pl.pallas_call(functools.partial(exchange_kernel, rows), out_shape=(jax.S...  87.7 us
    pallas_call x1, Pallas kernels, sum_products(): pl.pallas_call(sum_kernel, out_shape=jax.ShapeDtypeStruct((TILES, 1024, 1...  55.9 us
    pallas_call x1, Pallas kernels, products(): pl.pallas_call(product_kernel, grid=(4,), out_shape=(jax.ShapeDtypeStruct...  22.6 us
    pallas_call x1, Pallas kernels, update(): pl.pallas_call(update_kernel, grid=(4,), out_shape=jax.ShapeDtypeStruct(v...  18.5 us

profile of v2, /device:TPU:1, one launch (start us, length us, event | category | flops | bytes accessed | tf_op | source)
XLA Modules:
  0.0 184.8 jit_solution(13188150190484231927)
XLA Ops:
  0.0 87.7 %exchange.1 = (f32[128,2,2,8,256]{4,3,2,1,0:T(8,128)}, s32[128,2,128]{2,1,0:T(2,128)}) custom-call(f32[2,2,1024,256]{3,2,1,0:T(8,128)} %store_ref.1, s32[2,128]{1,0:T(2,128)} %ids_ref.1), custom_call_target="tpu_custom_call" | custom-call | tf_op jit(solution)/shard_map/exchange/pallas_call | solution.py:200
  87.8 22.6 %products.1 = (f32[8,1024,128]{2,1,0:T(8,128)}, f32[1024,128]{1,0:T(8,128)}, f32[2,1024,512]{2,1,0:T(8,128)}) custom-call(s32[2]{0:T(128)} %offsets_ref.1, s32[128,2,128]{2,1,0:T(2,128)} %get-tuple-element.10.ids_ref, f32[128,2,2,8,256]{4,3,2,1,0:T(8,128)} %get-tuple-element.11.blocks_ref, f32[2,2,256,256]{3,2,1,0:T(8,128)} %tri_ref.3, ...), custom_call_target="tpu_custom_call" | custom-call | tf_op jit(solution)/shard_map/products/pallas_call | solution.py:327
  110.4 55.9 %sum_products.1.g_ref.y_ref = f32[9,1024,128]{2,1,0:T(8,128)} custom-call(f32[8,1024,128]{2,1,0:T(8,128)} %get-tuple-element.12.y_ref, f32[1024,128]{1,0:T(8,128)} %get-tuple-element.13.g_ref), custom_call_target="tpu_custom_call" | custom-call | tf_op jit(solution)/shard_map/sum_products/pallas_call | solution.py:527
  166.3 18.5 %update.1 = f32[2,1024,1024]{2,1,0:T(8,128)} custom-call(f32[9,1024,128]{2,1,0:T(8,128)} %sum_products.1.g_ref.y_ref, f32[9,1024,128]{2,1,0:T(8,128)} %sum_products.1.g_ref.y_ref, f32[2,1024,512]{2,1,0:T(8,128)} %get-tuple-element.14.x_ref, f32[2,2,256,256]{3,2,1,0:T(8,128)} %tri_ref.3, f32[2,1024,1024]{2,1,0:T(8,128)} %vectors_ref.3), custom_call_target="tpu_custom_call" | custom-call | tf_op jit(solution)/shard_map/update/pallas_call | solution.py:578

commit v3 on v0

v3 whole, which is shorter than its diff:
```python
import jax
import jax.numpy as jnp
from jax import lax
from jax.experimental import pallas as pl
from jax.experimental.pallas import tpu as pltpu
from jax.sharding import PartitionSpec as P


MESH = pl.DeviceIdType.MESH


def strip_of(x, y, z, core):
    return ((x * 2 + z % 2) * 4 + y) * 4 + (z // 2) * 2 + core


VMEM_LIMIT = 60 * 1024 * 1024


def split(value):
    high = value.astype(jnp.bfloat16)
    return high, (value - high.astype(jnp.float32)).astype(jnp.bfloat16)


def dot(first_op, second_op):
    return jnp.dot(first_op, second_op, preferred_element_type=jnp.float32)


def split_dot(first_op, second_op):
    return (
        dot(first_op[0], second_op[0]) + dot(first_op[0], second_op[1]) + dot(first_op[1], second_op[0])
    )


def left_forms(real_part, imag_part):
    return split(real_part + imag_part), split(real_part), split(imag_part)


def right_forms(real_part, imag_part):
    return split(real_part), split(imag_part - real_part), split(real_part + imag_part)


def complex_dot(left, right):
    shared = split_dot(left[0], right[0])
    real_part = shared - split_dot(left[2], right[2])
    imag_part = shared + split_dot(left[1], right[1])
    return real_part, imag_part


def adjoint_upper(tri_ref, panel):
    shape = tri_ref.shape[2:]
    upper = lax.broadcasted_iota(jnp.int32, shape, 0) <= lax.broadcasted_iota(jnp.int32, shape, 1)
    return jnp.where(upper, tri_ref[panel, 0], 0.0).T, -jnp.where(upper, tri_ref[panel, 1], 0.0).T


TILES = 8
STAGES = 10
COUNTS = [256, 128, 64, 32, 56, 24, 32, 64, 128, 256]
BASES = [0, 256, 384, 448, 480]


def arrival_order(chunk_cost, last_stage):
    free = [0.0] * 7
    ready = []
    order = []
    now = 0.0
    chunk = 0
    while ready or chunk < TILES // 2:
        ready.sort()
        if chunk < TILES // 2 and (not ready or ready[0][0] > now):
            order.append((chunk, None))
            now += chunk_cost
            for tile in (2 * chunk, 2 * chunk + 1):
                free[6] = max(free[6], now) + 0.3
                ready.append((free[6] + 1.6, tile, 0))
            chunk += 1
            continue
        arrived, tile, stage = ready.pop(0)
        order.append((tile, stage))
        now = max(now, arrived) + 0.15
        following = stage + 1
        if following > last_stage:
            continue
        if following in (4, 5):
            finish = now + 0.3
        else:
            if following == 9:
                link, cost = 6, 0.3
            elif following < 4:
                link, cost = (tile + following - 1) % 6, 2.0 / 2 ** (following - 1)
            else:
                link, cost = (tile + 8 - following) % 6, 2.0 / 2 ** (8 - following)
            free[link] = max(free[link], now) + cost
            finish = free[link]
        ready.append((finish + 1.6, tile, following))
    return order


def main_kernel(
    offsets_ref,
    ids_ref,
    store_ref,
    tri_ref,
    vectors_ref,
    y_out_ref,
    x_out_ref,
    z_out_ref,
    z_ref,
    first_blocks_ref,
    second_blocks_ref,
    all_ids_ref,
    order_ref,
    slot_ref,
    panel_ref,
    left_ref,
    x_ref,
    part_ref,
    held_ref,
    landed_ref,
    total_ref,
    block_send_sem,
    block_recv_sem,
    id_send_sem,
    id_recv_sem,
    send_sem,
    recv_sem,
    local_sem,
):
    blocks_refs = (first_blocks_ref, second_blocks_ref)
    row = lax.axis_index("row")
    col = lax.axis_index("col")
    me = row * 4 + col
    x = row // 8
    y = row % 4
    z = (col // 2) * 2 + (row // 4) % 2
    here = (x, y, z)
    core = col % 2

    barrier = pltpu.get_barrier_semaphore()

    def greet(step, carry):
        peer = (me + step) % 128
        pl.semaphore_signal(barrier, inc=1, device_id=(peer // 4, peer % 4), device_id_type=MESH)
        return carry

    lax.fori_loop(1, 128, greet, 0)

    def listed(strip):
        return pl.ds(pl.multiple_of(strip * 8, 8), 8)

    fetch_vectors = pltpu.make_async_copy(vectors_ref, z_ref, local_sem.at[0])
    fetch_blocks = [
        pltpu.make_async_copy(
            store_ref.at[panel, :, listed(me), :], blocks_refs[panel].at[me], local_sem.at[1 + 9 * panel]
        )
        for panel in range(2)
    ]
    fetch_ids = pltpu.make_async_copy(ids_ref, all_ids_ref.at[me], local_sem.at[2])
    fetch_blocks[0].start()
    fetch_blocks[1].start()
    fetch_ids.start()
    pl.semaphore_wait(barrier, 127)

    def strip_at(step, sign):
        spread = (step // 2 * 27) % 64
        return strip_of(
            (x + sign * (spread % 4) + 4) % 4,
            (y + sign * ((spread // 4) % 4) + 4) % 4,
            (z + sign * (spread // 16) + 4) % 4,
            (core + step) % 2,
        )

    def block_copy(panel, step, strip, source):
        return pltpu.make_async_remote_copy(
            store_ref.at[panel, :, listed(strip), :],
            blocks_refs[panel].at[source],
            block_send_sem.at[panel, step],
            block_recv_sem.at[panel, step],
            device_id=(strip // 4, strip % 4),
            device_id_type=MESH,
        )

    def id_copy(step, strip, source):
        return pltpu.make_async_remote_copy(
            ids_ref,
            all_ids_ref.at[source],
            id_send_sem.at[step],
            id_recv_sem.at[step],
            device_id=(strip // 4, strip % 4),
            device_id_type=MESH,
        )

    def send_ids(step, carry):
        id_copy(step, strip_at(step, 1), me).start()
        return carry

    def send_blocks(panel, first, last):
        def body(step, carry):
            block_copy(panel, step, strip_at(step, 1), me).start()
            return carry

        lax.fori_loop(first, last, body, 0)

    def wait_blocks(panel):
        def body(step, carry):
            block_copy(panel, step, strip_at(step, 1), strip_at(step, -1)).wait_recv()
            return carry

        lax.fori_loop(1, 128, body, 0)

    send_blocks(0, 1, 32)
    lax.fori_loop(1, 128, send_ids, 0)
    send_blocks(0, 32, 128)
    fetch_vectors.start()
    send_blocks(1, 1, 24)
    next_block = [24]

    def send_some(count):
        first = next_block[0]
        last = min(first + count, 128)
        if last > first:
            send_blocks(1, first, last)
        next_block[0] = last

    fetch_blocks[0].wait()
    fetch_blocks[1].wait()
    fetch_ids.wait()

    def wait_ids(step, carry):
        id_copy(step, strip_at(step, 1), strip_at(step, -1)).wait_recv()
        return carry

    lax.fori_loop(1, 128, wait_ids, 0)
    source_index = lax.broadcasted_iota(jnp.int32, (128, 128), 0)
    lane = lax.broadcasted_iota(jnp.int32, (128, 128), 1)
    order_ref[...] = jnp.zeros_like(order_ref)
    for panel in range(2):
        own = jnp.sum(jnp.where(lane == me, all_ids_ref[:, panel, :], 0), axis=1, keepdims=True)
        order_ref[panel : panel + 1, :] = jnp.max(
            jnp.where(own - me * 128 == lane, source_index, 0), axis=0, keepdims=True
        )
    fetch_order = pltpu.make_async_copy(order_ref, slot_ref, local_sem.at[3])
    fetch_order.start()
    fetch_order.wait()
    fetch_vectors.wait()

    def place_panel(panel):
        def place_block(block, carry):
            first = pl.multiple_of(block * 8, 8)
            row_index = me * 1024 + block * 8 + lax.broadcasted_iota(jnp.int32, (8, 256), 0)
            slot = slot_ref[panel, block]
            limit = offsets_ref[panel] + lax.broadcasted_iota(jnp.int32, (8, 256), 1)
            below = row_index > limit
            diagonal = jnp.where(row_index == limit, 1.0, 0.0)
            panel_ref[0, pl.ds(first, 8), :] = jnp.where(below, blocks_refs[panel][slot, 0], diagonal)
            panel_ref[1, pl.ds(first, 8), :] = jnp.where(below, blocks_refs[panel][slot, 1], 0.0)
            return carry

        lax.fori_loop(0, 128, place_block, 0, unroll=4)

        def turn(step, carry):
            rows = pl.ds(pl.multiple_of(step * 256, 256), 256)
            forms = left_forms(panel_ref[0, rows, :].T, -panel_ref[1, rows, :].T)
            for form in range(3):
                for piece in range(2):
                    left_ref[form, piece * 256 : (piece + 1) * 256, rows] = forms[form][piece]
            return carry

        lax.fori_loop(0, 4, turn, 0)

    def scale_panel(panel):
        factor = right_forms(*adjoint_upper(tri_ref, panel))

        def scale_rows(step, carry):
            rows = pl.ds(pl.multiple_of(step * 256, 256), 256)
            scaled = complex_dot(left_forms(panel_ref[0, rows, :], panel_ref[1, rows, :]), factor)
            forms = left_forms(*scaled)
            for form in range(3):
                for piece in range(2):
                    x_ref[form, piece, rows, :] = forms[form][piece]
            return carry

        lax.fori_loop(0, 4, scale_rows, 0)

    def chunk_columns(chunk):
        return slice(chunk * 256, (chunk + 1) * 256)

    def form_products(panel, chunk):
        columns = chunk_columns(chunk)
        forms = right_forms(z_ref[0, :, columns], z_ref[1, :, columns])
        sums = []
        for form in range(3):
            high, low = forms[form]
            both = dot(left_ref[form], high)
            sums.append(both[0:256] + both[256:512] + dot(left_ref[form, 0:256, :], low))
        real_part = sums[0] - sums[2]
        imag_part = sums[0] + sums[1]
        for side in range(2):
            part_ref[panel, 2 * chunk + side, 0:256, :] = real_part[:, side * 128 : (side + 1) * 128]
            part_ref[panel, 2 * chunk + side, 256:512, :] = imag_part[:, side * 128 : (side + 1) * 128]

    def apply_first(chunk):
        columns = chunk_columns(chunk)
        summed = jnp.concatenate([total_ref[0, 2 * chunk], total_ref[0, 2 * chunk + 1]], axis=1)
        forms = right_forms(summed[0:256], summed[256:512])

        def apply_rows(step, carry):
            rows = pl.ds(pl.multiple_of(step * 512, 512), 512)
            left = [(x_ref[form, 0, rows, :], x_ref[form, 1, rows, :]) for form in range(3)]
            real_part, imag_part = complex_dot(left, forms)
            z_ref[0, rows, columns] -= real_part
            z_ref[1, rows, columns] -= imag_part
            return carry

        lax.fori_loop(0, 2, apply_rows, 0)
        copy = pltpu.make_async_copy(z_ref.at[:, :, columns], z_out_ref.at[:, :, columns], local_sem.at[4 + chunk])
        copy.start()
        return copy

    def device(place, core):
        strip = strip_of(*place, core)
        return (strip // 4, strip % 4)

    sibling = device(here, 1 - core)
    other = [place + 1 - 2 * (place % 2) for place in here] + [3 - place for place in here]
    bits = [((place + 1) // 2) % 2 for place in here] + [place // 2 for place in here]

    def across(links):
        place = list(here)
        for link in links:
            place[link % 3] = other[link]
        return device(place, core)

    def rows_at(first, count):
        return pl.ds(pl.multiple_of(first, 8), count)

    def send(panel, tile, stage, source, target, peer):
        pltpu.make_async_remote_copy(
            source,
            target,
            send_sem.at[panel, tile, stage],
            recv_sem.at[panel, tile, stage],
            device_id=peer,
            device_id_type=MESH,
        ).start()

    def wait(panel, tile, stage, sem, counts):
        some = landed_ref.at[panel, tile, pl.ds(0, counts[stage]), :]
        pltpu.make_async_copy(some, some, sem.at[panel, tile, stage]).wait()

    def order_of(tile):
        return [(tile + step) % 6 for step in range(6)]

    def quarter(tile, flips=0):
        first, second = order_of(tile)[3:5]
        high = 1 - bits[first] if flips & 4 else bits[first]
        low = 1 - bits[second] if flips & 2 else bits[second]
        return high * 2 + low

    def flipped(tile, flips):
        return across([link for place, link in enumerate(order_of(tile)[3:]) if flips & (4 >> place)])

    lows = [[0] * TILES, [0] * TILES]

    def begin(panel, tile):
        send(
            panel,
            tile,
            0,
            part_ref.at[panel, tile, rows_at((1 - core) * 256, 256), :],
            landed_ref.at[panel, tile, pl.ds(0, 256), :],
            sibling,
        )

    def advance(panel, tile, stage):
        order = order_of(tile)
        low = lows[panel][tile]
        held = held_ref.at[panel, tile]
        landed = landed_ref.at[panel, tile]
        total = total_ref.at[panel, tile]
        wait(panel, tile, stage, recv_sem, COUNTS)
        if stage == 0:
            held[...] = part_ref[panel, tile, rows_at(core * 256, 256), :] + landed[0:256, :]
        elif stage < 4:
            size = COUNTS[stage]
            held[rows_at(low, size), :] += landed[BASES[stage] : BASES[stage] + size, :]
        elif stage == 4:
            final = held[rows_at(low + quarter(tile) * 8, 8), :]
            for flips in range(1, 8):
                final += landed[BASES[4] + flips * 8 - 8 : BASES[4] + flips * 8, :]
            total[rows_at(core * 256 + low + quarter(tile) * 8, 8), :] = final
        if stage < 3:
            size = COUNTS[stage + 1]
            link = order[stage]
            keep = bits[link]
            send(
                panel,
                tile,
                stage + 1,
                held.at[rows_at(low + (1 - keep) * size, size), :],
                landed.at[pl.ds(BASES[stage + 1], size), :],
                across([link]),
            )
            lows[panel][tile] = low + keep * size
        elif stage == 3:
            for flips in range(1, 8):
                send(
                    panel,
                    tile,
                    4,
                    held.at[rows_at(low + quarter(tile, flips) * 8, 8), :],
                    landed.at[pl.ds(BASES[4] + flips * 8 - 8, 8), :],
                    flipped(tile, flips),
                )
        elif stage == 4:
            place = total.at[rows_at(core * 256 + low + quarter(tile) * 8, 8), :]
            for flips in (2, 4, 6):
                send(panel, tile, 5, place, place, flipped(tile, flips))
        elif stage < 9:
            if stage > 5:
                low = low - bits[order[8 - stage]] * COUNTS[stage]
                lows[panel][tile] = low
            place = total.at[rows_at(core * 256 + low, COUNTS[stage + 1]), :]
            send(panel, tile, stage + 1, place, place, across([order[7 - stage]]) if stage < 8 else sibling)

    wait_blocks(0)
    place_panel(0)
    for tile, stage in arrival_order(2.0, 8):
        if stage is None:
            form_products(0, tile)
            begin(0, 2 * tile)
            begin(0, 2 * tile + 1)
            send_some(8)
            if tile == TILES // 2 - 1:
                scale_panel(0)
        else:
            advance(0, tile, stage)
            send_some(2)
    send_some(128)

    wait_blocks(1)
    place_panel(1)
    written = []
    for tile, stage in arrival_order(3.5, 9):
        if stage is None:
            wait(0, 2 * tile, 9, recv_sem, COUNTS)
            wait(0, 2 * tile + 1, 9, recv_sem, COUNTS)
            written.append(apply_first(tile))
            form_products(1, tile)
            begin(1, 2 * tile)
            begin(1, 2 * tile + 1)
            if tile == TILES // 2 - 1:
                scale_panel(1)
                x_copy = pltpu.make_async_copy(x_ref, x_out_ref, local_sem.at[8])
                x_copy.start()
        else:
            advance(1, tile, stage)
    y_copy = pltpu.make_async_copy(total_ref.at[1], y_out_ref, local_sem.at[9])
    y_copy.start()

    def wait_sent(step, carry):
        strip = strip_at(step, 1)
        id_copy(step, strip, me).wait_send()
        for panel in range(2):
            block_copy(panel, step, strip, me).wait_send()
        return carry

    lax.fori_loop(1, 128, wait_sent, 0)
    for panel in range(2):
        for tile in range(TILES):
            for stage in range(STAGES):
                wait(panel, tile, stage, send_sem, COUNTS)
    for copy in written:
        copy.wait()
    x_copy.wait()
    y_copy.wait()


def main(vectors, panel_store, block_ids, offsets, tri_factors):
    f32 = jnp.float32
    bf16 = jnp.bfloat16
    whole = pl.BlockSpec(memory_space=pltpu.VMEM)
    anywhere = pl.BlockSpec(memory_space=pl.ANY)
    dma = pltpu.SemaphoreType.DMA
    return pl.pallas_call(
        main_kernel,
        out_shape=(
            jax.ShapeDtypeStruct((TILES, 512, 128), f32),
            jax.ShapeDtypeStruct((3, 2, 1024, 256), bf16),
            jax.ShapeDtypeStruct((2, 1024, 1024), f32),
        ),
        in_specs=[pl.BlockSpec(memory_space=pltpu.SMEM), whole, anywhere, whole, anywhere],
        out_specs=[anywhere] * 3,
        scratch_shapes=[
            pltpu.VMEM((2, 1024, 1024), f32),
            pltpu.VMEM((128, 2, 8, 256), f32),
            pltpu.VMEM((128, 2, 8, 256), f32),
            pltpu.VMEM((128, 2, 128), jnp.int32),
            pltpu.VMEM((8, 128), jnp.int32),
            pltpu.SMEM((8, 128), jnp.int32),
            pltpu.VMEM((2, 1024, 256), f32),
            pltpu.VMEM((3, 512, 1024), bf16),
            pltpu.VMEM((3, 2, 1024, 256), bf16),
            pltpu.VMEM((2, TILES, 512, 128), f32),
            pltpu.VMEM((2, TILES, 256, 128), f32),
            pltpu.VMEM((2, TILES, 544, 128), f32),
            pltpu.VMEM((2, TILES, 512, 128), f32),
            dma((2, 128)),
            dma((2, 128)),
            dma((128,)),
            dma((128,)),
            dma((2, TILES, STAGES)),
            dma((2, TILES, STAGES)),
            dma((11,)),
        ],
        compiler_params=pltpu.CompilerParams(
            vmem_limit_bytes=VMEM_LIMIT, collective_id=0, has_side_effects=True
        ),
        name="main",
    )(offsets, block_ids, panel_store, tri_factors, vectors)


def update_kernel(y_ref, x_ref, vectors_ref, out_ref):
    left = [(x_ref[form, 0], x_ref[form, 1]) for form in range(3)]
    summed = jnp.concatenate([y_ref[0], y_ref[1]], axis=1)
    real_part, imag_part = complex_dot(left, right_forms(summed[0:256], summed[256:512]))
    out_ref[0] = vectors_ref[0] - real_part
    out_ref[1] = vectors_ref[1] - imag_part


def update(total, scaled, vectors):
    columns = pl.BlockSpec((2, 1024, 256), lambda step: (0, 0, step))
    return pl.pallas_call(
        update_kernel,
        grid=(4,),
        out_shape=jax.ShapeDtypeStruct(vectors.shape, jnp.float32),
        in_specs=[
            pl.BlockSpec((2, 512, 128), lambda step: (step, 0, 0)),
            pl.BlockSpec((3, 2, 1024, 256), lambda step: (0, 0, 0, 0)),
            columns,
        ],
        out_specs=columns,
        compiler_params=pltpu.CompilerParams(vmem_limit_bytes=VMEM_LIMIT, dimension_semantics=("arbitrary",)),
        name="update",
    )(total, scaled, vectors)


def per_device(vectors, panel_store, block_ids, offsets, tri_factors):
    total, scaled, current = main(vectors, panel_store, block_ids, offsets, tri_factors)
    return update(total, scaled, current)


def solution(mesh):
    placed = (
        P(None, ("row", "col"), None),
        P(None, None, ("row", "col"), None),
        P(None, ("row", "col")),
        P(),
        P(),
    )
    return jax.shard_map(
        per_device,
        mesh=mesh,
        in_specs=placed,
        out_specs=P(None, ("row", "col"), None),
        check_vma=False,
    )
```

time: 561 us -> 177 us (0.32)
  waiting for transfers between devices: 336 us -> 0 us
  Pallas kernels: 0 us -> 177 us
  matrix products: 82.2 us -> 0 us
  other arithmetic: 55.5 us -> 0 us
  local copies, waits for them, and re-layouts: 45.8 us -> 0 us
  starting transfers between devices: 22.2 us -> 0 us
  between operations: 13.9 us -> 0.01 us
    psum x2 -> x0, waiting for transfers between devices: 291 us -> none  [reduce_strips(): return lax.psum(partial_sum, ('row', 'col'))]
    pallas_call x0 -> x2, Pallas kernels: none -> 177 us  [the longest x1 165 us: main(): pl.pallas_call(main_kernel, out_shape=(jax.ShapeDtypeStruct((TILES, 512,...]
    dot_general x24 -> x0, matrix products: 82.2 us -> none  [the longest x16 46.4 us: matmul(): jnp.dot(first_op, second_op, precision=highest, preferred_element_type=jn...]
    all_to_all x2 -> x0, waiting for transfers between devices: 44.9 us -> none  [the longest x1 44.9 us: per_device(): lax.all_to_all(outgoing, ('row', 'col'), split_axis=2, concat_axis=2, til...]
    slice x1 -> x0, other arithmetic: 33.5 us -> none  [mask_panel(): imag_part = jnp.where(below, values[1], jnp.zeros_like(values[1]))]
    all_to_all x2 -> x0, starting transfers between devices: 21.7 us -> none  [the longest x1 11.5 us: per_device(): lax.all_to_all(labels, ('row', 'col'), split_axis=2, concat_axis=2, tiled...]
    gather x1 -> x0, local copies, waits for them, and re-layouts: 14.6 us -> none  [per_device(): placed = jnp.take_along_axis(arrived, ordering[:, None, :, None], axis=2)]
    reshape x2 -> x0, local copies, waits for them, and re-layouts: 12.2 us -> none  [per_device(): panel_store.reshape(panel_count, 2, slot_count, block_rows * col_width)]
  transfers between devices with their start and end apart: 4 -> 0, of which waited for: 3 -> 0; matrix products, arithmetic and copies ran while one was open for 4% -> 0% of each run, Pallas kernels for 0% -> 0%
where the time goes in v3:
time: 177 us
  Pallas kernels  177 us (100%)
    pallas_call x1, Pallas kernels, main(): pl.pallas_call(main_kernel, out_shape=(jax.ShapeDtypeStruct((TILES, 512,...  165 us
    pallas_call x1, Pallas kernels, update(): pl.pallas_call(update_kernel, grid=(4,), out_shape=jax.ShapeDtypeStruct(v...  11.3 us

profile of v3, /device:TPU:1, one launch (start us, length us, event | category | flops | bytes accessed | tf_op | source)
XLA Modules:
  0.0 176.6 jit_solution(16363821378596743445)
XLA Ops:
  0.0 165.3 %main.1 = (f32[8,512,128]{2,1,0:T(8,128)}, bf16[3,2,1024,256]{3,2,1,0:T(8,128)(2,1)}, f32[2,1024,1024]{2,1,0:T(8,128)}) custom-call(s32[2]{0:T(128)} %offsets_ref.1, s32[2,128]{1,0:T(2,128)} %ids_ref.1, f32[2,2,1024,256]{3,2,1,0:T(8,128)} %store_ref.1, f32[2,2,256,256]{3,2,1,0:T(8,128)} %tri_ref.1, f32[2,1024,1024]{2,1,0:T(8,128)} %vectors_ref.1), custom_call_target="tpu_custom_call" | custom-call | tf_op jit(solution)/shard_map/main/pallas_call | solution.py:484
  165.3 11.3 %update.1 = f32[2,1024,1024]{2,1,0:T(8,128)} custom-call(f32[8,512,128]{2,1,0:T(8,128)} %get-tuple-element.8.y_ref, bf16[3,2,1024,256]{3,2,1,0:T(8,128)(2,1)} %get-tuple-element.9.x_ref, f32[2,1024,1024]{2,1,0:T(8,128)} %get-tuple-element.10.vectors_ref), custom_call_target="tpu_custom_call" | custom-call | tf_op jit(solution)/shard_map/update/pallas_call | solution.py:532

commit v4 on v0

v4 whole, which is shorter than its diff:
```python
import jax
import jax.numpy as jnp
from jax import lax
from jax.experimental import pallas as pl
from jax.experimental.pallas import tpu as pltpu
from jax.sharding import PartitionSpec as P


MESH = pl.DeviceIdType.MESH


def strip_of(x, y, z, core):
    return ((x * 2 + z % 2) * 4 + y) * 4 + (z // 2) * 2 + core


VMEM_LIMIT = 60 * 1024 * 1024


def split(value):
    high = value.astype(jnp.bfloat16)
    return high, (value - high.astype(jnp.float32)).astype(jnp.bfloat16)


def dot(first_op, second_op):
    return jnp.dot(first_op, second_op, preferred_element_type=jnp.float32)


def split_dot(first_op, second_op):
    return (
        dot(first_op[0], second_op[0]) + dot(first_op[0], second_op[1]) + dot(first_op[1], second_op[0])
    )


def left_forms(real_part, imag_part):
    return split(real_part + imag_part), split(real_part), split(imag_part)


def right_forms(real_part, imag_part):
    return split(real_part), split(imag_part - real_part), split(real_part + imag_part)


def complex_dot(left, right):
    shared = split_dot(left[0], right[0])
    real_part = shared - split_dot(left[2], right[2])
    imag_part = shared + split_dot(left[1], right[1])
    return real_part, imag_part


def adjoint_upper(tri_ref, panel):
    shape = tri_ref.shape[2:]
    upper = lax.broadcasted_iota(jnp.int32, shape, 0) <= lax.broadcasted_iota(jnp.int32, shape, 1)
    return jnp.where(upper, tri_ref[panel, 0], 0.0).T, -jnp.where(upper, tri_ref[panel, 1], 0.0).T


GROUPS = (
    ((0, 32), (32, 32), (64, 32), (96, 32)),
    ((0, 32), (32, 32), (64, 32), (96, 16), (112, 16)),
)


def product_kernel(
    offsets_ref,
    ids_ref,
    store_ref,
    tri_ref,
    vectors_ref,
    y_out_ref,
    x_out_ref,
    slot_out_ref,
    z_ref,
    first_blocks_ref,
    second_blocks_ref,
    all_ids_ref,
    order_ref,
    slot_ref,
    first_panel_ref,
    second_panel_ref,
    rows_ref,
    match_ref,
    left_ref,
    factor_ref,
    y_ref,
    x_ref,
    block_send_sem,
    block_recv_sem,
    id_send_sem,
    id_recv_sem,
    local_sem,
):
    blocks_refs = (first_blocks_ref, second_blocks_ref)
    panel_refs = (first_panel_ref, second_panel_ref)
    row = lax.axis_index("row")
    col = lax.axis_index("col")
    me = row * 4 + col
    x = row // 8
    y = row % 4
    z = (col // 2) * 2 + (row // 4) % 2
    core = col % 2

    barrier = pltpu.get_barrier_semaphore()

    def greet(step, carry):
        peer = (me + step) % 128
        pl.semaphore_signal(barrier, inc=1, device_id=(peer // 4, peer % 4), device_id_type=MESH)
        return carry

    lax.fori_loop(1, 128, greet, 0)

    def listed(strip):
        return pl.ds(pl.multiple_of(strip * 8, 8), 8)

    own_copies = [
        pltpu.make_async_copy(store_ref.at[panel, :, listed(me), :], blocks_refs[panel].at[0], local_sem.at[panel])
        for panel in range(2)
    ]
    own_copies.append(pltpu.make_async_copy(ids_ref, all_ids_ref.at[0], local_sem.at[2]))
    for copy in own_copies:
        copy.start()
    fetch_vectors = pltpu.make_async_copy(vectors_ref, z_ref, local_sem.at[3])
    fetch_vectors.start()
    pl.semaphore_wait(barrier, 127)

    def strip_at(step, sign):
        spread = (step // 2 * 27) % 64
        return strip_of(
            (x + sign * (spread % 4) + 4) % 4,
            (y + sign * ((spread // 4) % 4) + 4) % 4,
            (z + sign * (spread // 16) + 4) % 4,
            (core + step) % 2,
        )

    def block_copy(panel, step):
        strip = strip_at(step, 1)
        return pltpu.make_async_remote_copy(
            store_ref.at[panel, :, listed(strip), :],
            blocks_refs[panel].at[step],
            block_send_sem.at[panel, step],
            block_recv_sem.at[panel, step],
            device_id=(strip // 4, strip % 4),
            device_id_type=MESH,
        )

    def id_copy(step):
        strip = strip_at(step, 1)
        return pltpu.make_async_remote_copy(
            ids_ref,
            all_ids_ref.at[step],
            id_send_sem.at[step],
            id_recv_sem.at[step],
            device_id=(strip // 4, strip % 4),
            device_id_type=MESH,
        )

    def send_ids(step, carry):
        id_copy(step).start()
        return carry

    def send_blocks(panel, first, last):
        def body(step, carry):
            block_copy(panel, step).start()
            return carry

        lax.fori_loop(first, last, body, 0)

    send_blocks(0, 1, 24)
    lax.fori_loop(1, 128, send_ids, 0)
    send_blocks(0, 24, 128)
    send_blocks(1, 1, 128)

    for panel in range(2):
        forms = right_forms(*adjoint_upper(tri_ref, panel))
        for form in range(3):
            for piece in range(2):
                factor_ref[panel, form, piece] = forms[form][piece]

    for copy in own_copies:
        copy.wait()

    def wait_ids(step, carry):
        id_copy(step).wait_recv()
        return carry

    lax.fori_loop(1, 128, wait_ids, 0)
    down = lax.broadcasted_iota(jnp.int32, (128, 128), 0)
    lane = lax.broadcasted_iota(jnp.int32, (128, 128), 1)
    order_ref[...] = jnp.zeros_like(order_ref)
    places = []
    for panel in range(2):
        own = jnp.sum(jnp.where(lane == me, all_ids_ref[:, panel, :], 0), axis=1, keepdims=True) % 128
        places.append(jnp.sum(jnp.where(down == lane, own, 0), axis=0, keepdims=True))
        order_ref[panel : panel + 1, :] = places[panel]
    slot_of_place = jnp.max(jnp.where(places[0] == down, lane, 0), axis=1, keepdims=True)
    order_ref[2:3, :] = jnp.max(jnp.where(places[1] == down, slot_of_place, 0), axis=0, keepdims=True)
    fetch_order = pltpu.make_async_copy(order_ref, slot_ref, local_sem.at[4])
    fetch_order.start()
    fetch_order.wait()
    write_order = pltpu.make_async_copy(order_ref, slot_out_ref, local_sem.at[5])
    write_order.start()
    fetch_vectors.wait()

    def take_group(panel, first, count):
        size = count * 8
        start = first * 8
        begin = first == 0
        values = panel_refs[panel]

        def wait_block(step, carry):
            block_copy(panel, step).wait_recv()
            return carry

        lax.fori_loop(max(first, 1), first + count, wait_block, 0)

        def take_block(step, carry):
            slot = first + step
            place = slot_ref[panel, slot]
            near = pl.ds(pl.multiple_of(step * 8, 8), 8)
            row_index = me * 1024 + place * 8 + lax.broadcasted_iota(jnp.int32, (8, 256), 0)
            limit = offsets_ref[panel] + lax.broadcasted_iota(jnp.int32, (8, 256), 1)
            below = row_index > limit
            diagonal = jnp.where(row_index == limit, 1.0, 0.0)
            values[0, slot] = jnp.where(below, blocks_refs[panel][slot, 0], diagonal)
            values[1, slot] = jnp.where(below, blocks_refs[panel][slot, 1], 0.0)
            rows_ref[0, near, :] = z_ref[0, place]
            rows_ref[1, near, :] = z_ref[1, place]
            if panel == 1:
                matching = slot_ref[2, slot]
                match_ref[0, near, :] = first_panel_ref[0, matching]
                match_ref[1, near, :] = first_panel_ref[1, matching]
            return carry

        lax.fori_loop(0, count, take_block, 0, unroll=4)

        own = [values[part, first : first + count].reshape(size, 256) for part in range(2)]
        forms = left_forms(own[0].T, -own[1].T)
        for form in range(3):
            for piece in range(2):
                left_ref[form, piece * 256 : (piece + 1) * 256, 0:size] = forms[form][piece]

        def adjoint_products(right):
            sums = []
            for form in range(3):
                high, low = right[form]
                both = dot(left_ref[form, :, 0:size], high)
                sums.append(both[0:256] + both[256:512] + dot(left_ref[form, 0:256, 0:size], low))
            return sums[0] - sums[2], sums[0] + sums[1]

        def add_tiles(tile, parts):
            for part in range(2):
                for side in range(2):
                    value = parts[part][:, side * 128 : (side + 1) * 128]
                    target = y_ref.at[tile + side, part * 256 : (part + 1) * 256, :]
                    if begin:
                        target[...] = value
                    else:
                        target[...] += value

        def take_columns(chunk, carry):
            columns = pl.ds(pl.multiple_of(chunk * 256, 256), 256)
            right = right_forms(rows_ref[0, 0:size, columns], rows_ref[1, 0:size, columns])
            add_tiles(panel * 8 + 2 * chunk, adjoint_products(right))
            return carry

        lax.fori_loop(0, 4, take_columns, 0)

        if panel == 1:
            matched = (match_ref[0, 0:size, :], match_ref[1, 0:size, :])
            add_tiles(16, adjoint_products(right_forms(*matched)))
            for which, source in enumerate((matched, own)):
                factor = [(factor_ref[which, form, 0], factor_ref[which, form, 1]) for form in range(3)]
                scaled = complex_dot(left_forms(*source), factor)
                for part in range(2):
                    x_ref[part, start : start + size, which * 256 : (which + 1) * 256] = scaled[part]

    for panel in range(2):
        for first, count in GROUPS[panel]:
            take_group(panel, first, count)

    y_copy = pltpu.make_async_copy(y_ref, y_out_ref, local_sem.at[6])
    x_copy = pltpu.make_async_copy(x_ref, x_out_ref, local_sem.at[7])
    y_copy.start()
    x_copy.start()

    def wait_sent(step, carry):
        id_copy(step).wait_send()
        block_copy(0, step).wait_send()
        block_copy(1, step).wait_send()
        return carry

    lax.fori_loop(1, 128, wait_sent, 0)
    write_order.wait()
    y_copy.wait()
    x_copy.wait()


def products(vectors, panel_store, block_ids, offsets, tri_factors):
    f32 = jnp.float32
    bf16 = jnp.bfloat16
    whole = pl.BlockSpec(memory_space=pltpu.VMEM)
    anywhere = pl.BlockSpec(memory_space=pl.ANY)
    dma = pltpu.SemaphoreType.DMA
    return pl.pallas_call(
        product_kernel,
        out_shape=(
            jax.ShapeDtypeStruct((TILES, 512, 128), f32),
            jax.ShapeDtypeStruct((2, 1024, 512), f32),
            jax.ShapeDtypeStruct((8, 128), jnp.int32),
        ),
        in_specs=[pl.BlockSpec(memory_space=pltpu.SMEM), whole, anywhere, whole, anywhere],
        out_specs=[anywhere] * 3,
        scratch_shapes=[
            pltpu.VMEM((2, 128, 8, 1024), f32),
            pltpu.VMEM((128, 2, 8, 256), f32),
            pltpu.VMEM((128, 2, 8, 256), f32),
            pltpu.VMEM((128, 2, 128), jnp.int32),
            pltpu.VMEM((8, 128), jnp.int32),
            pltpu.SMEM((8, 128), jnp.int32),
            pltpu.VMEM((2, 128, 8, 256), f32),
            pltpu.VMEM((2, 128, 8, 256), f32),
            pltpu.VMEM((2, 256, 1024), f32),
            pltpu.VMEM((2, 256, 256), f32),
            pltpu.VMEM((3, 512, 256), bf16),
            pltpu.VMEM((2, 3, 2, 256, 256), bf16),
            pltpu.VMEM((TILES, 512, 128), f32),
            pltpu.VMEM((2, 1024, 512), f32),
            dma((2, 128)),
            dma((2, 128)),
            dma((128,)),
            dma((128,)),
            dma((8,)),
        ],
        compiler_params=pltpu.CompilerParams(
            vmem_limit_bytes=VMEM_LIMIT, collective_id=0, has_side_effects=True
        ),
        name="products",
    )(offsets, block_ids, panel_store, tri_factors, vectors.reshape(2, 128, 8, 1024))


TILES = 18
STAGES = 10
COUNTS = [256, 128, 64, 32, 56, 24, 32, 64, 128, 256]
BASES = [0, 256, 384, 448, 480]


def arrival_order():
    free = [0.0] * 7
    ready = []
    for tile in range(TILES):
        free[6] += 0.3
        ready.append((free[6] + 1.6, tile, 0))
    order = []
    now = 0.0
    while ready:
        ready.sort()
        arrived, tile, stage = ready.pop(0)
        order.append((tile, stage))
        now = max(now, arrived) + 0.15
        following = stage + 1
        if following == STAGES:
            continue
        if following in (4, 5):
            finish = now + 0.3
        else:
            if following == 9:
                link, cost = 6, 0.3
            elif following < 4:
                link, cost = (tile + following - 1) % 6, 2.0 / 2 ** (following - 1)
            else:
                link, cost = (tile + 8 - following) % 6, 2.0 / 2 ** (8 - following)
            free[link] = max(free[link], now) + cost
            finish = free[link]
        ready.append((finish + 1.6, tile, following))
    return order


def sum_kernel(part_ref, total_ref, held_ref, landed_ref, send_sem, recv_sem):
    row = lax.axis_index("row")
    col = lax.axis_index("col")
    here = (row // 8, row % 4, (col // 2) * 2 + (row // 4) % 2)
    core = col % 2

    def device(place, core):
        strip = strip_of(*place, core)
        return (strip // 4, strip % 4)

    sibling = device(here, 1 - core)
    other = [place + 1 - 2 * (place % 2) for place in here] + [3 - place for place in here]
    bits = [((place + 1) // 2) % 2 for place in here] + [place // 2 for place in here]

    def across(links):
        place = list(here)
        for link in links:
            place[link % 3] = other[link]
        return device(place, core)

    barrier = pltpu.get_barrier_semaphore()
    peers = [sibling]
    for first in (None, 0, 3):
        for second in (None, 1, 4):
            for third in (None, 2, 5):
                chosen = [link for link in (first, second, third) if link is not None]
                if chosen:
                    peers.append(across(chosen))
    for peer in peers:
        pl.semaphore_signal(barrier, inc=1, device_id=peer, device_id_type=MESH)
    pl.semaphore_wait(barrier, len(peers))

    def rows_at(first, count):
        return pl.ds(pl.multiple_of(first, 8), count)

    def send(tile, stage, source, target, peer):
        pltpu.make_async_remote_copy(
            source,
            target,
            send_sem.at[tile, stage],
            recv_sem.at[tile, stage],
            device_id=peer,
            device_id_type=MESH,
        ).start()

    def wait(tile, stage, sem, counts):
        some = landed_ref.at[tile, pl.ds(0, counts[stage]), :]
        pltpu.make_async_copy(some, some, sem.at[tile, stage]).wait()

    def order_of(tile):
        return [(tile + step) % 6 for step in range(6)]

    def quarter(tile, flips=0):
        first, second = order_of(tile)[3:5]
        high = 1 - bits[first] if flips & 4 else bits[first]
        low = 1 - bits[second] if flips & 2 else bits[second]
        return high * 2 + low

    def flipped(tile, flips):
        return across([link for place, link in enumerate(order_of(tile)[3:]) if flips & (4 >> place)])

    lows = [0] * TILES

    def begin(tile):
        send(
            tile,
            0,
            part_ref.at[tile, rows_at((1 - core) * 256, 256), :],
            landed_ref.at[tile, pl.ds(0, 256), :],
            sibling,
        )

    def advance(tile, stage):
        order = order_of(tile)
        low = lows[tile]
        held = held_ref.at[tile]
        landed = landed_ref.at[tile]
        total = total_ref.at[tile]
        wait(tile, stage, recv_sem, COUNTS)
        if stage == 0:
            held[...] = part_ref[tile, rows_at(core * 256, 256), :] + landed[0:256, :]
        elif stage < 4:
            size = COUNTS[stage]
            held[rows_at(low, size), :] += landed[BASES[stage] : BASES[stage] + size, :]
        elif stage == 4:
            final = held[rows_at(low + quarter(tile) * 8, 8), :]
            for flips in range(1, 8):
                final += landed[BASES[4] + flips * 8 - 8 : BASES[4] + flips * 8, :]
            total[rows_at(core * 256 + low + quarter(tile) * 8, 8), :] = final
        if stage < 3:
            size = COUNTS[stage + 1]
            link = order[stage]
            keep = bits[link]
            send(
                tile,
                stage + 1,
                held.at[rows_at(low + (1 - keep) * size, size), :],
                landed.at[pl.ds(BASES[stage + 1], size), :],
                across([link]),
            )
            lows[tile] = low + keep * size
        elif stage == 3:
            for flips in range(1, 8):
                send(
                    tile,
                    4,
                    held.at[rows_at(low + quarter(tile, flips) * 8, 8), :],
                    landed.at[pl.ds(BASES[4] + flips * 8 - 8, 8), :],
                    flipped(tile, flips),
                )
        elif stage == 4:
            place = total.at[rows_at(core * 256 + low + quarter(tile) * 8, 8), :]
            for flips in (2, 4, 6):
                send(tile, 5, place, place, flipped(tile, flips))
        elif stage < 9:
            if stage > 5:
                low = low - bits[order[8 - stage]] * COUNTS[stage]
                lows[tile] = low
            place = total.at[rows_at(core * 256 + low, COUNTS[stage + 1]), :]
            send(tile, stage + 1, place, place, across([order[7 - stage]]) if stage < 8 else sibling)

    for tile in range(TILES):
        begin(tile)
    for tile, stage in arrival_order():
        advance(tile, stage)
    for tile in range(TILES):
        for stage in range(STAGES):
            wait(tile, stage, send_sem, COUNTS)


def sum_products(partial):
    f32 = jnp.float32
    whole = pl.BlockSpec(memory_space=pltpu.VMEM)
    dma = pltpu.SemaphoreType.DMA
    return pl.pallas_call(
        sum_kernel,
        out_shape=jax.ShapeDtypeStruct((TILES, 512, 128), f32),
        in_specs=[whole],
        out_specs=whole,
        scratch_shapes=[
            pltpu.VMEM((TILES, 256, 128), f32),
            pltpu.VMEM((TILES, 544, 128), f32),
            dma((TILES, STAGES)),
            dma((TILES, STAGES)),
        ],
        compiler_params=pltpu.CompilerParams(
            vmem_limit_bytes=VMEM_LIMIT, collective_id=1, has_side_effects=True
        ),
        name="sum_products",
    )(partial)


def update_kernel(slot_ref, g_ref, first_ref, second_ref, x_ref, tri_ref, vectors_ref, out_ref, left_ref, change_ref):
    def parts(tiles_ref):
        joined = jnp.concatenate([tiles_ref[0], tiles_ref[1]], axis=1)
        return joined[0:256], joined[256:512]

    @pl.when(pl.program_id(0) == 0)
    def _():
        cross = complex_dot(left_forms(*parts(g_ref)), right_forms(*adjoint_upper(tri_ref, 0)))
        cross = right_forms(*cross)

        def correct_rows(step, carry):
            rows = pl.ds(pl.multiple_of(step * 256, 256), 256)
            second = left_forms(x_ref[0, rows, 256:512], x_ref[1, rows, 256:512])
            real_part, imag_part = complex_dot(second, cross)
            first = left_forms(x_ref[0, rows, 0:256] - real_part, x_ref[1, rows, 0:256] - imag_part)
            for form in range(3):
                for piece in range(2):
                    left_ref[form, piece, rows, 0:256] = first[form][piece]
                    left_ref[form, piece, rows, 256:512] = second[form][piece]
            return carry

        lax.fori_loop(0, 4, correct_rows, 0)

    left = [(left_ref[form, 0], left_ref[form, 1]) for form in range(3)]
    first = parts(first_ref)
    second = parts(second_ref)
    summed = [jnp.concatenate([first[part], second[part]], axis=0) for part in range(2)]
    change_ref[0], change_ref[1] = complex_dot(left, right_forms(*summed))

    def put_block(slot, carry):
        rows = pl.ds(pl.multiple_of(slot_ref[1, slot] * 8, 8), 8)
        near = pl.ds(pl.multiple_of(slot * 8, 8), 8)
        for part in range(2):
            out_ref[part, rows, :] = vectors_ref[part, rows, :] - change_ref[part, near, :]
        return carry

    lax.fori_loop(0, 128, put_block, 0, unroll=8)


def update(slots, total, scaled, tri_factors, vectors):
    whole = pl.BlockSpec(memory_space=pltpu.VMEM)
    columns = pl.BlockSpec((2, 1024, 256), lambda step: (0, 0, step))
    return pl.pallas_call(
        update_kernel,
        grid=(4,),
        out_shape=jax.ShapeDtypeStruct(vectors.shape, jnp.float32),
        in_specs=[
            pl.BlockSpec(memory_space=pltpu.SMEM),
            pl.BlockSpec((2, 512, 128), lambda step: (8, 0, 0)),
            pl.BlockSpec((2, 512, 128), lambda step: (step, 0, 0)),
            pl.BlockSpec((2, 512, 128), lambda step: (step + 4, 0, 0)),
            whole,
            whole,
            columns,
        ],
        out_specs=columns,
        scratch_shapes=[pltpu.VMEM((3, 2, 1024, 512), jnp.bfloat16), pltpu.VMEM((2, 1024, 256), jnp.float32)],
        compiler_params=pltpu.CompilerParams(vmem_limit_bytes=VMEM_LIMIT, dimension_semantics=("arbitrary",)),
        name="update",
    )(slots, total, total, total, scaled, tri_factors, vectors)


def per_device(vectors, panel_store, block_ids, offsets, tri_factors):
    partial, scaled, slots = products(vectors, panel_store, block_ids, offsets, tri_factors)
    total = sum_products(partial)
    return update(slots, total, scaled, tri_factors, vectors)


def solution(mesh):
    placed = (
        P(None, ("row", "col"), None),
        P(None, None, ("row", "col"), None),
        P(None, ("row", "col")),
        P(),
        P(),
    )
    return jax.shard_map(
        per_device,
        mesh=mesh,
        in_specs=placed,
        out_specs=P(None, ("row", "col"), None),
        check_vma=False,
    )
```

time: 561 us -> 162 us (0.29)
  waiting for transfers between devices: 336 us -> 0 us
  Pallas kernels: 0 us -> 162 us
  matrix products: 82.2 us -> 0 us
  other arithmetic: 55.5 us -> 0 us
  local copies, waits for them, and re-layouts: 45.8 us -> 0 us
  starting transfers between devices: 22.2 us -> 0 us
  between operations: 13.9 us -> 0.02 us
    psum x2 -> x0, waiting for transfers between devices: 291 us -> none  [reduce_strips(): return lax.psum(partial_sum, ('row', 'col'))]
    pallas_call x0 -> x3, Pallas kernels: none -> 162 us  [the longest x1 83.2 us: products(): pl.pallas_call(product_kernel, out_shape=(jax.ShapeDtypeStruct((TILES, 51...]
    dot_general x24 -> x0, matrix products: 82.2 us -> none  [the longest x16 46.4 us: matmul(): jnp.dot(first_op, second_op, precision=highest, preferred_element_type=jn...]
    all_to_all x2 -> x0, waiting for transfers between devices: 44.9 us -> none  [the longest x1 44.9 us: per_device(): lax.all_to_all(outgoing, ('row', 'col'), split_axis=2, concat_axis=2, til...]
    slice x1 -> x0, other arithmetic: 33.5 us -> none  [mask_panel(): imag_part = jnp.where(below, values[1], jnp.zeros_like(values[1]))]
    all_to_all x2 -> x0, starting transfers between devices: 21.7 us -> none  [the longest x1 11.5 us: per_device(): lax.all_to_all(labels, ('row', 'col'), split_axis=2, concat_axis=2, tiled...]
    gather x1 -> x0, local copies, waits for them, and re-layouts: 14.6 us -> none  [per_device(): placed = jnp.take_along_axis(arrived, ordering[:, None, :, None], axis=2)]
    reshape x2 -> x0, local copies, waits for them, and re-layouts: 12.2 us -> none  [per_device(): panel_store.reshape(panel_count, 2, slot_count, block_rows * col_width)]
  transfers between devices with their start and end apart: 4 -> 0, of which waited for: 3 -> 0; matrix products, arithmetic and copies ran while one was open for 4% -> 0% of each run, Pallas kernels for 0% -> 0%
where the time goes in v4:
time: 162 us
  Pallas kernels  162 us (100%)
    pallas_call x1, Pallas kernels, products(): pl.pallas_call(product_kernel, out_shape=(jax.ShapeDtypeStruct((TILES, 51...  83.2 us
    pallas_call x1, Pallas kernels, sum_products(): pl.pallas_call(sum_kernel, out_shape=jax.ShapeDtypeStruct((TILES, 512, 12...  57.3 us
    pallas_call x1, Pallas kernels, update(): pl.pallas_call(update_kernel, grid=(4,), out_shape=jax.ShapeDtypeStruct(v...  21.5 us

profile of v4, /device:TPU:1, one launch (start us, length us, event | category | flops | bytes accessed | tf_op | source)
XLA Modules:
  0.0 162.0 jit_solution(13278509294192565865)
XLA Ops:
  0.0 83.2 %products.1 = (f32[18,512,128]{2,1,0:T(8,128)}, f32[2,1024,512]{2,1,0:T(8,128)}, s32[8,128]{1,0:T(8,128)}) custom-call(s32[2]{0:T(128)} %offsets_ref.1, s32[2,128]{1,0:T(2,128)} %ids_ref.1, f32[2,2,1024,256]{3,2,1,0:T(8,128)} %store_ref.1, f32[2,2,256,256]{3,2,1,0:T(8,128)} %tri_ref.3, f32[2,128,8,1024]{3,2,1,0:T(8,128)} %bitcast.1), custom_call_target="tpu_custom_call" | custom-call | tf_op jit(solution)/shard_map/products/pallas_call | solution.py:301
  83.2 57.3 %sum_products.1.g_ref.first_ref.second_ref = f32[18,512,128]{2,1,0:T(8,128)} custom-call(f32[18,512,128]{2,1,0:T(8,128)} %get-tuple-element.9.part_ref), custom_call_target="tpu_custom_call" | custom-call | tf_op jit(solution)/shard_map/sum_products/pallas_call | solution.py:509
  140.5 21.5 %update.1 = f32[2,1024,1024]{2,1,0:T(8,128)} custom-call(s32[8,128]{1,0:T(8,128)} %get-tuple-element.8.slot_ref, f32[18,512,128]{2,1,0:T(8,128)} %sum_products.1.g_ref.first_ref.second_ref, f32[18,512,128]{2,1,0:T(8,128)} %sum_products.1.g_ref.first_ref.second_ref, f32[18,512,128]{2,1,0:T(8,128)} %sum_products.1.g_ref.first_ref.second_ref, ...), custom_call_target="tpu_custom_call" | custom-call | tf_op jit(solution)/shard_map/update/pallas_call | solution.py:569

commit v5 on v4

--- a/solution.py
+++ b/solution.py
@@ -25,25 +25,27 @@
     return jnp.dot(first_op, second_op, preferred_element_type=jnp.float32)
 
 
-def split_dot(first_op, second_op):
-    return (
-        dot(first_op[0], second_op[0]) + dot(first_op[0], second_op[1]) + dot(first_op[1], second_op[0])
-    )
+def left_pieces(value):
+    high, low = split(value)
+    return jnp.concatenate([high, high, low], axis=1)
+
+
+def right_pieces(value):
+    high, low = split(value)
+    return jnp.concatenate([high, low, high], axis=0)
 
 
 def left_forms(real_part, imag_part):
-    return split(real_part + imag_part), split(real_part), split(imag_part)
+    return left_pieces(real_part + imag_part), left_pieces(real_part), left_pieces(imag_part)
 
 
 def right_forms(real_part, imag_part):
-    return split(real_part), split(imag_part - real_part), split(real_part + imag_part)
+    return right_pieces(real_part), right_pieces(imag_part - real_part), right_pieces(real_part + imag_part)
 
 
 def complex_dot(left, right):
-    shared = split_dot(left[0], right[0])
-    real_part = shared - split_dot(left[2], right[2])
-    imag_part = shared + split_dot(left[1], right[1])
-    return real_part, imag_part
+    shared = dot(left[0], right[0])
+    return shared - dot(left[2], right[2]), shared + dot(left[1], right[1])
 
 
 def adjoint_upper(tri_ref, panel):
@@ -53,8 +55,8 @@
 
 
 GROUPS = (
-    ((0, 32), (32, 32), (64, 32), (96, 32)),
-    ((0, 32), (32, 32), (64, 32), (96, 16), (112, 16)),
+    ((0, 64), (64, 64)),
+    ((0, 64), (64, 32), (96, 16), (112, 16)),
 )
 
 
@@ -170,8 +172,7 @@
     for panel in range(2):
         forms = right_forms(*adjoint_upper(tri_ref, panel))
         for form in range(3):
-            for piece in range(2):
-                factor_ref[panel, form, piece] = forms[form][piece]
+            factor_ref[panel, form] = forms[form]
 
     for copy in own_copies:
         copy.wait()
@@ -233,16 +234,10 @@
         own = [values[part, first : first + count].reshape(size, 256) for part in range(2)]
         forms = left_forms(own[0].T, -own[1].T)
         for form in range(3):
-            for piece in range(2):
-                left_ref[form, piece * 256 : (piece + 1) * 256, 0:size] = forms[form][piece]
+            left_ref[form, :, 0 : 3 * size] = forms[form]
 
         def adjoint_products(right):
-            sums = []
-            for form in range(3):
-                high, low = right[form]
-                both = dot(left_ref[form, :, 0:size], high)
-                sums.append(both[0:256] + both[256:512] + dot(left_ref[form, 0:256, 0:size], low))
-            return sums[0] - sums[2], sums[0] + sums[1]
+            return complex_dot([left_ref[form, :, 0 : 3 * size] for form in range(3)], right)
 
         def add_tiles(tile, parts):
             for part in range(2):
@@ -257,7 +252,7 @@
         def take_columns(chunk, carry):
             columns = pl.ds(pl.multiple_of(chunk * 256, 256), 256)
             right = right_forms(rows_ref[0, 0:size, columns], rows_ref[1, 0:size, columns])
-            add_tiles(panel * 8 + 2 * chunk, adjoint_products(right))
+            add_tiles(4 * chunk + 2 * panel, adjoint_products(right))
             return carry
 
         lax.fori_loop(0, 4, take_columns, 0)
@@ -266,8 +261,7 @@
             matched = (match_ref[0, 0:size, :], match_ref[1, 0:size, :])
             add_tiles(16, adjoint_products(right_forms(*matched)))
             for which, source in enumerate((matched, own)):
-                factor = [(factor_ref[which, form, 0], factor_ref[which, form, 1]) for form in range(3)]
-                scaled = complex_dot(left_forms(*source), factor)
+                scaled = complex_dot(left_forms(*source), [factor_ref[which, form] for form in range(3)])
                 for part in range(2):
                     x_ref[part, start : start + size, which * 256 : (which + 1) * 256] = scaled[part]
 
@@ -316,10 +310,10 @@
             pltpu.SMEM((8, 128), jnp.int32),
             pltpu.VMEM((2, 128, 8, 256), f32),
             pltpu.VMEM((2, 128, 8, 256), f32),
-            pltpu.VMEM((2, 256, 1024), f32),
-            pltpu.VMEM((2, 256, 256), f32),
-            pltpu.VMEM((3, 512, 256), bf16),
-            pltpu.VMEM((2, 3, 2, 256, 256), bf16),
+            pltpu.VMEM((2, 512, 1024), f32),
+            pltpu.VMEM((2, 512, 256), f32),
+            pltpu.VMEM((3, 256, 1536), bf16),
+            pltpu.VMEM((2, 3, 768, 256), bf16),
             pltpu.VMEM((TILES, 512, 128), f32),
             pltpu.VMEM((2, 1024, 512), f32),
             dma((2, 128)),
@@ -341,34 +335,46 @@
 BASES = [0, 256, 384, 448, 480]
 
 
-def arrival_order():
+FIRST_TILES = 9
+
+
+def step_order():
+    sent = 0.0
     free = [0.0] * 7
+    now = 0.0
     ready = []
-    for tile in range(TILES):
-        free[6] += 0.3
-        ready.append((free[6] + 1.6, tile, 0))
     order = []
-    now = 0.0
+    waiting = list(range(TILES - 2, TILES)) + list(range(TILES - 2))
+
+    def send(tile, stage):
+        nonlocal sent, now
+        size = COUNTS[stage] * 0.512
+        now += 0.05 * {4: 7, 5: 3}.get(stage, 1)
+        sent = max(sent, now) + size / 230
+        arrival = sent
+        if stage not in (4, 5):
+            link = 6 if stage in (0, 9) else (tile + (stage - 1 if stage < 4 else 8 - stage)) % 6
+            free[link] = max(free[link], sent - size / 230) + size / (600 if link == 6 else 50)
+            arrival = max(arrival, free[link])
+        ready.append((arrival + 1.5, tile, stage))
+
+    def start():
+        if waiting:
+            tile = waiting.pop(0)
+            order.append((tile, 0))
+            send(tile, 0)
+
+    for _ in range(FIRST_TILES):
+        start()
     while ready:
         ready.sort()
-        arrived, tile, stage = ready.pop(0)
-        order.append((tile, stage))
-        now = max(now, arrived) + 0.15
-        following = stage + 1
-        if following == STAGES:
-            continue
-        if following in (4, 5):
-            finish = now + 0.3
-        else:
-            if following == 9:
-                link, cost = 6, 0.3
-            elif following < 4:
-                link, cost = (tile + following - 1) % 6, 2.0 / 2 ** (following - 1)
-            else:
-                link, cost = (tile + 8 - following) % 6, 2.0 / 2 ** (8 - following)
-            free[link] = max(free[link], now) + cost
-            finish = free[link]
-        ready.append((finish + 1.6, tile, following))
+        arrival, tile, stage = ready.pop(0)
+        order.append((tile, stage + 1))
+        now = max(now, arrival) + 0.12
+        if stage < STAGES - 1:
+            send(tile, stage + 1)
+        if stage == 2:
+            start()
     return order
 
 
@@ -493,10 +499,11 @@
             place = total.at[rows_at(core * 256 + low, COUNTS[stage + 1]), :]
             send(tile, stage + 1, place, place, across([order[7 - stage]]) if stage < 8 else sibling)
 
-    for tile in range(TILES):
-        begin(tile)
-    for tile, stage in arrival_order():
-        advance(tile, stage)
+    for tile, step in step_order():
+        if step == 0:
+            begin(tile)
+        else:
+            advance(tile, step - 1)
     for tile in range(TILES):
         for stage in range(STAGES):
             wait(tile, stage, send_sem, COUNTS)
@@ -524,14 +531,14 @@
     )(partial)
 
 
-def update_kernel(slot_ref, g_ref, first_ref, second_ref, x_ref, tri_ref, vectors_ref, out_ref, left_ref, change_ref):
-    def parts(tiles_ref):
-        joined = jnp.concatenate([tiles_ref[0], tiles_ref[1]], axis=1)
+def update_kernel(slot_ref, g_ref, y_ref, x_ref, tri_ref, vectors_ref, out_ref, left_ref, change_ref):
+    def parts(tiles_ref, first):
+        joined = jnp.concatenate([tiles_ref[first], tiles_ref[first + 1]], axis=1)
         return joined[0:256], joined[256:512]
 
     @pl.when(pl.program_id(0) == 0)
     def _():
-        cross = complex_dot(left_forms(*parts(g_ref)), right_forms(*adjoint_upper(tri_ref, 0)))
+        cross = complex_dot(left_forms(*parts(g_ref, 0)), right_forms(*adjoint_upper(tri_ref, 0)))
         cross = right_forms(*cross)
 
         def correct_rows(step, carry):
@@ -540,16 +547,17 @@
             real_part, imag_part = complex_dot(second, cross)
             first = left_forms(x_ref[0, rows, 0:256] - real_part, x_ref[1, rows, 0:256] - imag_part)
             for form in range(3):
-                for piece in range(2):
-                    left_ref[form, piece, rows, 0:256] = first[form][piece]
-                    left_ref[form, piece, rows, 256:512] = second[form][piece]
+                for piece in range(3):
+                    start = piece * 512
+                    left_ref[form, rows, start : start + 256] = first[form][:, piece * 256 : (piece + 1) * 256]
+                    left_ref[form, rows, start + 256 : start + 512] = second[form][:, piece * 256 : (piece + 1) * 256]
             return carry
 
         lax.fori_loop(0, 4, correct_rows, 0)
 
-    left = [(left_ref[form, 0], left_ref[form, 1]) for form in range(3)]
-    first = parts(first_ref)
-    second = parts(second_ref)
+    left = [left_ref[form] for form in range(3)]
+    first = parts(y_ref, 0)
+    second = parts(y_ref, 2)
     summed = [jnp.concatenate([first[part], second[part]], axis=0) for part in range(2)]
     change_ref[0], change_ref[1] = complex_dot(left, right_forms(*summed))
 
@@ -573,17 +581,16 @@
         in_specs=[
             pl.BlockSpec(memory_space=pltpu.SMEM),
             pl.BlockSpec((2, 512, 128), lambda step: (8, 0, 0)),
-            pl.BlockSpec((2, 512, 128), lambda step: (step, 0, 0)),
-            pl.BlockSpec((2, 512, 128), lambda step: (step + 4, 0, 0)),
+            pl.BlockSpec((4, 512, 128), lambda step: (step, 0, 0)),
             whole,
             whole,
             columns,
         ],
         out_specs=columns,
-        scratch_shapes=[pltpu.VMEM((3, 2, 1024, 512), jnp.bfloat16), pltpu.VMEM((2, 1024, 256), jnp.float32)],
+        scratch_shapes=[pltpu.VMEM((3, 1024, 1536), jnp.bfloat16), pltpu.VMEM((2, 1024, 256), jnp.float32)],
         compiler_params=pltpu.CompilerParams(vmem_limit_bytes=VMEM_LIMIT, dimension_semantics=("arbitrary",)),
         name="update",
-    )(slots, total, total, total, scaled, tri_factors, vectors)
+    )(slots, total, total, scaled, tri_factors, vectors)
 
 
 def per_device(vectors, panel_store, block_ids, offsets, tri_factors):

time: 162 us -> 171 us (1.056)
  Pallas kernels: 162 us -> 171 us
    pallas_call x1, Pallas kernels: 57.3 us -> 67.4 us  [sum_products(): pl.pallas_call(sum_kernel, out_shape=jax.ShapeDtypeStruct((TILES, 512, 12...]
where the time goes in v5:
time: 171 us
  Pallas kernels  171 us (100%)
    pallas_call x1, Pallas kernels, products(): pl.pallas_call(product_kernel, out_shape=(jax.ShapeDtypeStruct((TILES, 51...  82.4 us
    pallas_call x1, Pallas kernels, sum_products(): pl.pallas_call(sum_kernel, out_shape=jax.ShapeDtypeStruct((TILES, 512, 12...  67.4 us
    pallas_call x1, Pallas kernels, update(): pl.pallas_call(update_kernel, grid=(4,), out_shape=jax.ShapeDtypeStruct(v...  21.5 us

profile of v5, /device:TPU:1, one launch (start us, length us, event | category | flops | bytes accessed | tf_op | source)
XLA Modules:
  0.0 171.3 jit_solution(3855013269191961076)
XLA Ops:
  0.0 82.4 %products.1 = (f32[18,512,128]{2,1,0:T(8,128)}, f32[2,1024,512]{2,1,0:T(8,128)}, s32[8,128]{1,0:T(8,128)}) custom-call(s32[2]{0:T(128)} %offsets_ref.1, s32[2,128]{1,0:T(2,128)} %ids_ref.1, f32[2,2,1024,256]{3,2,1,0:T(8,128)} %store_ref.1, f32[2,2,256,256]{3,2,1,0:T(8,128)} %tri_ref.3, f32[2,128,8,1024]{3,2,1,0:T(8,128)} %bitcast.1), custom_call_target="tpu_custom_call" | custom-call | tf_op jit(solution)/shard_map/products/pallas_call | solution.py:295
  82.4 67.4 %sum_products.1.g_ref.y_ref = f32[18,512,128]{2,1,0:T(8,128)} custom-call(f32[18,512,128]{2,1,0:T(8,128)} %get-tuple-element.9.part_ref), custom_call_target="tpu_custom_call" | custom-call | tf_op jit(solution)/shard_map/sum_products/pallas_call | solution.py:516
  149.8 21.5 %update.1 = f32[2,1024,1024]{2,1,0:T(8,128)} custom-call(s32[8,128]{1,0:T(8,128)} %get-tuple-element.8.slot_ref, f32[18,512,128]{2,1,0:T(8,128)} %sum_products.1.g_ref.y_ref, f32[18,512,128]{2,1,0:T(8,128)} %sum_products.1.g_ref.y_ref, f32[2,1024,512]{2,1,0:T(8,128)} %get-tuple-element.10.x_ref, f32[2,2,256,256]{3,2,1,0:T(8,128)} %tri_ref.3, ...), custom_call_target="tpu_custom_call" | custom-call | tf_op jit(solution)/shard_map/update/pallas_call | solution.py:577

commit v6 on v5

v6 whole, which is shorter than its diff:
```python
import jax
import jax.numpy as jnp
from jax import lax
from jax.experimental import pallas as pl
from jax.experimental.pallas import tpu as pltpu
from jax.sharding import PartitionSpec as P


MESH = pl.DeviceIdType.MESH


def strip_of(x, y, z, core):
    return ((x * 2 + z % 2) * 4 + y) * 4 + (z // 2) * 2 + core


VMEM_LIMIT = 60 * 1024 * 1024


def split(value):
    high = value.astype(jnp.bfloat16)
    return high, (value - high.astype(jnp.float32)).astype(jnp.bfloat16)


def dot(first_op, second_op):
    return jnp.dot(first_op, second_op, preferred_element_type=jnp.float32)


def left_pieces(value):
    high, low = split(value)
    return jnp.concatenate([high, high, low], axis=1)


def right_pieces(value):
    high, low = split(value)
    return jnp.concatenate([high, low, high], axis=0)


def left_forms(real_part, imag_part):
    return left_pieces(real_part + imag_part), left_pieces(real_part), left_pieces(imag_part)


def right_forms(real_part, imag_part):
    return right_pieces(real_part), right_pieces(imag_part - real_part), right_pieces(real_part + imag_part)


def complex_dot(left, right):
    shared = dot(left[0], right[0])
    return shared - dot(left[2], right[2]), shared + dot(left[1], right[1])


def adjoint_upper(tri_ref, panel):
    shape = tri_ref.shape[2:]
    upper = lax.broadcasted_iota(jnp.int32, shape, 0) <= lax.broadcasted_iota(jnp.int32, shape, 1)
    return jnp.where(upper, tri_ref[panel, 0], 0.0).T, -jnp.where(upper, tri_ref[panel, 1], 0.0).T


GROUPS = (
    ((0, 64), (64, 64)),
    ((0, 64), (64, 32), (96, 16), (112, 16)),
)


def product_kernel(
    offsets_ref,
    ids_ref,
    store_ref,
    tri_ref,
    vectors_ref,
    y_out_ref,
    x_out_ref,
    slot_out_ref,
    z_ref,
    first_blocks_ref,
    second_blocks_ref,
    relay_ref,
    all_ids_ref,
    order_ref,
    slot_ref,
    first_panel_ref,
    second_panel_ref,
    rows_ref,
    match_ref,
    left_ref,
    factor_ref,
    y_ref,
    x_ref,
    block_send_sem,
    block_recv_sem,
    id_send_sem,
    id_recv_sem,
    hop_send_sem,
    hop_recv_sem,
    last_send_sem,
    local_sem,
):
    blocks_refs = (first_blocks_ref, second_blocks_ref)
    panel_refs = (first_panel_ref, second_panel_ref)
    row = lax.axis_index("row")
    col = lax.axis_index("col")
    me = row * 4 + col
    x = row // 8
    y = row % 4
    z = (col // 2) * 2 + (row // 4) % 2
    core = col % 2

    barrier = pltpu.get_barrier_semaphore()

    def greet(step, carry):
        peer = (me + step) % 128
        pl.semaphore_signal(barrier, inc=1, device_id=(peer // 4, peer % 4), device_id_type=MESH)
        return carry

    lax.fori_loop(1, 128, greet, 0)

    def listed(strip):
        return pl.ds(pl.multiple_of(strip * 8, 8), 8)

    own_copies = [
        pltpu.make_async_copy(store_ref.at[panel, :, listed(me), :], blocks_refs[panel].at[0], local_sem.at[panel])
        for panel in range(2)
    ]
    own_copies.append(pltpu.make_async_copy(ids_ref, all_ids_ref.at[0], local_sem.at[2]))
    for copy in own_copies:
        copy.start()
    fetch_vectors = pltpu.make_async_copy(vectors_ref, z_ref, local_sem.at[3])
    fetch_vectors.start()
    pl.semaphore_wait(barrier, 127)

    def offset(step):
        spread = (step // 2 * 27) % 64
        return spread % 4, (spread // 4) % 4, spread // 16

    def opposite(shift):
        return (shift // 2) * (1 - shift % 2)

    def strip_at(step):
        dx, dy, dz = offset(step)
        return strip_of((x + dx) % 4, (y + dy) % 4, (z + dz) % 4, (core + step) % 2)

    def is_opposite(step):
        dx, dy, dz = offset(step)
        return opposite(dx) + opposite(dy) + opposite(dz) > 0

    def is_relayed(step):
        dx, dy, dz = offset(step)
        return (opposite(dx) + opposite(dy) + opposite(dz)) * (step % 2) > 0

    def relay_of(step):
        dx, dy, dz = offset(step)
        return strip_of((x + opposite(dx)) % 4, (y + opposite(dy)) % 4, (z + opposite(dz)) % 4, core)

    def relayed_target(step):
        dx, dy, dz = offset(step)
        return strip_of(
            (x + 4 - opposite(dx) + dx) % 4,
            (y + 4 - opposite(dy) + dy) % 4,
            (z + 4 - opposite(dz) + dz) % 4,
            (core + step) % 2,
        )

    def remote(source, target, sent, received, strip):
        return pltpu.make_async_remote_copy(
            source,
            target,
            sent,
            received,
            device_id=(strip // 4, strip % 4),
            device_id_type=MESH,
        )

    def block_copy(panel, step):
        strip = strip_at(step)
        return remote(
            store_ref.at[panel, :, listed(strip), :],
            blocks_refs[panel].at[step],
            block_send_sem.at[panel, step],
            block_recv_sem.at[panel, step],
            strip,
        )

    def hop_copy(step):
        return remote(
            store_ref.at[:, :, listed(strip_at(step)), :],
            relay_ref.at[step // 2],
            hop_send_sem.at[step // 2],
            hop_recv_sem.at[step // 2],
            relay_of(step),
        )

    def last_copy(panel, step):
        return remote(
            relay_ref.at[step // 2, panel],
            blocks_refs[panel].at[step],
            last_send_sem.at[panel, step // 2],
            block_recv_sem.at[panel, step],
            relayed_target(step),
        )

    def id_copy(step):
        return remote(ids_ref, all_ids_ref.at[step], id_send_sem.at[step], id_recv_sem.at[step], strip_at(step))

    def send_ids(step, carry):
        id_copy(step).start()
        return carry

    def send_opposite(step, carry):
        @pl.when(is_relayed(step))
        def _():
            hop_copy(step).start()
            block_copy(0, step - 1).start()

        return carry

    def send_first(step, carry):
        @pl.when(jnp.logical_not(is_opposite(step)))
        def _():
            block_copy(0, step).start()

        return carry

    def send_second(step, carry):
        @pl.when(jnp.logical_not(is_relayed(step)))
        def _():
            block_copy(1, step).start()

        return carry

    def forward_first(step, carry):
        @pl.when(is_relayed(step))
        def _():
            hop_copy(step).wait_recv()
            last_copy(0, step).start()

        return carry

    def forward_second(step, carry):
        @pl.when(is_relayed(step))
        def _():
            last_copy(1, step).start()

        return carry

    lax.fori_loop(1, 128, send_opposite, 0)
    lax.fori_loop(1, 128, send_ids, 0)
    lax.fori_loop(1, 128, send_first, 0)

    for panel in range(2):
        forms = right_forms(*adjoint_upper(tri_ref, panel))
        for form in range(3):
            factor_ref[panel, form] = forms[form]

    for copy in own_copies:
        copy.wait()

    def wait_ids(step, carry):
        id_copy(step).wait_recv()
        return carry

    lax.fori_loop(1, 128, wait_ids, 0)
    down = lax.broadcasted_iota(jnp.int32, (128, 128), 0)
    lane = lax.broadcasted_iota(jnp.int32, (128, 128), 1)
    order_ref[...] = jnp.zeros_like(order_ref)
    places = []
    for panel in range(2):
        own = jnp.sum(jnp.where(lane == me, all_ids_ref[:, panel, :], 0), axis=1, keepdims=True) % 128
        places.append(jnp.sum(jnp.where(down == lane, own, 0), axis=0, keepdims=True))
        order_ref[panel : panel + 1, :] = places[panel]
        order_ref[panel + 3 : panel + 4, :] = jnp.max(jnp.where(own == lane, down, 0), axis=0, keepdims=True)
    slot_of_place = jnp.max(jnp.where(places[0] == down, lane, 0), axis=1, keepdims=True)
    order_ref[2:3, :] = jnp.max(jnp.where(places[1] == down, slot_of_place, 0), axis=0, keepdims=True)
    fetch_order = pltpu.make_async_copy(order_ref, slot_ref, local_sem.at[4])
    fetch_order.start()
    fetch_order.wait()
    write_order = pltpu.make_async_copy(order_ref, slot_out_ref, local_sem.at[5])
    write_order.start()
    fetch_vectors.wait()

    def take_group(panel, first, count):
        size = count * 8
        start = first * 8
        begin = first == 0
        values = panel_refs[panel]

        def wait_block(step, carry):
            block_copy(panel, step).wait_recv()
            return carry

        lax.fori_loop(max(first, 1), first + count, wait_block, 0)

        def take_block(step, carry):
            slot = first + step
            place = slot_ref[panel, slot]
            near = pl.ds(pl.multiple_of(step * 8, 8), 8)
            row_index = me * 1024 + place * 8 + lax.broadcasted_iota(jnp.int32, (8, 256), 0)
            limit = offsets_ref[panel] + lax.broadcasted_iota(jnp.int32, (8, 256), 1)
            below = row_index > limit
            diagonal = jnp.where(row_index == limit, 1.0, 0.0)
            values[0, slot] = jnp.where(below, blocks_refs[panel][slot, 0], diagonal)
            values[1, slot] = jnp.where(below, blocks_refs[panel][slot, 1], 0.0)
            rows_ref[0, near, :] = z_ref[0, place]
            rows_ref[1, near, :] = z_ref[1, place]
            if panel == 1:
                matching = slot_ref[2, slot]
                match_ref[0, near, :] = first_panel_ref[0, matching]
                match_ref[1, near, :] = first_panel_ref[1, matching]
            return carry

        lax.fori_loop(0, count, take_block, 0, unroll=4)

        own = [values[part, first : first + count].reshape(size, 256) for part in range(2)]
        forms = left_forms(own[0].T, -own[1].T)
        for form in range(3):
            left_ref[form, :, 0 : 3 * size] = forms[form]

        def adjoint_products(right):
            return complex_dot([left_ref[form, :, 0 : 3 * size] for form in range(3)], right)

        def add_tiles(tile, parts):
            for part in range(2):
                for side in range(2):
                    value = parts[part][:, side * 128 : (side + 1) * 128]
                    target = y_ref.at[tile + side, part * 256 : (part + 1) * 256, :]
                    if begin:
                        target[...] = value
                    else:
                        target[...] += value

        def take_columns(chunk, carry):
            columns = pl.ds(pl.multiple_of(chunk * 256, 256), 256)
            right = right_forms(rows_ref[0, 0:size, columns], rows_ref[1, 0:size, columns])
            add_tiles(4 * chunk + 2 * panel, adjoint_products(right))
            return carry

        lax.fori_loop(0, 4, take_columns, 0)

        if panel == 1:
            matched = (match_ref[0, 0:size, :], match_ref[1, 0:size, :])
            add_tiles(16, adjoint_products(right_forms(*matched)))
            for which, source in enumerate((matched, own)):
                scaled = complex_dot(left_forms(*source), [factor_ref[which, form] for form in range(3)])
                for part in range(2):
                    x_ref[part, start : start + size, which * 256 : (which + 1) * 256] = scaled[part]

    lax.fori_loop(1, 128, forward_first, 0)
    lax.fori_loop(1, 128, send_second, 0)
    for panel in range(2):
        for first, count in GROUPS[panel]:
            take_group(panel, first, count)
            if panel == 0 and first == 0:
                lax.fori_loop(1, 128, forward_second, 0)

    y_copy = pltpu.make_async_copy(y_ref, y_out_ref, local_sem.at[6])
    x_copy = pltpu.make_async_copy(x_ref, x_out_ref, local_sem.at[7])
    y_copy.start()
    x_copy.start()

    def wait_sent(step, carry):
        id_copy(step).wait_send()
        relayed = is_relayed(step)

        @pl.when(relayed)
        def _():
            hop_copy(step).wait_send()
            last_copy(0, step).wait_send()
            last_copy(1, step).wait_send()

        @pl.when(jnp.logical_not(relayed))
        def _():
            block_copy(0, step).wait_send()
            block_copy(1, step).wait_send()

        return carry

    lax.fori_loop(1, 128, wait_sent, 0)
    write_order.wait()
    y_copy.wait()
    x_copy.wait()


def products(vectors, panel_store, block_ids, offsets, tri_factors):
    f32 = jnp.float32
    bf16 = jnp.bfloat16
    whole = pl.BlockSpec(memory_space=pltpu.VMEM)
    anywhere = pl.BlockSpec(memory_space=pl.ANY)
    dma = pltpu.SemaphoreType.DMA
    return pl.pallas_call(
        product_kernel,
        out_shape=(
            jax.ShapeDtypeStruct((18, 512, 128), f32),
            jax.ShapeDtypeStruct((2, 1024, 512), f32),
            jax.ShapeDtypeStruct((8, 128), jnp.int32),
        ),
        in_specs=[pl.BlockSpec(memory_space=pltpu.SMEM), whole, anywhere, whole, anywhere],
        out_specs=[anywhere] * 3,
        scratch_shapes=[
            pltpu.VMEM((2, 128, 8, 1024), f32),
            pltpu.VMEM((128, 2, 8, 256), f32),
            pltpu.VMEM((128, 2, 8, 256), f32),
            pltpu.VMEM((64, 2, 2, 8, 256), f32),
            pltpu.VMEM((128, 2, 128), jnp.int32),
            pltpu.VMEM((8, 128), jnp.int32),
            pltpu.SMEM((8, 128), jnp.int32),
            pltpu.VMEM((2, 128, 8, 256), f32),
            pltpu.VMEM((2, 128, 8, 256), f32),
            pltpu.VMEM((2, 512, 1024), f32),
            pltpu.VMEM((2, 512, 256), f32),
            pltpu.VMEM((3, 256, 1536), bf16),
            pltpu.VMEM((2, 3, 768, 256), bf16),
            pltpu.VMEM((18, 512, 128), f32),
            pltpu.VMEM((2, 1024, 512), f32),
            dma((2, 128)),
            dma((2, 128)),
            dma((128,)),
            dma((128,)),
            dma((64,)),
            dma((64,)),
            dma((2, 64)),
            dma((8,)),
        ],
        compiler_params=pltpu.CompilerParams(
            vmem_limit_bytes=VMEM_LIMIT, collective_id=0, has_side_effects=True
        ),
        name="products",
    )(offsets, block_ids, panel_store, tri_factors, vectors.reshape(2, 128, 8, 1024))


TILES = 9
LINKS = ((), (0,), (1, 2), (3, 4, 5))
HALF_STAGES = len(LINKS)
STAGES = 2 * HALF_STAGES
SIZES = [1024, 512, 256, 64, 8]
COUNTS = [SIZES[stage] - SIZES[stage + 1] for stage in range(HALF_STAGES)]
BASES = [sum(COUNTS[:stage]) for stage in range(HALF_STAGES)]


def level_of(stage):
    return stage if stage < HALF_STAGES else STAGES - 1 - stage


def step_order():
    free = [0.0] * 7
    now = 0.0
    ready = []
    order = []
    work = []
    finished = set()
    queued = set()

    def send(tile, stage):
        nonlocal now
        level = level_of(stage)
        now += 0.06 * (2 ** len(LINKS[level]) - 1 if level else 1)
        if level == 0:
            free[6] = max(free[6], now) + 512 * 0.512 / 600
            arrival = free[6]
        else:
            arrival = now
            for link in LINKS[level]:
                link = (tile + link) % 6
                free[link] = max(free[link], now) + SIZES[level] / 2 * 0.512 / 50
                arrival = max(arrival, free[link])
        ready.append((arrival + 2.5, tile, stage))

    for tile in [TILES - 1] + list(range(TILES - 1)):
        send(tile, 0)
    while ready or work:
        ready.sort()
        if ready and (ready[0][0] <= now or not work):
            arrival, tile, stage = ready.pop(0)
            order.append((tile, stage))
            now = max(now, arrival) + (0.05 + COUNTS[stage] * 0.0006 if stage < HALF_STAGES else 0.03)
            if stage < STAGES - 1:
                send(tile, stage + 1)
            else:
                finished.add(tile)
            if TILES - 1 in finished:
                if None not in queued:
                    queued.add(None)
                    work += [(None, piece) for piece in range(4)]
                for chunk in range(4):
                    if chunk not in queued and {2 * chunk, 2 * chunk + 1} <= finished:
                        queued.add(chunk)
                        work += [(-1 - chunk, piece) for piece in range(4)]
        else:
            order.append(work.pop(0))
            now += 0.8
    return order


def sum_kernel(
    slot_ref,
    part_ref,
    x_in_ref,
    tri_ref,
    vectors_ref,
    out_ref,
    total_ref,
    held_ref,
    landed_ref,
    x_ref,
    left_ref,
    cross_ref,
    right_ref,
    z_ref,
    change_ref,
    result_ref,
    send_sem,
    recv_sem,
    local_sem,
):
    row = lax.axis_index("row")
    col = lax.axis_index("col")
    here = (row // 8, row % 4, (col // 2) * 2 + (row // 4) % 2)
    core = col % 2

    fetch_x = pltpu.make_async_copy(x_in_ref, x_ref, local_sem.at[0])
    fetch_z = pltpu.make_async_copy(vectors_ref, z_ref, local_sem.at[1])

    def device(place, core):
        strip = strip_of(*place, core)
        return (strip // 4, strip % 4)

    sibling = device(here, 1 - core)
    other = [place + 1 - 2 * (place % 2) for place in here] + [3 - place for place in here]
    bits = [((place + 1) // 2) % 2 for place in here] + [place // 2 for place in here]

    def across(links):
        place = list(here)
        for link in links:
            place[link % 3] = other[link]
        return device(place, core)

    barrier = pltpu.get_barrier_semaphore()
    peers = [sibling]
    for first in (None, 0, 3):
        for second in (None, 1, 4):
            for third in (None, 2, 5):
                chosen = [link for link in (first, second, third) if link is not None]
                if chosen:
                    peers.append(across(chosen))
    for peer in peers:
        pl.semaphore_signal(barrier, inc=1, device_id=peer, device_id_type=MESH)
    pl.semaphore_wait(barrier, len(peers))

    def rows_at(first, count):
        return pl.ds(pl.multiple_of(first, 8), count)

    def send(tile, stage, source, target, peer):
        pltpu.make_async_remote_copy(
            source,
            target,
            send_sem.at[tile, stage],
            recv_sem.at[tile, stage],
            device_id=peer,
            device_id_type=MESH,
        ).start()

    def wait(tile, stage, sem):
        some = landed_ref.at[tile, pl.ds(0, COUNTS[level_of(stage)]), :]
        pltpu.make_async_copy(some, some, sem.at[tile, stage]).wait()

    def links_of(tile, level):
        return [(tile + link) % 6 for link in LINKS[level]]

    def share(tile, level, flips=0):
        index = 0
        for place, link in enumerate(links_of(tile, level)):
            index = index * 2 + (1 - bits[link] if flips >> place & 1 else bits[link])
        return index

    def flipped(tile, level, flips):
        return across([link for place, link in enumerate(links_of(tile, level)) if flips >> place & 1])

    lows = [0] * TILES

    def split_rows(tile, level):
        held = held_ref.at[tile]
        size = SIZES[level + 1]
        for flips in range(1, 2 ** len(LINKS[level])):
            send(
                tile,
                level,
                held.at[rows_at(lows[tile] + share(tile, level, flips) * size, size), :],
                landed_ref.at[tile, pl.ds(BASES[level] + (flips - 1) * size, size), :],
                flipped(tile, level, flips),
            )
        lows[tile] = lows[tile] + share(tile, level) * size

    def return_rows(tile, level):
        size = SIZES[level + 1]
        place = total_ref.at[tile, rows_at(core * 512 + lows[tile], size), :]
        for flips in range(1, 2 ** len(LINKS[level])):
            send(tile, STAGES - 1 - level, place, place, flipped(tile, level, flips))

    def advance(tile, stage):
        level = level_of(stage)
        held = held_ref.at[tile]
        wait(tile, stage, recv_sem)
        if stage == 0:
            held[...] = part_ref[tile, rows_at(core * 512, 512), :] + landed_ref[tile, 0:512, :]
            split_rows(tile, 1)
        elif stage < HALF_STAGES:
            size = SIZES[level + 1]
            value = held[rows_at(lows[tile], size), :]
            for piece in range(2 ** len(LINKS[level]) - 1):
                start = BASES[level] + piece * size
                value += landed_ref[tile, start : start + size, :]
            if stage < HALF_STAGES - 1:
                held[rows_at(lows[tile], size), :] = value
                split_rows(tile, level + 1)
            else:
                total_ref[tile, rows_at(core * 512 + lows[tile], size), :] = value
                return_rows(tile, level)
        elif stage < STAGES - 1:
            lows[tile] = lows[tile] - share(tile, level) * SIZES[level + 1]
            if level > 1:
                return_rows(tile, level - 1)
            else:
                place = total_ref.at[tile, rows_at(core * 512, 512), :]
                send(tile, STAGES - 1, place, place, sibling)

    def parts(tile):
        values = total_ref[tile]
        real_part = jnp.concatenate([values[0:256], values[512:768]], axis=1)
        imag_part = jnp.concatenate([values[256:512], values[768:1024]], axis=1)
        return real_part, imag_part

    def correct(piece):
        if piece == 0:
            fetch_x.wait()
            cross = complex_dot(left_forms(*parts(TILES - 1)), right_forms(*adjoint_upper(tri_ref, 0)))
            cross = right_forms(*cross)
            for form in range(3):
                cross_ref[form] = cross[form]
        rows = slice(piece * 256, (piece + 1) * 256)
        second = left_forms(x_ref[0, rows, 256:512], x_ref[1, rows, 256:512])
        real_part, imag_part = complex_dot(second, [cross_ref[form] for form in range(3)])
        first = left_forms(x_ref[0, rows, 0:256] - real_part, x_ref[1, rows, 0:256] - imag_part)
        for form in range(3):
            for part in range(3):
                start = part * 512
                left_ref[form, rows, start : start + 256] = first[form][:, part * 256 : (part + 1) * 256]
                left_ref[form, rows, start + 256 : start + 512] = second[form][:, part * 256 : (part + 1) * 256]

    written = []

    def apply(chunk, piece):
        if piece == 0:
            first = parts(2 * chunk)
            second = parts(2 * chunk + 1)
            forms = right_forms(*[jnp.concatenate([first[part], second[part]], axis=0) for part in range(2)])
            for form in range(3):
                right_ref[form] = forms[form]
        rows = slice(piece * 256, (piece + 1) * 256)
        change = complex_dot([left_ref[form, rows, :] for form in range(3)], [right_ref[form] for form in range(3)])
        for part in range(2):
            change_ref[part, piece * 32 : (piece + 1) * 32] = change[part].reshape(32, 8, 256)
        if piece < 3:
            return
        if not written:
            fetch_z.wait()
        if len(written) > 1:
            written[-2].wait()
        columns = slice(chunk * 256, (chunk + 1) * 256)
        result = result_ref.at[len(written) % 2]

        def put_block(block, carry):
            slot = slot_ref[4, block]
            rows = pl.ds(pl.multiple_of(block * 8, 8), 8)
            for part in range(2):
                result[part, rows, :] = z_ref[part, rows, columns] - change_ref[part, slot]
            return carry

        lax.fori_loop(0, 128, put_block, 0, unroll=8)
        copy = pltpu.make_async_copy(result, out_ref.at[:, :, columns], local_sem.at[2 + len(written)])
        copy.start()
        written.append(copy)

    for tile in [TILES - 1] + list(range(TILES - 1)):
        send(
            tile,
            0,
            part_ref.at[tile, rows_at((1 - core) * 512, 512), :],
            landed_ref.at[tile, pl.ds(0, 512), :],
            sibling,
        )
    fetch_x.start()
    fetch_z.start()
    for tile, step in step_order():
        if tile is None:
            correct(step)
        elif tile < 0:
            apply(-1 - tile, step)
        else:
            advance(tile, step)
    for tile in range(TILES):
        for stage in range(STAGES):
            wait(tile, stage, send_sem)
    for copy in written[-2:]:
        copy.wait()


def sum_and_update(slots, partial, scaled, tri_factors, vectors):
    f32 = jnp.float32
    bf16 = jnp.bfloat16
    whole = pl.BlockSpec(memory_space=pltpu.VMEM)
    anywhere = pl.BlockSpec(memory_space=pl.ANY)
    dma = pltpu.SemaphoreType.DMA
    return pl.pallas_call(
        sum_kernel,
        out_shape=jax.ShapeDtypeStruct(vectors.shape, f32),
        in_specs=[pl.BlockSpec(memory_space=pltpu.SMEM), whole, anywhere, whole, anywhere],
        out_specs=anywhere,
        scratch_shapes=[
            pltpu.VMEM((TILES, 1024, 128), f32),
            pltpu.VMEM((TILES, 512, 128), f32),
            pltpu.VMEM((TILES, 1024, 128), f32),
            pltpu.VMEM((2, 1024, 512), f32),
            pltpu.VMEM((3, 1024, 1536), bf16),
            pltpu.VMEM((3, 768, 256), bf16),
            pltpu.VMEM((3, 1536, 256), bf16),
            pltpu.VMEM((2, 1024, 1024), f32),
            pltpu.VMEM((2, 128, 8, 256), f32),
            pltpu.VMEM((2, 2, 1024, 256), f32),
            dma((TILES, STAGES)),
            dma((TILES, STAGES)),
            dma((6,)),
        ],
        compiler_params=pltpu.CompilerParams(
            vmem_limit_bytes=VMEM_LIMIT, collective_id=1, has_side_effects=True
        ),
        name="sum_and_update",
    )(slots, partial.reshape(TILES, 1024, 128), scaled, tri_factors, vectors)


def per_device(vectors, panel_store, block_ids, offsets, tri_factors):
    partial, scaled, slots = products(vectors, panel_store, block_ids, offsets, tri_factors)
    return sum_and_update(slots, partial, scaled, tri_factors, vectors)


def solution(mesh):
    placed = (
        P(None, ("row", "col"), None),
        P(None, None, ("row", "col"), None),
        P(None, ("row", "col")),
        P(),
        P(),
    )
    return jax.shard_map(
        per_device,
        mesh=mesh,
        in_specs=placed,
        out_specs=P(None, ("row", "col"), None),
        check_vma=False,
    )
```

time: 171 us -> 182 us (1.064)
  local copies, waits for them, and re-layouts: 0 us -> 8.44 us
  Pallas kernels: 171 us -> 173 us
    unnamed x0 -> x1, local copies, waits for them, and re-layouts: none -> 8.44 us
    pallas_call x3 -> x2, Pallas kernels: 171 us -> 173 us  [the longest x1 111 us: products(): pl.pallas_call(product_kernel, out_shape=(jax.ShapeDtypeStruct((18, 512,...]
where the time goes in v6:
time: 182 us; the launch traced here: 181 us
  Pallas kernels  173 us (95%)
  local copies, waits for them, and re-layouts  8.44 us (5%)
    pallas_call x1, Pallas kernels, products(): pl.pallas_call(product_kernel, out_shape=(jax.ShapeDtypeStruct((18, 512,...  111 us
    pallas_call x1, Pallas kernels, sum_and_update(): pl.pallas_call(sum_kernel, out_shape=jax.ShapeDtypeStruct(vectors.shape,...  61.6 us
    unnamed x1, local copies, waits for them, and re-layouts  8.44 us

profile of v6, /device:TPU:1, one launch (start us, length us, event | category | flops | bytes accessed | tf_op | source)
XLA Modules:
  0.0 181.5 jit_solution(7112329372883957738)
XLA Ops:
  0.0 111.5 %products.1 = (f32[18,512,128]{2,1,0:T(8,128)}, f32[2,1024,512]{2,1,0:T(8,128)}, s32[8,128]{1,0:T(8,128)}) custom-call(s32[2]{0:T(128)} %offsets_ref.1, s32[2,128]{1,0:T(2,128)} %ids_ref.1, f32[2,2,1024,256]{3,2,1,0:T(8,128)} %store_ref.1, f32[2,2,256,256]{3,2,1,0:T(8,128)} %tri_ref.3, f32[2,128,8,1024]{3,2,1,0:T(8,128)} %bitcast.2), custom_call_target="tpu_custom_call" | custom-call | tf_op jit(solution)/shard_map/products/pallas_call | solution.py:386
  111.5 61.6 %sum_and_update.1 = f32[2,1024,1024]{2,1,0:T(8,128)} custom-call(s32[8,128]{1,0:T(8,128)} %get-tuple-element.8.slot_ref, f32[9,1024,128]{2,1,0:T(8,128)} %bitcast.3, f32[2,1024,512]{2,1,0:T(8,128)} %get-tuple-element.10.x_in_ref, f32[2,2,256,256]{3,2,1,0:T(8,128)} %tri_ref.3, f32[2,1024,1024]{2,1,0:T(8,128)} %vectors_ref.1), custom_call_target="tpu_custom_call" | custom-call | tf_op jit(solution)/shard_map/sum_and_update/pallas_call | solution.py:709
  173.0 8.4 %copy.7 = f32[2,1024,1024]{2,1,0:T(8,128)} copy(f32[2,1024,1024]{2,1,0:T(8,128)} %sum_and_update.1) | data formatting | bytes 16777216

commit v7 on v0

v7 whole, which is shorter than its diff:
```python
import jax
import jax.numpy as jnp
from jax import lax
from jax.experimental import pallas as pl
from jax.experimental.pallas import tpu as pltpu
from jax.sharding import PartitionSpec as P


MESH = pl.DeviceIdType.MESH


def strip_of(x, y, z, core):
    return ((x * 2 + z % 2) * 4 + y) * 4 + (z // 2) * 2 + core


VMEM_LIMIT = 60 * 1024 * 1024


def split(value):
    high = value.astype(jnp.bfloat16)
    return high, (value - high.astype(jnp.float32)).astype(jnp.bfloat16)


def dot(first_op, second_op):
    return jnp.dot(first_op, second_op, preferred_element_type=jnp.float32)


def left_pieces(value):
    high, low = split(value)
    return jnp.concatenate([high, high, low], axis=1)


def right_pieces(value):
    high, low = split(value)
    return jnp.concatenate([high, low, high], axis=0)


def left_forms(real_part, imag_part):
    return left_pieces(real_part + imag_part), left_pieces(real_part), left_pieces(imag_part)


def right_forms(real_part, imag_part):
    return right_pieces(real_part), right_pieces(imag_part - real_part), right_pieces(real_part + imag_part)


def complex_dot(left, right):
    shared = dot(left[0], right[0])
    return shared - dot(left[2], right[2]), shared + dot(left[1], right[1])


def adjoint_upper(tri_ref, panel):
    shape = tri_ref.shape[2:]
    upper = lax.broadcasted_iota(jnp.int32, shape, 0) <= lax.broadcasted_iota(jnp.int32, shape, 1)
    return jnp.where(upper, tri_ref[panel, 0], 0.0).T, -jnp.where(upper, tri_ref[panel, 1], 0.0).T


GROUPS = (
    ((0, 64), (64, 64)),
    ((0, 64), (64, 32), (96, 16), (112, 16)),
)


TILES = 9
LINKS = ((), (0,), (1, 2), (3, 4, 5))
HALF_STAGES = len(LINKS)
STAGES = 2 * HALF_STAGES
SIZES = [1024, 512, 256, 64, 8]
COUNTS = [SIZES[stage] - SIZES[stage + 1] for stage in range(HALF_STAGES)]
BASES = [sum(COUNTS[:stage]) for stage in range(HALF_STAGES)]


def level_of(stage):
    return stage if stage < HALF_STAGES else STAGES - 1 - stage


def step_order():
    free = [0.0] * 7
    now = 0.0
    ready = []
    order = []
    work = []
    finished = set()
    queued = set()

    def send(tile, stage):
        nonlocal now
        level = level_of(stage)
        now += 0.06 * (2 ** len(LINKS[level]) - 1 if level else 1)
        if level == 0:
            free[6] = max(free[6], now) + 512 * 0.512 / 600
            arrival = free[6]
        else:
            arrival = now
            for link in LINKS[level]:
                link = (tile + link) % 6
                free[link] = max(free[link], now) + SIZES[level] / 2 * 0.512 / 50
                arrival = max(arrival, free[link])
        ready.append((arrival + 2.5, tile, stage))

    for tile in range(0, TILES - 1, 2):
        ready.append((0.0, tile, 0))
    for tile in [TILES - 1] + list(range(1, TILES - 1, 2)):
        now += 0.5
        send(tile, 0)
    while ready or work:
        ready.sort()
        if ready and (ready[0][0] <= now or not work):
            arrival, tile, stage = ready.pop(0)
            order.append((tile, stage))
            now = max(now, arrival) + (0.05 + COUNTS[stage] * 0.0006 if stage < HALF_STAGES else 0.03)
            if stage < STAGES - 1:
                send(tile, stage + 1)
            else:
                finished.add(tile)
            if TILES - 1 in finished:
                if None not in queued:
                    queued.add(None)
                    work += [(None, piece) for piece in range(4)]
                for chunk in range(4):
                    if chunk not in queued and {2 * chunk, 2 * chunk + 1} <= finished:
                        queued.add(chunk)
                        work += [(-1 - chunk, piece) for piece in range(4)]
        else:
            order.append(work.pop(0))
            now += 0.8
    return order


def main_kernel(
    offsets_ref,
    ids_ref,
    store_ref,
    tri_ref,
    vectors_ref,
    out_ref,
    z_ref,
    first_blocks_ref,
    second_blocks_ref,
    all_ids_ref,
    order_ref,
    slot_ref,
    first_panel_ref,
    second_panel_ref,
    rows_ref,
    match_ref,
    adjoint_ref,
    factor_ref,
    part_ref,
    x_ref,
    total_ref,
    held_ref,
    landed_ref,
    left_ref,
    cross_ref,
    right_ref,
    block_send_sem,
    block_recv_sem,
    id_sem,
    send_sem,
    recv_sem,
    local_sem,
):
    blocks_refs = (first_blocks_ref, second_blocks_ref)
    panel_refs = (first_panel_ref, second_panel_ref)
    row = lax.axis_index("row")
    col = lax.axis_index("col")
    me = row * 4 + col
    x = row // 8
    y = row % 4
    z = (col // 2) * 2 + (row // 4) % 2
    here = (x, y, z)
    core = col % 2

    barrier = pltpu.get_barrier_semaphore()

    def greet(step, carry):
        peer = (me + step) % 128
        pl.semaphore_signal(barrier, inc=1, device_id=(peer // 4, peer % 4), device_id_type=MESH)
        return carry

    lax.fori_loop(1, 128, greet, 0)

    def listed(strip):
        return pl.ds(pl.multiple_of(strip * 8, 8), 8)

    own_copies = [
        pltpu.make_async_copy(store_ref.at[panel, :, listed(me), :], blocks_refs[panel].at[0], local_sem.at[panel])
        for panel in range(2)
    ]
    own_copies.append(pltpu.make_async_copy(ids_ref, all_ids_ref.at[0], local_sem.at[2]))
    for copy in own_copies:
        copy.start()
    fetch_vectors = pltpu.make_async_copy(vectors_ref, z_ref, local_sem.at[3])
    fetch_vectors.start()

    for panel in range(2):
        forms = right_forms(*adjoint_upper(tri_ref, panel))
        for form in range(3):
            factor_ref[panel, form] = forms[form]

    pl.semaphore_wait(barrier, 127)

    def remote(source, target, sent, received, device):
        return pltpu.make_async_remote_copy(
            source,
            target,
            sent,
            received,
            device_id=device,
            device_id_type=MESH,
        )

    def strip_at(step):
        spread = (step // 2 * 27) % 64
        return strip_of(
            (x + spread % 4) % 4, (y + (spread // 4) % 4) % 4, (z + spread // 16) % 4, (core + step) % 2
        )

    def send_blocks(panel, group, first, last):
        def body(step, carry):
            strip = strip_at(step)
            remote(
                store_ref.at[panel, :, listed(strip), :],
                blocks_refs[panel].at[step],
                block_send_sem.at[panel],
                block_recv_sem.at[panel, group],
                (strip // 4, strip % 4),
            ).start()
            return carry

        lax.fori_loop(first, last, body, 0)

    def send_ids(step, carry):
        strip = strip_at(step)
        remote(ids_ref, all_ids_ref.at[step], id_sem.at[0], id_sem.at[1], (strip // 4, strip % 4)).start()
        return carry

    def await_bytes(some, sem):
        pltpu.make_async_copy(some, some, sem).wait()

    send_blocks(0, 0, 1, 24)
    lax.fori_loop(1, 128, send_ids, 0)
    send_blocks(0, 0, 24, 64)
    for panel in range(2):
        for group, (first, count) in enumerate(GROUPS[panel]):
            if panel + group > 0:
                send_blocks(panel, group, max(first, 1), first + count)

    for copy in own_copies:
        copy.wait()
    await_bytes(all_ids_ref.at[pl.ds(1, 127)], id_sem.at[1])
    down = lax.broadcasted_iota(jnp.int32, (128, 128), 0)
    lane = lax.broadcasted_iota(jnp.int32, (128, 128), 1)
    order_ref[...] = jnp.zeros_like(order_ref)
    places = []
    for panel in range(2):
        own = jnp.sum(jnp.where(lane == me, all_ids_ref[:, panel, :], 0), axis=1, keepdims=True) % 128
        places.append(jnp.sum(jnp.where(down == lane, own, 0), axis=0, keepdims=True))
        order_ref[panel : panel + 1, :] = places[panel]
        order_ref[panel + 3 : panel + 4, :] = jnp.max(jnp.where(own == lane, down, 0), axis=0, keepdims=True)
    slot_of_place = jnp.max(jnp.where(places[0] == down, lane, 0), axis=1, keepdims=True)
    order_ref[2:3, :] = jnp.max(jnp.where(places[1] == down, slot_of_place, 0), axis=0, keepdims=True)
    fetch_order = pltpu.make_async_copy(order_ref, slot_ref, local_sem.at[4])
    fetch_order.start()
    fetch_order.wait()
    fetch_vectors.wait()

    def take_group(panel, group, begin_tile):
        first, count = GROUPS[panel][group]
        size = count * 8
        start = first * 8
        begin = first == 0
        values = panel_refs[panel]

        await_bytes(
            blocks_refs[panel].at[pl.ds(max(first, 1), first + count - max(first, 1))], block_recv_sem.at[panel, group]
        )

        def take_block(step, carry):
            slot = first + step
            place = slot_ref[panel, slot]
            near = pl.ds(pl.multiple_of(step * 8, 8), 8)
            row_index = me * 1024 + place * 8 + lax.broadcasted_iota(jnp.int32, (8, 256), 0)
            limit = offsets_ref[panel] + lax.broadcasted_iota(jnp.int32, (8, 256), 1)
            below = row_index > limit
            diagonal = jnp.where(row_index == limit, 1.0, 0.0)
            values[0, slot] = jnp.where(below, blocks_refs[panel][slot, 0], diagonal)
            values[1, slot] = jnp.where(below, blocks_refs[panel][slot, 1], 0.0)
            for part in range(2):
                wanted = z_ref[part, place]
                for chunk in range(4):
                    at = pl.ds(pl.multiple_of(chunk % 2 * 512 + step * 8, 8), 8)
                    rows_ref[chunk // 2, part, at, :] = wanted[:, chunk * 256 : (chunk + 1) * 256]
            if panel == 1:
                matching = slot_ref[2, slot]
                match_ref[0, near, :] = first_panel_ref[0, matching]
                match_ref[1, near, :] = first_panel_ref[1, matching]
            return carry

        lax.fori_loop(0, count, take_block, 0, unroll=4)

        own = [values[part, first : first + count].reshape(size, 256) for part in range(2)]
        forms = left_forms(own[0].T, -own[1].T)
        for form in range(3):
            adjoint_ref[form, :, 0 : 3 * size] = forms[form]

        def adjoint_products(right):
            return complex_dot([adjoint_ref[form, :, 0 : 3 * size] for form in range(3)], right)

        def add_tile(tile, parts):
            for part in range(2):
                for side in range(2):
                    value = parts[part][:, side * 128 : (side + 1) * 128]
                    start = side * 512 + part * 256
                    target = part_ref.at[tile, start : start + 256, :]
                    if begin:
                        target[...] = value
                    else:
                        target[...] += value

        if panel == 1:
            matched = (match_ref[0, 0:size, :], match_ref[1, 0:size, :])
            add_tile(TILES - 1, adjoint_products(right_forms(*matched)))
            if begin_tile is not None:
                begin_tile(TILES - 1)

        def take_columns(chunk, carry):
            at = pl.ds(pl.multiple_of(chunk % 2 * 512, 512), size)
            right = right_forms(rows_ref[chunk // 2, 0, at, :], rows_ref[chunk // 2, 1, at, :])
            add_tile(2 * chunk + panel, adjoint_products(right))
            return carry

        if begin_tile is None:
            lax.fori_loop(0, 4, take_columns, 0)
        else:
            for chunk in range(4):
                take_columns(chunk, 0)
                begin_tile(2 * chunk + panel)

        if panel == 1:
            for which, source in enumerate((matched, own)):
                scaled = complex_dot(left_forms(*source), [factor_ref[which, form] for form in range(3)])
                for part in range(2):
                    x_ref[part, start : start + size, which * 256 : (which + 1) * 256] = scaled[part]

    def device(place, core):
        strip = strip_of(*place, core)
        return (strip // 4, strip % 4)

    sibling = device(here, 1 - core)
    other = [place + 1 - 2 * (place % 2) for place in here] + [3 - place for place in here]
    bits = [((place + 1) // 2) % 2 for place in here] + [place // 2 for place in here]

    def across(links):
        place = list(here)
        for link in links:
            place[link % 3] = other[link]
        return device(place, core)

    def rows_at(first, count):
        return pl.ds(pl.multiple_of(first, 8), count)

    def send(tile, stage, source, target, peer):
        remote(source, target, send_sem.at[tile, stage], recv_sem.at[tile, stage], peer).start()

    def wait(tile, stage, sem):
        some = landed_ref.at[tile, pl.ds(0, COUNTS[level_of(stage)]), :]
        pltpu.make_async_copy(some, some, sem.at[tile, stage]).wait()

    def links_of(tile, level):
        return [(tile + link) % 6 for link in LINKS[level]]

    def share(tile, level, flips=0):
        index = 0
        for place, link in enumerate(links_of(tile, level)):
            index = index * 2 + (1 - bits[link] if flips >> place & 1 else bits[link])
        return index

    def flipped(tile, level, flips):
        return across([link for place, link in enumerate(links_of(tile, level)) if flips >> place & 1])

    lows = [0] * TILES

    def split_rows(tile, level):
        held = held_ref.at[tile]
        size = SIZES[level + 1]
        for flips in range(1, 2 ** len(LINKS[level])):
            send(
                tile,
                level,
                held.at[rows_at(lows[tile] + share(tile, level, flips) * size, size), :],
                landed_ref.at[tile, pl.ds(BASES[level] + (flips - 1) * size, size), :],
                flipped(tile, level, flips),
            )
        lows[tile] = lows[tile] + share(tile, level) * size

    def return_rows(tile, level):
        size = SIZES[level + 1]
        place = total_ref.at[tile, rows_at(core * 512 + lows[tile], size), :]
        for flips in range(1, 2 ** len(LINKS[level])):
            send(tile, STAGES - 1 - level, place, place, flipped(tile, level, flips))

    def advance(tile, stage):
        level = level_of(stage)
        held = held_ref.at[tile]
        wait(tile, stage, recv_sem)
        if stage == 0:
            held[...] = part_ref[tile, rows_at(core * 512, 512), :] + landed_ref[tile, 0:512, :]
            split_rows(tile, 1)
        elif stage < HALF_STAGES:
            size = SIZES[level + 1]
            value = held[rows_at(lows[tile], size), :]
            for piece in range(2 ** len(LINKS[level]) - 1):
                start = BASES[level] + piece * size
                value += landed_ref[tile, start : start + size, :]
            if stage < HALF_STAGES - 1:
                held[rows_at(lows[tile], size), :] = value
                split_rows(tile, level + 1)
            else:
                total_ref[tile, rows_at(core * 512 + lows[tile], size), :] = value
                return_rows(tile, level)
        elif stage < STAGES - 1:
            lows[tile] = lows[tile] - share(tile, level) * SIZES[level + 1]
            if level > 1:
                return_rows(tile, level - 1)
            else:
                place = total_ref.at[tile, rows_at(core * 512, 512), :]
                send(tile, STAGES - 1, place, place, sibling)

    def parts(tile):
        values = total_ref[tile]
        real_part = jnp.concatenate([values[0:256], values[512:768]], axis=1)
        imag_part = jnp.concatenate([values[256:512], values[768:1024]], axis=1)
        return real_part, imag_part

    def correct(piece):
        if piece == 0:
            cross = complex_dot(left_forms(*parts(TILES - 1)), right_forms(*adjoint_upper(tri_ref, 0)))
            cross = right_forms(*cross)
            for form in range(3):
                cross_ref[form] = cross[form]
        rows = slice(piece * 256, (piece + 1) * 256)
        second = left_forms(x_ref[0, rows, 256:512], x_ref[1, rows, 256:512])
        real_part, imag_part = complex_dot(second, [cross_ref[form] for form in range(3)])
        first = left_forms(x_ref[0, rows, 0:256] - real_part, x_ref[1, rows, 0:256] - imag_part)
        for form in range(3):
            for part in range(2):
                source = slice((part + 1) * 256, (part + 2) * 256)
                start = part * 512
                left_ref[form, rows, start : start + 256] = first[form][:, source]
                left_ref[form, rows, start + 256 : start + 512] = second[form][:, source]

    written = []

    def apply(chunk, piece):
        if piece == 0:
            first = parts(2 * chunk)
            second = parts(2 * chunk + 1)
            forms = right_forms(*[jnp.concatenate([first[part], second[part]], axis=0) for part in range(2)])
            for form in range(3):
                right_ref[form, 0:512, :] = forms[form][512:1024]
                right_ref[form, 512:1024, :] = forms[form][0:512]
                right_ref[form, 1024:1536, :] = forms[form][0:512]
        rows = slice(piece * 256, (piece + 1) * 256)
        sums = [
            dot(left_ref[form, rows, 0:512], right_ref[form, 0:512, :])
            + dot(left_ref[form, rows, :], right_ref[form, 512:1536, :])
            for form in range(3)
        ]
        change = (sums[0] - sums[2], sums[0] + sums[1])
        for part in range(2):
            first_blocks_ref[piece * 32 : (piece + 1) * 32, part] = change[part].reshape(32, 8, 256)
        if piece < 3:
            return
        if len(written) > 1:
            written[-2].wait()
        columns = slice(chunk * 256, (chunk + 1) * 256)
        result = rows_ref.at[len(written) % 2]

        def put_block(block, carry):
            slot = slot_ref[4, block]
            rows = pl.ds(pl.multiple_of(block * 8, 8), 8)
            for part in range(2):
                result[part, rows, :] = z_ref[part, block, :, columns] - first_blocks_ref[slot, part]
            return carry

        lax.fori_loop(0, 128, put_block, 0, unroll=8)
        copy = pltpu.make_async_copy(result, out_ref.at[:, :, columns], local_sem.at[5 + len(written)])
        copy.start()
        written.append(copy)

    def begin(tile):
        send(
            tile,
            0,
            part_ref.at[tile, rows_at((1 - core) * 512, 512), :],
            landed_ref.at[tile, pl.ds(0, 512), :],
            sibling,
        )

    for panel in range(2):
        for group in range(len(GROUPS[panel])):
            take_group(panel, group, begin if group == len(GROUPS[panel]) - 1 else None)
    for tile, step in step_order():
        if tile is None:
            correct(step)
        elif tile < 0:
            apply(-1 - tile, step)
        else:
            advance(tile, step)
    await_bytes(all_ids_ref.at[pl.ds(0, 127)], id_sem.at[0])
    for panel in range(2):
        await_bytes(blocks_refs[panel].at[pl.ds(0, 127)], block_send_sem.at[panel])
    for tile in range(TILES):
        for stage in range(STAGES):
            wait(tile, stage, send_sem)
    for copy in written[-2:]:
        copy.wait()


def per_device(vectors, panel_store, block_ids, offsets, tri_factors):
    f32 = jnp.float32
    bf16 = jnp.bfloat16
    whole = pl.BlockSpec(memory_space=pltpu.VMEM)
    anywhere = pl.BlockSpec(memory_space=pl.ANY)
    dma = pltpu.SemaphoreType.DMA
    return pl.pallas_call(
        main_kernel,
        out_shape=jax.ShapeDtypeStruct(vectors.shape, f32),
        in_specs=[pl.BlockSpec(memory_space=pltpu.SMEM), whole, anywhere, whole, anywhere],
        out_specs=anywhere,
        scratch_shapes=[
            pltpu.VMEM((2, 128, 8, 1024), f32),
            pltpu.VMEM((128, 2, 8, 256), f32),
            pltpu.VMEM((128, 2, 8, 256), f32),
            pltpu.VMEM((128, 2, 128), jnp.int32),
            pltpu.VMEM((8, 128), jnp.int32),
            pltpu.SMEM((8, 128), jnp.int32),
            pltpu.VMEM((2, 128, 8, 256), f32),
            pltpu.VMEM((2, 128, 8, 256), f32),
            pltpu.VMEM((2, 2, 1024, 256), f32),
            pltpu.VMEM((2, 512, 256), f32),
            pltpu.VMEM((3, 256, 1536), bf16),
            pltpu.VMEM((2, 3, 768, 256), bf16),
            pltpu.VMEM((TILES, 1024, 128), f32),
            pltpu.VMEM((2, 1024, 512), f32),
            pltpu.VMEM((TILES, 1024, 128), f32),
            pltpu.VMEM((TILES, 512, 128), f32),
            pltpu.VMEM((TILES, 1024, 128), f32),
            pltpu.VMEM((3, 1024, 1024), bf16),
            pltpu.VMEM((3, 768, 256), bf16),
            pltpu.VMEM((3, 1536, 256), bf16),
            dma((2,)),
            dma((2, 4)),
            dma((2,)),
            dma((TILES, STAGES)),
            dma((TILES, STAGES)),
            dma((9,)),
        ],
        compiler_params=pltpu.CompilerParams(
            vmem_limit_bytes=VMEM_LIMIT, collective_id=0, has_side_effects=True
        ),
        name="main",
    )(offsets, block_ids, panel_store, tri_factors, vectors.reshape(2, 128, 8, 1024))


def solution(mesh):
    placed = (
        P(None, ("row", "col"), None),
        P(None, None, ("row", "col"), None),
        P(None, ("row", "col")),
        P(),
        P(),
    )
    return jax.shard_map(
        per_device,
        mesh=mesh,
        in_specs=placed,
        out_specs=P(None, ("row", "col"), None),
        check_vma=False,
    )
```

time: 561 us -> 140 us (0.25)
  waiting for transfers between devices: 336 us -> 0 us
  Pallas kernels: 0 us -> 132 us
  matrix products: 82.2 us -> 0 us
  other arithmetic: 55.5 us -> 0 us
  local copies, waits for them, and re-layouts: 45.8 us -> 8.44 us
  starting transfers between devices: 22.2 us -> 0 us
  between operations: 13.9 us -> 0.01 us
    psum x2 -> x0, waiting for transfers between devices: 291 us -> none  [reduce_strips(): return lax.psum(partial_sum, ('row', 'col'))]
    pallas_call x0 -> x1, Pallas kernels: none -> 132 us  [per_device(): pl.pallas_call(main_kernel, out_shape=jax.ShapeDtypeStruct(vectors.shape,...]
    dot_general x24 -> x0, matrix products: 82.2 us -> none  [the longest x16 46.4 us: matmul(): jnp.dot(first_op, second_op, precision=highest, preferred_element_type=jn...]
    all_to_all x2 -> x0, waiting for transfers between devices: 44.9 us -> none  [the longest x1 44.9 us: per_device(): lax.all_to_all(outgoing, ('row', 'col'), split_axis=2, concat_axis=2, til...]
    slice x1 -> x0, other arithmetic: 33.5 us -> none  [mask_panel(): imag_part = jnp.where(below, values[1], jnp.zeros_like(values[1]))]
    all_to_all x2 -> x0, starting transfers between devices: 21.7 us -> none  [the longest x1 11.5 us: per_device(): lax.all_to_all(labels, ('row', 'col'), split_axis=2, concat_axis=2, tiled...]
    gather x1 -> x0, local copies, waits for them, and re-layouts: 14.6 us -> none  [per_device(): placed = jnp.take_along_axis(arrived, ordering[:, None, :, None], axis=2)]
    reshape x2 -> x0, local copies, waits for them, and re-layouts: 12.2 us -> none  [per_device(): panel_store.reshape(panel_count, 2, slot_count, block_rows * col_width)]
  transfers between devices with their start and end apart: 4 -> 0, of which waited for: 3 -> 0; matrix products, arithmetic and copies ran while one was open for 4% -> 0% of each run, Pallas kernels for 0% -> 0%
where the time goes in v7:
time: 140 us
  Pallas kernels  132 us (94%)
  local copies, waits for them, and re-layouts  8.44 us (6%)
    pallas_call x1, Pallas kernels, per_device(): pl.pallas_call(main_kernel, out_shape=jax.ShapeDtypeStruct(vectors.shape,...  132 us
    unnamed x1, local copies, waits for them, and re-layouts  8.44 us

profile of v7, /device:TPU:1, one launch (start us, length us, event | category | flops | bytes accessed | tf_op | source)
XLA Modules:
  0.0 140.1 jit_solution(17316123419238635473)
XLA Ops:
  0.0 131.6 %main.1 = f32[2,1024,1024]{2,1,0:T(8,128)} custom-call(s32[2]{0:T(128)} %offsets_ref.1, s32[2,128]{1,0:T(2,128)} %ids_ref.1, f32[2,2,1024,256]{3,2,1,0:T(8,128)} %store_ref.1, f32[2,2,256,256]{3,2,1,0:T(8,128)} %tri_ref.1, f32[2,128,8,1024]{3,2,1,0:T(8,128)} %bitcast.1), custom_call_target="tpu_custom_call" | custom-call | tf_op jit(solution)/shard_map/main/pallas_call | solution.py:527
  131.6 8.4 %copy.7 = f32[2,1024,1024]{2,1,0:T(8,128)} copy(f32[2,1024,1024]{2,1,0:T(8,128)} %main.1) | data formatting | bytes 16777216

commit v8 on v7

--- a/solution.py
+++ b/solution.py
@@ -98,7 +98,7 @@
         ready.append((arrival + 2.5, tile, stage))
 
     for tile in range(0, TILES - 1, 2):
-        ready.append((0.0, tile, 0))
+        ready.append((0.0, tile, 1))
     for tile in [TILES - 1] + list(range(1, TILES - 1, 2)):
         now += 0.5
         send(tile, 0)
@@ -238,9 +238,9 @@
     def await_bytes(some, sem):
         pltpu.make_async_copy(some, some, sem).wait()
 
-    send_blocks(0, 0, 1, 24)
+    send_blocks(0, 0, 1, 48)
     lax.fori_loop(1, 128, send_ids, 0)
-    send_blocks(0, 0, 24, 64)
+    send_blocks(0, 0, 48, 64)
     for panel in range(2):
         for group, (first, count) in enumerate(GROUPS[panel]):
             if panel + group > 0:
@@ -500,6 +500,9 @@
 
     for panel in range(2):
         for group in range(len(GROUPS[panel])):
+            if panel == 1 and group == 2:
+                for tile in range(0, TILES - 1, 2):
+                    advance(tile, 0)
             take_group(panel, group, begin if group == len(GROUPS[panel]) - 1 else None)
     for tile, step in step_order():
         if tile is None:
@@ -518,13 +521,28 @@
         copy.wait()
 
 
+def move_kernel(source_ref, target_ref, sem):
+    copies = []
+    for piece in range(16):
+        rows = pl.ds(piece % 8 * 128, 128)
+        copies.append(
+            pltpu.make_async_copy(
+                source_ref.at[piece // 8, rows, :], target_ref.at[piece // 8, rows, :], sem.at[piece]
+            )
+        )
+    for copy in copies:
+        copy.start()
+    for copy in copies:
+        copy.wait()
+
+
 def per_device(vectors, panel_store, block_ids, offsets, tri_factors):
     f32 = jnp.float32
     bf16 = jnp.bfloat16
     whole = pl.BlockSpec(memory_space=pltpu.VMEM)
     anywhere = pl.BlockSpec(memory_space=pl.ANY)
     dma = pltpu.SemaphoreType.DMA
-    return pl.pallas_call(
+    result = pl.pallas_call(
         main_kernel,
         out_shape=jax.ShapeDtypeStruct(vectors.shape, f32),
         in_specs=[pl.BlockSpec(memory_space=pltpu.SMEM), whole, anywhere, whole, anywhere],
@@ -562,6 +580,14 @@
         ),
         name="main",
     )(offsets, block_ids, panel_store, tri_factors, vectors.reshape(2, 128, 8, 1024))
+    return pl.pallas_call(
+        move_kernel,
+        out_shape=jax.ShapeDtypeStruct(vectors.shape, f32),
+        in_specs=[anywhere],
+        out_specs=anywhere,
+        scratch_shapes=[dma((16,))],
+        name="move",
+    )(result)
 
 
 def solution(mesh):

time: 140 us -> 390 us (2.79)
  Pallas kernels: 132 us -> 390 us
  local copies, waits for them, and re-layouts: 8.44 us -> 0 us
    pallas_call x0 -> x1, Pallas kernels: none -> 255 us  [per_device(): pl.pallas_call(move_kernel, out_shape=jax.ShapeDtypeStruct(vectors.shape,...]
    unnamed x1 -> x0, local copies, waits for them, and re-layouts: 8.44 us -> none
where the time goes in v8:
time: 390 us
  Pallas kernels  390 us (100%)
    pallas_call x1, Pallas kernels, per_device(): pl.pallas_call(move_kernel, out_shape=jax.ShapeDtypeStruct(vectors.shape,...  255 us
    pallas_call x1, Pallas kernels, per_device(): pl.pallas_call(main_kernel, out_shape=jax.ShapeDtypeStruct(vectors.shape,...  134 us

profile of v8, /device:TPU:1, one launch (start us, length us, event | category | flops | bytes accessed | tf_op | source)
XLA Modules:
  0.0 389.8 jit_solution(15186643860773383830)
XLA Ops:
  0.0 134.3 %main.1.source_ref = f32[2,1024,1024]{2,1,0:T(8,128)} custom-call(s32[2]{0:T(128)} %offsets_ref.1, s32[2,128]{1,0:T(2,128)} %ids_ref.1, f32[2,2,1024,256]{3,2,1,0:T(8,128)} %store_ref.1, f32[2,2,256,256]{3,2,1,0:T(8,128)} %tri_ref.1, f32[2,128,8,1024]{3,2,1,0:T(8,128)} %bitcast.1), custom_call_target="tpu_custom_call" | custom-call | tf_op jit(solution)/shard_map/main/pallas_call | solution.py:545
  134.3 255.4 %move.1 = f32[2,1024,1024]{2,1,0:T(8,128)} custom-call(f32[2,1024,1024]{2,1,0:T(8,128)} %main.1.source_ref), custom_call_target="tpu_custom_call" | custom-call | tf_op jit(solution)/shard_map/move/pallas_call | solution.py:583

commit v9 on v7

--- a/solution.py
+++ b/solution.py
@@ -56,7 +56,7 @@
 
 GROUPS = (
     ((0, 64), (64, 64)),
-    ((0, 64), (64, 32), (96, 16), (112, 16)),
+    ((0, 32), (32, 32), (64, 32), (96, 16), (112, 16)),
 )
 
 
@@ -133,6 +133,7 @@
     tri_ref,
     vectors_ref,
     out_ref,
+    listed_ref,
     z_ref,
     first_blocks_ref,
     second_blocks_ref,
@@ -151,7 +152,6 @@
     held_ref,
     landed_ref,
     left_ref,
-    cross_ref,
     right_ref,
     block_send_sem,
     block_recv_sem,
@@ -188,6 +188,11 @@
         for panel in range(2)
     ]
     own_copies.append(pltpu.make_async_copy(ids_ref, all_ids_ref.at[0], local_sem.at[2]))
+    fetch_store = [
+        pltpu.make_async_copy(store_ref.at[panel], listed_ref.at[panel], local_sem.at[9 + panel]) for panel in range(2)
+    ]
+    fetch_store[0].start()
+    fetch_store[1].start()
     for copy in own_copies:
         copy.start()
     fetch_vectors = pltpu.make_async_copy(vectors_ref, z_ref, local_sem.at[3])
@@ -220,7 +225,7 @@
         def body(step, carry):
             strip = strip_at(step)
             remote(
-                store_ref.at[panel, :, listed(strip), :],
+                listed_ref.at[panel, :, listed(strip), :],
                 blocks_refs[panel].at[step],
                 block_send_sem.at[panel],
                 block_recv_sem.at[panel, group],
@@ -238,9 +243,11 @@
     def await_bytes(some, sem):
         pltpu.make_async_copy(some, some, sem).wait()
 
+    fetch_store[0].wait()
     send_blocks(0, 0, 1, 24)
     lax.fori_loop(1, 128, send_ids, 0)
     send_blocks(0, 0, 24, 64)
+    fetch_store[1].wait()
     for panel in range(2):
         for group, (first, count) in enumerate(GROUPS[panel]):
             if panel + group > 0:
@@ -271,6 +278,7 @@
         start = first * 8
         begin = first == 0
         values = panel_refs[panel]
+        kept = first if panel == 0 else 0
 
         await_bytes(
             blocks_refs[panel].at[pl.ds(max(first, 1), first + count - max(first, 1))], block_recv_sem.at[panel, group]
@@ -284,8 +292,8 @@
             limit = offsets_ref[panel] + lax.broadcasted_iota(jnp.int32, (8, 256), 1)
             below = row_index > limit
             diagonal = jnp.where(row_index == limit, 1.0, 0.0)
-            values[0, slot] = jnp.where(below, blocks_refs[panel][slot, 0], diagonal)
-            values[1, slot] = jnp.where(below, blocks_refs[panel][slot, 1], 0.0)
+            values[0, kept + step] = jnp.where(below, blocks_refs[panel][slot, 0], diagonal)
+            values[1, kept + step] = jnp.where(below, blocks_refs[panel][slot, 1], 0.0)
             for part in range(2):
                 wanted = z_ref[part, place]
                 for chunk in range(4):
@@ -299,7 +307,7 @@
 
         lax.fori_loop(0, count, take_block, 0, unroll=4)
 
-        own = [values[part, first : first + count].reshape(size, 256) for part in range(2)]
+        own = [values[part, kept : kept + count].reshape(size, 256) for part in range(2)]
         forms = left_forms(own[0].T, -own[1].T)
         for form in range(3):
             adjoint_ref[form, :, 0 : 3 * size] = forms[form]
@@ -438,10 +446,10 @@
             cross = complex_dot(left_forms(*parts(TILES - 1)), right_forms(*adjoint_upper(tri_ref, 0)))
             cross = right_forms(*cross)
             for form in range(3):
-                cross_ref[form] = cross[form]
+                factor_ref[0, form] = cross[form]
         rows = slice(piece * 256, (piece + 1) * 256)
         second = left_forms(x_ref[0, rows, 256:512], x_ref[1, rows, 256:512])
-        real_part, imag_part = complex_dot(second, [cross_ref[form] for form in range(3)])
+        real_part, imag_part = complex_dot(second, [factor_ref[0, form] for form in range(3)])
         first = left_forms(x_ref[0, rows, 0:256] - real_part, x_ref[1, rows, 0:256] - imag_part)
         for form in range(3):
             for part in range(2):
@@ -518,18 +526,35 @@
         copy.wait()
 
 
+def move_kernel(source_ref, target_ref, held_ref, in_sem, out_sem):
+    into = []
+    out_of = []
+    for piece in range(16):
+        place = (piece // 8, pl.ds(piece % 8 * 128, 128))
+        into.append(pltpu.make_async_copy(source_ref.at[place], held_ref.at[place], in_sem.at[piece]))
+        out_of.append(pltpu.make_async_copy(held_ref.at[place], target_ref.at[place], out_sem.at[piece]))
+    for copy in into:
+        copy.start()
+    for arriving, leaving in zip(into, out_of):
+        arriving.wait()
+        leaving.start()
+    for copy in out_of:
+        copy.wait()
+
+
 def per_device(vectors, panel_store, block_ids, offsets, tri_factors):
     f32 = jnp.float32
     bf16 = jnp.bfloat16
     whole = pl.BlockSpec(memory_space=pltpu.VMEM)
     anywhere = pl.BlockSpec(memory_space=pl.ANY)
     dma = pltpu.SemaphoreType.DMA
-    return pl.pallas_call(
+    result = pl.pallas_call(
         main_kernel,
         out_shape=jax.ShapeDtypeStruct(vectors.shape, f32),
         in_specs=[pl.BlockSpec(memory_space=pltpu.SMEM), whole, anywhere, whole, anywhere],
         out_specs=anywhere,
         scratch_shapes=[
+            pltpu.VMEM((2, 2, 1024, 256), f32),
             pltpu.VMEM((2, 128, 8, 1024), f32),
             pltpu.VMEM((128, 2, 8, 256), f32),
             pltpu.VMEM((128, 2, 8, 256), f32),
@@ -537,9 +562,9 @@
             pltpu.VMEM((8, 128), jnp.int32),
             pltpu.SMEM((8, 128), jnp.int32),
             pltpu.VMEM((2, 128, 8, 256), f32),
-            pltpu.VMEM((2, 128, 8, 256), f32),
+            pltpu.VMEM((2, 32, 8, 256), f32),
             pltpu.VMEM((2, 2, 1024, 256), f32),
-            pltpu.VMEM((2, 512, 256), f32),
+            pltpu.VMEM((2, 256, 256), f32),
             pltpu.VMEM((3, 256, 1536), bf16),
             pltpu.VMEM((2, 3, 768, 256), bf16),
             pltpu.VMEM((TILES, 1024, 128), f32),
@@ -548,20 +573,28 @@
             pltpu.VMEM((TILES, 512, 128), f32),
             pltpu.VMEM((TILES, 1024, 128), f32),
             pltpu.VMEM((3, 1024, 1024), bf16),
-            pltpu.VMEM((3, 768, 256), bf16),
             pltpu.VMEM((3, 1536, 256), bf16),
             dma((2,)),
-            dma((2, 4)),
+            dma((2, 5)),
             dma((2,)),
             dma((TILES, STAGES)),
             dma((TILES, STAGES)),
-            dma((9,)),
+            dma((11,)),
         ],
         compiler_params=pltpu.CompilerParams(
             vmem_limit_bytes=VMEM_LIMIT, collective_id=0, has_side_effects=True
         ),
         name="main",
     )(offsets, block_ids, panel_store, tri_factors, vectors.reshape(2, 128, 8, 1024))
+    return pl.pallas_call(
+        move_kernel,
+        out_shape=jax.ShapeDtypeStruct(vectors.shape, f32),
+        in_specs=[anywhere],
+        out_specs=anywhere,
+        scratch_shapes=[pltpu.VMEM(vectors.shape, f32), dma((16,)), dma((16,))],
+        compiler_params=pltpu.CompilerParams(vmem_limit_bytes=VMEM_LIMIT),
+        name="move",
+    )(result)
 
 
 def solution(mesh):

time: 140 us -> 137 us (0.979)
  local copies, waits for them, and re-layouts: 8.44 us -> 0 us
  Pallas kernels: 132 us -> 137 us
    unnamed x1 -> x0, local copies, waits for them, and re-layouts: 8.44 us -> none
    pallas_call x0 -> x1, Pallas kernels: none -> 6.57 us  [per_device(): pl.pallas_call(move_kernel, out_shape=jax.ShapeDtypeStruct(vectors.shape,...]
where the time goes in v9:
time: 137 us
  Pallas kernels  137 us (100%)
    pallas_call x1, Pallas kernels, per_device(): pl.pallas_call(main_kernel, out_shape=jax.ShapeDtypeStruct(vectors.shape,...  130 us
    pallas_call x1, Pallas kernels, per_device(): pl.pallas_call(move_kernel, out_shape=jax.ShapeDtypeStruct(vectors.shape,...  6.57 us

profile of v9, /device:TPU:1, one launch (start us, length us, event | category | flops | bytes accessed | tf_op | source)
XLA Modules:
  0.0 137.2 jit_solution(4003229843864881917)
XLA Ops:
  0.0 130.4 %main.1.source_ref = f32[2,1024,1024]{2,1,0:T(8,128)} custom-call(s32[2]{0:T(128)} %offsets_ref.1, s32[2,128]{1,0:T(2,128)} %ids_ref.1, f32[2,2,1024,256]{3,2,1,0:T(8,128)} %store_ref.1, f32[2,2,256,256]{3,2,1,0:T(8,128)} %tri_ref.1, f32[2,128,8,1024]{3,2,1,0:T(8,128)} %bitcast.1), custom_call_target="tpu_custom_call" | custom-call | tf_op jit(solution)/shard_map/main/pallas_call | solution.py:551
  130.4 6.6 %move.1 = f32[2,1024,1024]{2,1,0:T(8,128)} custom-call(f32[2,1024,1024]{2,1,0:T(8,128)} %main.1.source_ref), custom_call_target="tpu_custom_call" | custom-call | tf_op jit(solution)/shard_map/move/pallas_call | solution.py:589

commit v10 on v9

--- a/solution.py
+++ b/solution.py
@@ -61,10 +61,12 @@
 
 
 TILES = 9
-LINKS = ((), (0,), (1, 2), (3, 4, 5))
+LINKS = ((), (0, 1), (2, 3), (4, 5))
+FIRST_LINKS = (3, 4, 2, 2, 5, 0, 4, 3, 0)
+APART = 2.5
 HALF_STAGES = len(LINKS)
 STAGES = 2 * HALF_STAGES
-SIZES = [1024, 512, 256, 64, 8]
+SIZES = [1024, 512, 128, 32, 8]
 COUNTS = [SIZES[stage] - SIZES[stage + 1] for stage in range(HALF_STAGES)]
 BASES = [sum(COUNTS[:stage]) for stage in range(HALF_STAGES)]
 
@@ -92,13 +94,15 @@
         else:
             arrival = now
             for link in LINKS[level]:
-                link = (tile + link) % 6
+                link = (FIRST_LINKS[tile] + link) % 6
                 free[link] = max(free[link], now) + SIZES[level] / 2 * 0.512 / 50
                 arrival = max(arrival, free[link])
+        if stage == 0 and tile < TILES - 1:
+            arrival = max(arrival, tile // 2 * APART + 0.5)
         ready.append((arrival + 2.5, tile, stage))
 
     for tile in range(0, TILES - 1, 2):
-        ready.append((0.0, tile, 0))
+        ready.append((tile // 2 * APART, tile, 0))
     for tile in [TILES - 1] + list(range(1, TILES - 1, 2)):
         now += 0.5
         send(tile, 0)
@@ -376,7 +380,7 @@
         pltpu.make_async_copy(some, some, sem.at[tile, stage]).wait()
 
     def links_of(tile, level):
-        return [(tile + link) % 6 for link in LINKS[level]]
+        return [(FIRST_LINKS[tile] + link) % 6 for link in LINKS[level]]
 
     def share(tile, level, flips=0):
         index = 0

time: 137 us -> 136 us (level)
  Pallas kernels: 137 us -> 135 us
    pallas_call x1, Pallas kernels: 130 us -> 129 us  [per_device(): pl.pallas_call(main_kernel, out_shape=jax.ShapeDtypeStruct(vectors.shape,...]
where the time goes in v10:
time: 136 us; the launch traced here: 135 us
  Pallas kernels  135 us (99%)
    pallas_call x1, Pallas kernels, per_device(): pl.pallas_call(main_kernel, out_shape=jax.ShapeDtypeStruct(vectors.shape,...  129 us
    pallas_call x1, Pallas kernels, per_device(): pl.pallas_call(move_kernel, out_shape=jax.ShapeDtypeStruct(vectors.shape,...  6.57 us

profile of v10, /device:TPU:1, one launch (start us, length us, event | category | flops | bytes accessed | tf_op | source)
XLA Modules:
  0.0 135.5 jit_solution(13206177669737338331)
XLA Ops:
  0.0 128.7 %main.1.source_ref = f32[2,1024,1024]{2,1,0:T(8,128)} custom-call(s32[2]{0:T(128)} %offsets_ref.1, s32[2,128]{1,0:T(2,128)} %ids_ref.1, f32[2,2,1024,256]{3,2,1,0:T(8,128)} %store_ref.1, f32[2,2,256,256]{3,2,1,0:T(8,128)} %tri_ref.1, f32[2,128,8,1024]{3,2,1,0:T(8,128)} %bitcast.1), custom_call_target="tpu_custom_call" | custom-call | tf_op jit(solution)/shard_map/main/pallas_call | solution.py:555
  128.7 6.6 %move.1 = f32[2,1024,1024]{2,1,0:T(8,128)} custom-call(f32[2,1024,1024]{2,1,0:T(8,128)} %main.1.source_ref), custom_call_target="tpu_custom_call" | custom-call | tf_op jit(solution)/shard_map/move/pallas_call | solution.py:593

commit v11 on v10

--- a/solution.py
+++ b/solution.py
@@ -221,8 +221,12 @@
 
     def strip_at(step):
         spread = (step // 2 * 27) % 64
+        sign = 1 - 2 * core
         return strip_of(
-            (x + spread % 4) % 4, (y + (spread // 4) % 4) % 4, (z + spread // 16) % 4, (core + step) % 2
+            (x + 4 + sign * (spread % 4)) % 4,
+            (y + 4 + sign * ((spread // 4) % 4)) % 4,
+            (z + 4 + sign * (spread // 16)) % 4,
+            (core + step) % 2,
         )
 
     def send_blocks(panel, group, first, last):

time: 136 us -> 141 us (1.037)
  Pallas kernels: 135 us -> 141 us
    pallas_call x1, Pallas kernels: 129 us -> 134 us  [per_device(): pl.pallas_call(main_kernel, out_shape=jax.ShapeDtypeStruct(vectors.shape,...]
where the time goes in v11:
time: 141 us
  Pallas kernels  141 us (100%)
    pallas_call x1, Pallas kernels, per_device(): pl.pallas_call(main_kernel, out_shape=jax.ShapeDtypeStruct(vectors.shape,...  134 us
    pallas_call x1, Pallas kernels, per_device(): pl.pallas_call(move_kernel, out_shape=jax.ShapeDtypeStruct(vectors.shape,...  6.57 us

profile of v11, /device:TPU:1, one launch (start us, length us, event | category | flops | bytes accessed | tf_op | source)
XLA Modules:
  0.0 140.9 jit_solution(8805139448227787648)
XLA Ops:
  0.0 134.1 %main.1.source_ref = f32[2,1024,1024]{2,1,0:T(8,128)} custom-call(s32[2]{0:T(128)} %offsets_ref.1, s32[2,128]{1,0:T(2,128)} %ids_ref.1, f32[2,2,1024,256]{3,2,1,0:T(8,128)} %store_ref.1, f32[2,2,256,256]{3,2,1,0:T(8,128)} %tri_ref.1, f32[2,128,8,1024]{3,2,1,0:T(8,128)} %bitcast.1), custom_call_target="tpu_custom_call" | custom-call | tf_op jit(solution)/shard_map/main/pallas_call | solution.py:559
  134.1 6.6 %move.1 = f32[2,1024,1024]{2,1,0:T(8,128)} custom-call(f32[2,1024,1024]{2,1,0:T(8,128)} %main.1.source_ref), custom_call_target="tpu_custom_call" | custom-call | tf_op jit(solution)/shard_map/move/pallas_call | solution.py:597

commit v12 on v10

--- a/solution.py
+++ b/solution.py
@@ -220,7 +220,7 @@
         )
 
     def strip_at(step):
-        spread = (step // 2 * 27) % 64
+        spread = (step // 2 * 21) % 64
         return strip_of(
             (x + spread % 4) % 4, (y + (spread // 4) % 4) % 4, (z + spread // 16) % 4, (core + step) % 2
         )

time: 136 us -> 143 us (1.051)
  Pallas kernels: 135 us -> 143 us
    pallas_call x1, Pallas kernels: 129 us -> 136 us  [per_device(): pl.pallas_call(main_kernel, out_shape=jax.ShapeDtypeStruct(vectors.shape,...]
where the time goes in v12:
time: 143 us
  Pallas kernels  143 us (100%)
    pallas_call x1, Pallas kernels, per_device(): pl.pallas_call(main_kernel, out_shape=jax.ShapeDtypeStruct(vectors.shape,...  136 us
    pallas_call x1, Pallas kernels, per_device(): pl.pallas_call(move_kernel, out_shape=jax.ShapeDtypeStruct(vectors.shape,...  6.57 us

profile of v12, /device:TPU:1, one launch (start us, length us, event | category | flops | bytes accessed | tf_op | source)
XLA Modules:
  0.0 142.9 jit_solution(12215597425938517910)
XLA Ops:
  0.0 136.2 %main.1.source_ref = f32[2,1024,1024]{2,1,0:T(8,128)} custom-call(s32[2]{0:T(128)} %offsets_ref.1, s32[2,128]{1,0:T(2,128)} %ids_ref.1, f32[2,2,1024,256]{3,2,1,0:T(8,128)} %store_ref.1, f32[2,2,256,256]{3,2,1,0:T(8,128)} %tri_ref.1, f32[2,128,8,1024]{3,2,1,0:T(8,128)} %bitcast.1), custom_call_target="tpu_custom_call" | custom-call | tf_op jit(solution)/shard_map/main/pallas_call | solution.py:555
  136.2 6.6 %move.1 = f32[2,1024,1024]{2,1,0:T(8,128)} custom-call(f32[2,1024,1024]{2,1,0:T(8,128)} %main.1.source_ref), custom_call_target="tpu_custom_call" | custom-call | tf_op jit(solution)/shard_map/move/pallas_call | solution.py:593
